TPU v7x, 32 devices: a whole 2x2x4 slice. The times are simulated.
32 devices in a mesh: expert: 8 (over y, x, core), dp: 4 (over z).
Axes of the slice: x: 2, y: 2, z: 4, core: 2. Of those that a mesh axis runs over, the one named last changes fastest.
Arguments:
- attn_rows: bfloat16 [4096, 7168], P('dp', 'expert'), may hold values from -6 to 6
- out_grad: bfloat16 [4096, 7168], P('dp', 'expert'), may hold values from -6 to 6
- routes: int32 [4096, 8], P(('dp', 'expert')), may hold values from 0 to 255, as said below
- gates: bfloat16 [4096, 8], P(('dp', 'expert')), may hold values from 0.049804688 to 0.5
- w_gate: bfloat16 [8, 7168, 2048], P('expert', None, 'dp'), may hold values from -0.0625 to 0.0625
- w_up: bfloat16 [8, 7168, 2048], P('expert', None, 'dp'), may hold values from -0.0625 to 0.0625
- w_down: bfloat16 [8, 2048, 7168], P('expert', 'dp'), may hold values from -0.125 to 0.125
Outputs:
- grad_input: bfloat16 [4096, 7168], P('dp', 'expert')
- grad_w_gate: bfloat16 [8, 7168, 2048], P('expert', None, 'dp')
- grad_w_up: bfloat16 [8, 7168, 2048], P('expert', None, 'dp')
Inputs may be any that keep to these rules, and one draw needn't show every extreme that they name: `routes`: each row names 8 different experts. In the 128 rows of one device (aligned blocks of 128 rows) no window expert (below 8) is named by more than 6 rows; in every device's rows some window expert is named by exactly 6 rows, and one window expert is named by exactly 6 rows of every device.
All inputs are finite; a program needn't handle non-finite values.
Results may differ from a plain program's by a relative error of at most 0.0058.
Values may be sent and summed in bfloat16 or wider, within the bound.
No kernel may reach another device: no remote copies, remote signals or barrier semaphores. Data moves between devices by JAX's collectives and lax.ppermute only.
A program may use at most 256 MiB of HBM per device.

v0:
```python
import jax
import jax.numpy as jnp
from jax import lax
from jax.sharding import PartitionSpec as P

TOP = 8


def slot_tables(route_blocks, experts, capacity):
    matches = (route_blocks[..., None] == jnp.arange(experts, dtype=jnp.int32)).astype(jnp.int32)
    per_token = jnp.sum(matches, axis=2)
    before = jnp.cumsum(per_token, axis=1) - per_token
    slot_of = jnp.sum(matches * before[:, :, None, :], axis=3)
    at_slot = (slot_of[..., None] == jnp.arange(capacity, dtype=jnp.int32)).astype(jnp.float32)
    return (matches.astype(jnp.float32), at_slot)


def deliver(payload, grad_payload, gate_slots, experts, groups):

    def spread(values):
        widened = jnp.broadcast_to(values[:, None], (values.shape[0], groups) + values.shape[1:])
        return widened.reshape((values.shape[0] * groups,) + values.shape[1:])

    arrived = (
        lax.all_to_all(spread(payload), ("expert", "dp"), split_axis=0, concat_axis=0, tiled=True),
        lax.all_to_all(
            spread(grad_payload), ("expert", "dp"), split_axis=0, concat_axis=0, tiled=True
        ),
        lax.all_to_all(
            spread(gate_slots), ("expert", "dp"), split_axis=0, concat_axis=0, tiled=True
        ),
    )

    def regroup(values):
        values = values.reshape((experts, groups) + values.shape[1:])
        return jnp.swapaxes(values, 0, 1)

    return (regroup(arrived[0]), regroup(arrived[1]), regroup(arrived[2]))


def give_back(partial_value, experts, groups):
    outgoing = jnp.swapaxes(partial_value, 0, 1).astype(jnp.bfloat16)
    outgoing = outgoing.reshape((experts * groups,) + partial_value.shape[2:])
    arrived = lax.all_to_all(outgoing, ("expert", "dp"), split_axis=0, concat_axis=0, tiled=True)
    arrived = arrived.reshape((experts, groups) + partial_value.shape[2:]).astype(jnp.float32)
    return jnp.sum(arrived, axis=1)


def expert_pass(token_rows, grad_rows, gate_rows, w_gate, w_up, w_down):
    gate_mat = w_gate[0]
    up_mat = w_up[0]
    down_mat = w_down[0]
    rows_dims = (((1,), (1,)), ((), ()))
    first_dims = (((0,), (0,)), ((), ()))
    gate_pre = jnp.dot(token_rows, gate_mat, preferred_element_type=jnp.float32)
    up_proj = jnp.dot(token_rows, up_mat, preferred_element_type=jnp.float32)
    sigma_gate = jax.nn.sigmoid(gate_pre)
    activated = gate_pre * sigma_gate
    back_proj = lax.dot_general(grad_rows, down_mat, rows_dims, preferred_element_type=jnp.float32)
    coef = gate_rows.astype(jnp.float32)[:, None]
    grad_hidden = coef * back_proj
    grad_gate = (grad_hidden * up_proj * sigma_gate * (1.0 + gate_pre * (1.0 - sigma_gate))).astype(
        jnp.bfloat16
    )
    grad_up = (grad_hidden * activated).astype(jnp.bfloat16)
    g_gate = lax.dot_general(
        token_rows, grad_gate, first_dims, preferred_element_type=jnp.float32
    ).astype(jnp.bfloat16)
    g_up = lax.dot_general(
        token_rows, grad_up, first_dims, preferred_element_type=jnp.float32
    ).astype(jnp.bfloat16)
    partial_value = lax.dot_general(
        grad_gate, gate_mat, rows_dims, preferred_element_type=jnp.float32
    )
    partial_value = partial_value + lax.dot_general(
        grad_up, up_mat, rows_dims, preferred_element_type=jnp.float32
    )
    return (partial_value, g_gate[None], g_up[None])


def per_device(attn_rows, out_grad, routes, gates, w_gate, w_up, w_down):
    experts = lax.axis_size("expert")
    groups = lax.axis_size("dp")
    own_rows = routes.shape[0]
    capacity = 3 * own_rows // 64
    highest = lax.Precision.HIGHEST
    own_matches, own_slots = slot_tables(routes[None], experts, capacity)
    gate_slots = jnp.einsum(
        "btke,btkc,btk->bec",
        own_matches,
        own_slots,
        gates[None].astype(jnp.float32),
        precision=highest,
    )[0].astype(jnp.bfloat16)
    shard_routes = lax.all_gather(routes, "expert", axis=0, tiled=True)
    matches, at_slot = slot_tables(shard_routes.reshape(experts, own_rows, TOP), experts, capacity)
    placement = jnp.einsum("btke,btkc->bect", matches, at_slot, precision=highest)
    place_bf = placement.astype(jnp.bfloat16)
    feat = attn_rows.shape[1]
    x_blocks = attn_rows.reshape(experts, own_rows, feat)
    dy_blocks = out_grad.reshape(experts, own_rows, feat)
    payload = jnp.einsum(
        "bect,btf->ebcf", place_bf, x_blocks, preferred_element_type=jnp.float32
    ).astype(jnp.bfloat16)
    grad_payload = jnp.einsum(
        "bect,btf->ebcf", place_bf, dy_blocks, preferred_element_type=jnp.float32
    ).astype(jnp.bfloat16)
    payload = payload.reshape(experts, experts * capacity, feat)
    grad_payload = grad_payload.reshape(experts, experts * capacity, feat)
    arrived_x, arrived_dy, arrived_g = deliver(payload, grad_payload, gate_slots, experts, groups)

    def assemble(values):
        values = values.reshape(groups, experts, experts, capacity, feat)
        return jnp.transpose(values, (0, 2, 3, 1, 4)).reshape(
            groups * experts * capacity, experts * feat
        )

    partial_value, g_gate, g_up = expert_pass(
        assemble(arrived_x), assemble(arrived_dy), arrived_g.reshape(-1), w_gate, w_up, w_down
    )
    partial_value = partial_value.reshape(groups, experts, capacity, experts, feat)
    partial_value = jnp.transpose(partial_value, (0, 3, 1, 2, 4)).reshape(
        groups, experts, experts * capacity, feat
    )
    summed = give_back(partial_value, experts, groups).reshape(experts, experts, capacity, feat)
    grad_input = (
        jnp.einsum("bect,ebcf->btf", placement, summed, precision=highest)
        .reshape(experts * own_rows, feat)
        .astype(jnp.bfloat16)
    )
    return (grad_input, g_gate, g_up)


def solution(mesh):
    return jax.shard_map(
        per_device,
        mesh=mesh,
        in_specs=(
            P("dp", "expert"),
            P("dp", "expert"),
            P(("dp", "expert"), None),
            P(("dp", "expert"), None),
            P("expert", None, "dp"),
            P("expert", None, "dp"),
            P("expert", "dp", None),
        ),
        out_specs=(P("dp", "expert"), P("expert", None, "dp"), P("expert", None, "dp")),
        check_vma=False,
    )
```

profile of v0, /device:TPU:0, one launch (start us, length us, event | category | flops | bytes accessed | tf_op | source)
XLA Modules:
  0.0 289.2 jit_solution(2233372598867504258)
XLA Ops:
  0.6 0.8 convert.8
  3.2 0.8 fusion.30
  4.4 0.7 copy.119
  5.1 7.3 %all-to-all-start = ((bf16[32,1,6]{2,1,0:T(2,128)(2,1)}), bf16[32,1,6]{2,1,0:T(2,128)(2,1)S(1)}, u32[]{:S(2)}, u32[]{:S(2)}) async-start(bf16[32,1,6]{2,1,0:T(2,128)(2,1)} %copy.119), calls=%async_computation | async-start | bytes 32768 | tf_op jit(solution)/shard_map/all_to_all | solution.py:29
  12.4 9.4 %all_gather.3 = s32[1024,8]{0,1:T(8,128)S(1)} all-gather(s32[128,8]{0,1:T(8,128)} %param.9), channel_id=1, replica_groups=mesh['expert'=8,'dp'=4] {'expert'}, dimensions={0}, use_global_device_ids=true | all-gather | bytes 36864 | tf_op jit(solution)/shard_map/all_gather | solution.py:95
  22.0 1.8 convert_reduce_fusion
  24.2 18.8 %select_reduce_fusion = s32[8,128,8]{2,1,0:T(8,128)S(1)} fusion(s32[8,128,8]{2,1,0:T(8,128)S(1)} %copy.113, s32[8,128,8]{2,1,0:T(8,128)S(1)} %copy.110), kind=kLoop, calls=%fused_computation.20 | loop fusion | flops 188416 | bytes 98304 | tf_op jit(solution)/shard_map/reduce_sum | solution.py:13
  43.0 6.2 %fusion.12 = f32[8,128,6,8]{3,2,1,0:T(8,128)} fusion(s32[8,128,8]{2,1,0:T(8,128)S(1)} %select_reduce_fusion, s32[8,128,8]{2,1,0:T(8,128)S(1)} %copy.110), kind=kOutput, calls=%fused_computation.18 | convolution fusion | flops 4964352 | bytes 262144 | tf_op jit(solution)/shard_map/btke,btkc->bect/dot_general | solution.py:97
  49.2 2.6 copy.114
  52.4 1.7 broadcast_in_dim.16
  54.1 4.6 %all-to-all-start.1 = ((bf16[32,48,896]{2,1,0:T(8,128)(2,1)}), bf16[32,48,896]{2,1,0:T(8,128)(2,1)}, u32[]{:S(2)}, u32[]{:S(2)}) async-start(bf16[32,48,896]{2,1,0:T(8,128)(2,1)} %bitcast.137), calls=%async_computation.1 | async-start | bytes 5505024 | tf_op jit(solution)/shard_map/all_to_all | solution.py:26
  58.8 1.9 fusion.46
  60.7 59.8 %all-to-all-done.1 = bf16[32,48,896]{2,1,0:T(8,128)(2,1)} async-done(((bf16[32,48,896]{2,1,0:T(8,128)(2,1)}), bf16[32,48,896]{2,1,0:T(8,128)(2,1)}, u32[]{:S(2)}, u32[]{:S(2)}) %all-to-all-start.1) | async-done | bytes 2752544 | tf_op jit(solution)/shard_map/all_to_all | solution.py:26
  120.5 1.7 broadcast_in_dim.18
  122.3 4.9 %all-to-all-start.2 = ((bf16[32,48,896]{2,1,0:T(8,128)(2,1)}), bf16[32,48,896]{2,1,0:T(8,128)(2,1)}, u32[]{:S(2)}, u32[]{:S(2)}) async-start(bf16[32,48,896]{2,1,0:T(8,128)(2,1)} %bitcast.135), calls=%async_computation.2 | async-start | bytes 5505024 | tf_op jit(solution)/shard_map/all_to_all | solution.py:25
  127.6 3.3 %copy.123 = bf16[4,8,48,896]{3,1,2,0:T(8,128)(2,1)S(1)} copy(bf16[4,8,48,896]{3,2,0,1:T(8,128)(2,1)} %bitcast.11) | data formatting | bytes 5505024 | tf_op jit(solution)/shard_map/transpose | solution.py:36
  131.0 2.1 copy.131
  133.0 55.7 %all-to-all-done.2 = bf16[32,48,896]{2,1,0:T(8,128)(2,1)} async-done(((bf16[32,48,896]{2,1,0:T(8,128)(2,1)}), bf16[32,48,896]{2,1,0:T(8,128)(2,1)}, u32[]{:S(2)}, u32[]{:S(2)}) %all-to-all-start.2) | async-done | bytes 2752544 | tf_op jit(solution)/shard_map/all_to_all | solution.py:25
  188.8 3.3 %copy.125 = bf16[4,8,48,896]{3,1,2,0:T(8,128)(2,1)S(1)} copy(bf16[4,8,48,896]{3,2,0,1:T(8,128)(2,1)} %bitcast.22) | data formatting | bytes 5505024 | tf_op jit(solution)/shard_map/transpose | solution.py:36
  192.7 5.9 %fusion.5 = f32[192,512]{1,0:T(8,128)S(1)} fusion(bf16[192,7168]{1,0:T(8,128)(2,1)S(1)} %bitcast.130, bf16[1,7168,512]{2,1,0:T(8,128)(2,1)} %param.11), kind=kOutput, calls=%fused_computation.8 | convolution fusion | flops 1409286144 | bytes 10485760 | tf_op jit(solution)/shard_map/dot_general | solution.py:55
  198.7 1.7 slice-done.5
  200.4 2.6 multiply_convert_fusion
  203.0 1.6 fusion.27
  204.9 2.5 fusion.3
  207.4 5.6 %fusion.2 = bf16[192,7168]{1,0:T(8,128)(2,1)S(1)} fusion(f32[192,7168]{1,0:T(8,128)S(1)} %fusion.3, bf16[192,512]{1,0:T(8,128)(2,1)S(1)} %get-tuple-element.3, bf16[1,7168,512]{2,1,0:T(8,128)(2,1)} %param.12), kind=kOutput, calls=%fused_computation.5 | convolution fusion | flops 1412038656 | bytes 15794176 | tf_op jit(solution)/shard_map/dot_general | solution.py:75
  213.5 2.1 copy.126
  215.7 4.7 %all-to-all-start.3 = ((bf16[32,48,896]{2,1,0:T(8,128)(2,1)}), bf16[32,48,896]{2,1,0:T(8,128)(2,1)}, u32[]{:S(2)}, u32[]{:S(2)}) async-start(bf16[32,48,896]{2,1,0:T(8,128)(2,1)} %bitcast.136), calls=%async_computation.3 | async-start | bytes 5505024 | tf_op jit(solution)/shard_map/all_to_all | solution.py:44
  220.4 7.2 %fusion.1 = bf16[1,7168,512]{2,1,0:T(8,128)(2,1)} fusion(bf16[192,7168]{1,0:T(8,128)(2,1)} %bitcast.132, bf16[192,512]{1,0:T(8,128)(2,1)S(1)} %get-tuple-element.3), kind=kOutput, calls=%fused_computation.3 | convolution fusion | flops 1412956160 | bytes 10289152 | tf_op jit(solution)/shard_map/dot_general | solution.py:69
  227.6 5.2 %fusion = bf16[1,7168,512]{2,1,0:T(8,128)(2,1)} fusion(bf16[192,7168]{1,0:T(8,128)(2,1)S(1)} %bitcast.133, bf16[192,512]{1,0:T(8,128)(2,1)S(1)} %fusion.27), kind=kOutput, calls=%fused_computation.2 | convolution fusion | flops 1412956160 | bytes 10289152 | tf_op jit(solution)/shard_map/dot_general | solution.py:66
  232.8 49.4 %all-to-all-done.3 = bf16[32,48,896]{2,1,0:T(8,128)(2,1)} async-done(((bf16[32,48,896]{2,1,0:T(8,128)(2,1)}), bf16[32,48,896]{2,1,0:T(8,128)(2,1)}, u32[]{:S(2)}, u32[]{:S(2)}) %all-to-all-start.3) | async-done | bytes 2752544 | tf_op jit(solution)/shard_map/all_to_all | solution.py:44
  282.2 2.3 convert_reduce_fusion.1
  285.0 4.2 %bitcast_convert_fusion = bf16[8,128,896]{2,1,0:T(8,128)(2,1)} fusion(f32[8,8,6,896]{3,0,2,1:T(8,128)S(1)} %bitcast.145, f32[8,128,6,8]{1,3,2,0:T(8,128)S(1)} %copy.114), kind=kOutput, calls=%fused_computation.22 | convolution fusion | flops 529399808 | bytes 3407872 | tf_op jit(solution)/shard_map/bect,ebcf->btf/dot_general | solution.py:127
  (48 shorter events, 5.4 us)
Async XLA Ops:
  0.6 51.2 %copy-start = (bf16[1024,896]{1,0:T(8,128)(2,1)S(1)}, bf16[1024,896]{1,0:T(8,128)(2,1)}, u32[]{:S(2)}) copy-start(bf16[1024,896]{1,0:T(8,128)(2,1)} %param.8) | copy-start | bytes 5505028
  5.1 47.3 %all-to-all-start = ((bf16[32,1,6]{2,1,0:T(2,128)(2,1)}), bf16[32,1,6]{2,1,0:T(2,128)(2,1)S(1)}, u32[]{:S(2)}, u32[]{:S(2)}) async-start(bf16[32,1,6]{2,1,0:T(2,128)(2,1)} %copy.119), calls=%async_computation | async-start | bytes 32768 | tf_op jit(solution)/shard_map/all_to_all | solution.py:29
  54.1 66.4 %all-to-all-start.1 = ((bf16[32,48,896]{2,1,0:T(8,128)(2,1)}), bf16[32,48,896]{2,1,0:T(8,128)(2,1)}, u32[]{:S(2)}, u32[]{:S(2)}) async-start(bf16[32,48,896]{2,1,0:T(8,128)(2,1)} %bitcast.137), calls=%async_computation.1 | async-start | bytes 5505024 | tf_op jit(solution)/shard_map/all_to_all | solution.py:26
  122.3 66.5 %all-to-all-start.2 = ((bf16[32,48,896]{2,1,0:T(8,128)(2,1)}), bf16[32,48,896]{2,1,0:T(8,128)(2,1)}, u32[]{:S(2)}, u32[]{:S(2)}) async-start(bf16[32,48,896]{2,1,0:T(8,128)(2,1)} %bitcast.135), calls=%async_computation.2 | async-start | bytes 5505024 | tf_op jit(solution)/shard_map/all_to_all | solution.py:25
  192.1 6.6 %slice-start.4 = ((s8[7340032]{0:T(1024)(128)(4,1)}), s8[4194304]{0:T(1024)(128)(4,1)S(1)}, s32[]{:S(2)}) async-start(s8[7340032]{0:T(1024)(128)(4,1)} %bitcast.153), calls=%async_computation.8 | async-start | bytes 8388608
  192.1 10.8 %slice-start.2 = ((s8[7340032]{0:T(1024)(128)(4,1)}), s8[4194304]{0:T(1024)(128)(4,1)S(1)}, s32[]{:S(2)}) async-start(s8[7340032]{0:T(1024)(128)(4,1)} %bitcast.143), calls=%async_computation.6 | async-start | bytes 8388608
  192.7 10.3 %copy-start.2 = (bf16[24,8,8,896]{3,1,2,0:T(8,128)(2,1)}, bf16[24,8,8,896]{3,1,2,0:T(8,128)(2,1)S(1)}, u32[]{:S(2)}) copy-start(bf16[24,8,8,896]{3,1,2,0:T(8,128)(2,1)S(1)} %copy.132) | copy-start | bytes 8257540
  192.7 6.0 %copy-start.4 = (bf16[24,8,8,896]{3,1,2,0:T(8,128)(2,1)S(1)}, bf16[24,8,8,896]{3,1,2,0:T(8,128)(2,1)}, u32[]{:S(2)}) copy-start(bf16[24,8,8,896]{3,1,2,0:T(8,128)(2,1)} %copy.131) | copy-start | bytes 8257540
  192.7 7.7 %slice-start.5 = ((s8[7340032]{0:T(1024)(128)(4,1)}), s8[3145728]{0:T(1024)(128)(4,1)S(1)}, s32[]{:S(2)}) async-start(s8[7340032]{0:T(1024)(128)(4,1)} %bitcast.153), calls=%async_computation.9 | async-start | bytes 6291456
  192.7 10.3 %slice-start.3 = ((s8[7340032]{0:T(1024)(128)(4,1)}), s8[3145728]{0:T(1024)(128)(4,1)S(1)}, s32[]{:S(2)}) async-start(s8[7340032]{0:T(1024)(128)(4,1)} %bitcast.143), calls=%async_computation.7 | async-start | bytes 6291456
  200.4 4.3 %slice-start = ((s8[7340032]{0:T(1024)(128)(4,1)}), s8[4194304]{0:T(1024)(128)(4,1)S(1)}, s32[]{:S(2)}) async-start(s8[7340032]{0:T(1024)(128)(4,1)} %bitcast.141), calls=%async_computation.4 | async-start | bytes 8388608
  203.0 1.9 slice-start.1
  215.7 66.5 %all-to-all-start.3 = ((bf16[32,48,896]{2,1,0:T(8,128)(2,1)}), bf16[32,48,896]{2,1,0:T(8,128)(2,1)}, u32[]{:S(2)}, u32[]{:S(2)}) async-start(bf16[32,48,896]{2,1,0:T(8,128)(2,1)} %bitcast.136), calls=%async_computation.3 | async-start | bytes 5505024 | tf_op jit(solution)/shard_map/all_to_all | solution.py:44
  220.4 7.2 %copy-start.3 = (bf16[24,8,8,896]{3,1,2,0:T(8,128)(2,1)S(1)}, bf16[24,8,8,896]{3,1,2,0:T(8,128)(2,1)}, u32[]{:S(2)}) copy-start(bf16[24,8,8,896]{3,1,2,0:T(8,128)(2,1)} %copy-done.2) | copy-start | bytes 8257540
  227.6 61.6 %copy-start.1 = (bf16[1024,896]{1,0:T(8,128)(2,1)S(1)}, bf16[1024,896]{1,0:T(8,128)(2,1)}, u32[]{:S(2)}) copy-start(bf16[1024,896]{1,0:T(8,128)(2,1)} %param.8) | copy-start | bytes 5505028
where the time goes:
time: 290 us; the launch traced here: 289 us
  waiting for transfers between devices  165 us (57%)
  matrix products  44.2 us (15%)
  other arithmetic  25.6 us (9%)
  local copies, waits for them, and re-layouts  22.5 us (8%)
  starting transfers between devices  21.5 us (7%)
  blocking collectives  9.44 us (3%)
    all_to_all x1, waiting for transfers between devices, deliver(): lax.all_to_all(spread(grad_payload), ('expert', 'dp'), split_axis=0, conc...  59.8 us
    all_to_all x1, waiting for transfers between devices, deliver(): lax.all_to_all(spread(payload), ('expert', 'dp'), split_axis=0, concat_ax...  55.7 us
    all_to_all x1, waiting for transfers between devices, give_back(): lax.all_to_all(outgoing, ('expert', 'dp'), split_axis=0, concat_axis=0, t...  49.4 us
    reduce_sum x2, other arithmetic, slot_tables(): slot_of = jnp.sum(matches * before[:, :, None, :], axis=3)  19.5 us
    all_gather x1, blocking collectives, per_device(): shard_routes = lax.all_gather(routes, 'expert', axis=0, tiled=True)  9.44 us
    all_to_all x1, starting transfers between devices, deliver(): lax.all_to_all(spread(gate_slots), ('expert', 'dp'), split_axis=0, concat...  7.3 us
    dot_general x1, matrix products, expert_pass(): lax.dot_general(token_rows, grad_up, first_dims, preferred_element_type=j...  7.15 us
    transpose x2, local copies, waits for them, and re-layouts, regroup(): return jnp.swapaxes(values, 0, 1)  6.65 us
  transfers between devices with their start and end apart: 4, of which 3 were waited for; matrix products, arithmetic and copies ran while one was open for 18% of the time, Pallas kernels for 0%

commit v1 on v0

v1 whole, which is shorter than its diff:
```python
import functools
import math

import jax
import jax.numpy as jnp
from jax import lax
from jax.experimental import pallas as pl
from jax.experimental.pallas import tpu as pltpu
from jax.sharding import PartitionSpec as P

BF = jnp.bfloat16
F32 = jnp.float32
VMEM_LIMIT = 48 * 1024 * 1024
ROWS_DIMS = (((1,), (1,)), ((), ()))
FIRST_DIMS = (((0,), (0,)), ((), ()))


def params(*semantics):
    return pltpu.CompilerParams(
        vmem_limit_bytes=VMEM_LIMIT, dimension_semantics=semantics or None
    )


def cost(flops, moved):
    return pl.CostEstimate(flops=int(flops), bytes_accessed=int(moved), transcendentals=0)


def compact_kernel(dims, table_ref, x_ref, dy_ref, x1, d1, x2, d2, gates_ref, onehot_ref):
    experts, blocks, own, top, first, second = dims
    tokens = blocks * own
    table = table_ref[...].astype(F32)
    ids = lax.broadcasted_iota(jnp.int32, (experts, 1), 0).astype(F32)
    match = jnp.zeros((experts, tokens), F32)
    weight = jnp.zeros((experts, tokens), F32)
    for k in range(top):
        hit = table[k : k + 1, :] == ids
        match = match + jnp.where(hit, 1.0, 0.0)
        weight = weight + jnp.where(hit, table[top + k : top + k + 1, :], 0.0)
    earlier = (
        lax.broadcasted_iota(jnp.int32, (own, own), 0)
        < lax.broadcasted_iota(jnp.int32, (own, own), 1)
    )
    earlier = jnp.where(earlier, 1.0, 0.0).astype(BF)
    codes = []
    for b in range(blocks):
        part = match[:, b * own : (b + 1) * own]
        rank = jnp.dot(part.astype(BF), earlier, preferred_element_type=F32)
        codes.append(jnp.where(part > 0.0, rank * blocks + b, -1.0))
    code = jnp.concatenate(codes, axis=1)
    slots = lax.broadcasted_iota(jnp.int32, (first + second, 1), 0).astype(F32)
    for e in range(experts):
        placed = jnp.where(slots == code[e : e + 1, :], 1.0, 0.0)
        coef = jnp.sum(placed * weight[e : e + 1, :], axis=1, keepdims=True)
        gates_ref[e] = jnp.broadcast_to(coef, (first + second, 128)).astype(BF)
        placed = placed.astype(BF)
        onehot_ref[e * first : (e + 1) * first, :] = placed[:first]
        start = experts * first + e * second
        onehot_ref[start : start + second, :] = placed[first:]
    split = experts * first
    for src, one, two in ((x_ref, x1, x2), (dy_ref, d1, d2)):
        rows = jnp.dot(onehot_ref[...], src[...], preferred_element_type=F32).astype(BF)
        one[...] = rows[:split].reshape(one.shape)
        two[...] = rows[split:].reshape(two.shape)


def compact(table, x, dy, experts, blocks, own, first, second):
    top = table.shape[0] // 2
    feat = x.shape[1]
    rows = experts * (first + second)
    tokens = blocks * own
    big = jax.ShapeDtypeStruct((experts, first, feat), BF)
    small = jax.ShapeDtypeStruct((experts, second, feat), BF)
    return pl.pallas_call(
        functools.partial(compact_kernel, (experts, blocks, own, top, first, second)),
        out_shape=(
            big,
            big,
            small,
            small,
            jax.ShapeDtypeStruct((experts, first + second, 128), BF),
            jax.ShapeDtypeStruct((rows, tokens), BF),
        ),
        compiler_params=params(),
        cost_estimate=cost(4 * rows * tokens * feat, 4 * tokens * feat + 4 * rows * feat),
        name="compact",
    )(table, x, dy)


def up_kernel(slots, *refs):
    x, (w_gate, w_up, gate_pre, up_proj) = refs[:slots], refs[slots:]
    rows = jnp.concatenate([r[0] for r in x], axis=0)

    @pl.when(pl.program_id(0) == 0)
    def _():
        gate_pre[...] = jnp.zeros_like(gate_pre)
        up_proj[...] = jnp.zeros_like(up_proj)

    gate_pre[...] += jnp.dot(rows, w_gate[0], preferred_element_type=F32)
    up_proj[...] += jnp.dot(rows, w_up[0], preferred_element_type=F32)


def up(x, w_gate, w_up):
    pieces, rows, feat = x[0].shape
    hidden = w_gate.shape[2]
    total = len(x) * rows
    x_spec = pl.BlockSpec((1, rows, feat), lambda f: (f, 0, 0))
    w_spec = pl.BlockSpec((1, feat, hidden), lambda f: (0, f, 0))
    o_spec = pl.BlockSpec((total, hidden), lambda f: (0, 0))
    out = jax.ShapeDtypeStruct((total, hidden), F32)
    return pl.pallas_call(
        functools.partial(up_kernel, len(x)),
        grid=(pieces,),
        in_specs=[x_spec] * len(x) + [w_spec] * 2,
        out_specs=(o_spec, o_spec),
        out_shape=(out, out),
        compiler_params=params("arbitrary"),
        cost_estimate=cost(4 * total * pieces * feat * hidden, 4 * pieces * feat * hidden),
        name="up",
    )(*x, w_gate, w_up)


def hidden_kernel(slots, start, origin, *refs):
    dy, (w_down, gates, gate_pre, up_proj, grad_gate, grad_up, acc) = refs[:slots], refs[slots:]
    rows = jnp.concatenate([r[0] for r in dy], axis=0)
    count = dy[0].shape[1]

    @pl.when(pl.program_id(0) == 0)
    def _():
        acc[...] = jnp.zeros_like(acc)

    acc[...] += lax.dot_general(rows, w_down[0], ROWS_DIMS, preferred_element_type=F32)

    @pl.when(pl.program_id(0) == pl.num_programs(0) - 1)
    def _():
        coef = jnp.concatenate(
            [gates[origin[k], start : start + count, :1] for k in range(slots)], axis=0
        )
        pre = gate_pre[...]
        sigma = jax.nn.sigmoid(pre)
        grad_hidden = coef.astype(F32) * acc[...]
        grad_gate[...] = (
            grad_hidden * up_proj[...] * sigma * (1.0 + pre * (1.0 - sigma))
        ).astype(BF)
        grad_up[...] = (grad_hidden * (pre * sigma)).astype(BF)


def hidden_grads(dy, w_down, gates, origin, start, gate_pre, up_proj):
    pieces, rows, feat = dy[0].shape
    hidden = w_down.shape[1]
    total = len(dy) * rows
    whole = lambda shape: pl.BlockSpec(shape, lambda f, o: (0,) * len(shape))
    out = jax.ShapeDtypeStruct((total, hidden), BF)
    return pl.pallas_call(
        functools.partial(hidden_kernel, len(dy), start),
        grid_spec=pltpu.PrefetchScalarGridSpec(
            num_scalar_prefetch=1,
            grid=(pieces,),
            in_specs=[pl.BlockSpec((1, rows, feat), lambda f, o: (f, 0, 0))] * len(dy)
            + [
                pl.BlockSpec((1, hidden, feat), lambda f, o: (0, 0, f)),
                whole(gates.shape),
                whole((total, hidden)),
                whole((total, hidden)),
            ],
            out_specs=(whole((total, hidden)), whole((total, hidden))),
            scratch_shapes=[pltpu.VMEM((total, hidden), F32)],
        ),
        out_shape=(out, out),
        compiler_params=params("arbitrary"),
        cost_estimate=cost(2 * total * pieces * feat * hidden, 2 * pieces * feat * hidden),
        name="hidden_grads",
    )(origin, *dy, w_down, gates, gate_pre, up_proj)


def back_kernel(grad_gate, grad_up, w_gate, w_up, *outs):
    value = lax.dot_general(grad_gate[...], w_gate[0], ROWS_DIMS, preferred_element_type=F32)
    value += lax.dot_general(grad_up[...], w_up[0], ROWS_DIMS, preferred_element_type=F32)
    rows = outs[0].shape[1]
    for k, out in enumerate(outs):
        out[0] = value[k * rows : (k + 1) * rows].astype(BF)


def back(grad_gate, grad_up, w_gate, w_up, slots, pieces):
    total, hidden = grad_gate.shape
    rows = total // slots
    feat = w_gate.shape[1] // pieces
    g_spec = pl.BlockSpec((total, hidden), lambda f: (0, 0))
    w_spec = pl.BlockSpec((1, feat, hidden), lambda f: (0, f, 0))
    return pl.pallas_call(
        back_kernel,
        grid=(pieces,),
        in_specs=[g_spec, g_spec, w_spec, w_spec],
        out_specs=[pl.BlockSpec((1, rows, feat), lambda f: (f, 0, 0))] * slots,
        out_shape=[jax.ShapeDtypeStruct((pieces, rows, feat), BF)] * slots,
        compiler_params=params("arbitrary"),
        cost_estimate=cost(4 * total * pieces * feat * hidden, 4 * pieces * feat * hidden),
        name="back",
    )(grad_gate, grad_up, w_gate, w_up)


def weights_kernel(slots, *refs):
    x, (gates, ups, g_gate, g_up) = refs[:slots], refs[slots:]
    rows = jnp.concatenate([r[0] for r in x], axis=0)
    g_gate[0] = lax.dot_general(rows, gates[...], FIRST_DIMS, preferred_element_type=F32).astype(BF)
    g_up[0] = lax.dot_general(rows, ups[...], FIRST_DIMS, preferred_element_type=F32).astype(BF)


def weight_grads(x, grad_gate, grad_up):
    pieces, _, feat = x[0].shape
    total, hidden = grad_gate.shape
    g_spec = pl.BlockSpec((total, hidden), lambda f: (0, 0))
    o_spec = pl.BlockSpec((1, feat, hidden), lambda f: (0, f, 0))
    out = jax.ShapeDtypeStruct((1, pieces * feat, hidden), BF)
    return pl.pallas_call(
        functools.partial(weights_kernel, len(x)),
        grid=(pieces,),
        in_specs=[pl.BlockSpec((1,) + v.shape[1:], lambda f: (f, 0, 0)) for v in x]
        + [g_spec, g_spec],
        out_specs=(o_spec, o_spec),
        out_shape=(out, out),
        compiler_params=params("arbitrary"),
        cost_estimate=cost(4 * total * pieces * feat * hidden, 4 * pieces * feat * hidden),
        name="weight_grads",
    )(*x, grad_gate, grad_up)


def scatter_kernel(onehot, one, two, out):
    split = one.shape[0]
    value = lax.dot_general(onehot[:split, :], one[...], FIRST_DIMS, preferred_element_type=F32)
    value += lax.dot_general(onehot[split:, :], two[...], FIRST_DIMS, preferred_element_type=F32)
    out[...] = value.astype(BF)


def scatter(onehot, one, two):
    rows, tokens = onehot.shape
    feat = one.shape[1]
    return pl.pallas_call(
        scatter_kernel,
        out_shape=jax.ShapeDtypeStruct((tokens, feat), BF),
        compiler_params=params(),
        cost_estimate=cost(2 * rows * tokens * feat, 2 * rows * tokens + 4 * tokens * feat),
        name="scatter",
    )(onehot, one, two)


def line_steps(n):
    right = {s: [(i, i + 1) for i in range(s - 1, n - 1)] for s in range(1, n)}
    left = {s: [(i, i - 1) for i in range(1, n - s + 1)] for s in range(1, n)}
    return right, left


def gather_line(arrays):
    n = lax.axis_size("dp")
    me = lax.axis_index("dp")
    right, left = line_steps(n)
    from_left = [{0: a} for a in arrays]
    from_right = [{0: a} for a in arrays]
    for s in range(1, n):
        for r, l in zip(from_left, from_right):
            r[s] = lax.ppermute(r[s - 1], "dp", right[s])
            l[s] = lax.ppermute(l[s - 1], "dp", left[s])
    return [
        [a] + [jnp.where(me >= k, r[k], l[n - k]) for k in range(1, n)]
        for a, r, l in zip(arrays, from_left, from_right)
    ]


def add(*values):
    total = values[0].astype(F32)
    for v in values[1:]:
        total = total + v.astype(F32)
    return total.astype(BF)


def sum_line(slots):
    n = len(slots)
    got_r, got_l = [], []
    for s in range(1, n):
        out_r = add(slots[s], *got_r)
        out_l = add(slots[n - s], *got_l)
        got_r = [lax.ppermute(out_r, "dp", [(i, i + 1) for i in range(s)])]
        got_l = [lax.ppermute(out_l, "dp", [(i, i - 1) for i in range(n - s, n)])]
    return add(slots[0], *got_r, *got_l)


def widen(values, fold):
    if fold == 1:
        return values
    pieces, rows, feat = values.shape
    values = values.reshape(pieces // fold, fold, rows, feat)
    return jnp.swapaxes(values, 1, 2).reshape(pieces // fold, rows, fold * feat)


def narrow(values, fold):
    if fold == 1:
        return values
    pieces, rows, feat = values.shape
    values = values.reshape(pieces, rows, fold, feat // fold)
    return jnp.swapaxes(values, 1, 2).reshape(pieces * fold, rows, feat // fold)


def per_device(attn_rows, out_grad, routes, gates, w_gate, w_up, w_down):
    experts = lax.axis_size("expert")
    groups = lax.axis_size("dp")
    own, top = routes.shape
    feat = attn_rows.shape[1]
    capacity = 3 * own // 64
    late = capacity // 3
    first, second = (capacity - late) * experts, late * experts
    fold = 128 // math.gcd(feat, 128)
    pieces = experts // fold

    named = jnp.minimum(routes, experts).astype(BF)
    table = lax.all_gather(jnp.concatenate([named, gates], axis=1), "expert", axis=0, tiled=True)
    x1, d1, x2, d2, coef, onehot = compact(
        table.T, attn_rows, out_grad, experts, experts, own, first, second
    )

    def exchange(values):
        return lax.all_to_all(values, "expert", split_axis=0, concat_axis=0, tiled=True)

    x1, d1, x2, d2 = exchange(x1), exchange(d1), exchange(x2), exchange(d2)
    own_coef = lax.dynamic_index_in_dim(coef, lax.axis_index("expert"), 0, keepdims=False)
    all_coef = lax.all_gather(own_coef, "dp", axis=0)
    origin = lax.rem(
        lax.axis_index("dp") + groups - jnp.arange(groups, dtype=jnp.int32), groups
    ).astype(jnp.int32)

    x1s, d1s = gather_line([x1, d1])
    x2s, d2s = gather_line([x2, d2])
    x1s, d1s, x2s, d2s = [[widen(v, fold) for v in s] for s in (x1s, d1s, x2s, d2s)]

    def chunk(xs, ds, start):
        gate_pre, up_proj = up(xs, w_gate, w_up)
        grad_gate, grad_up = hidden_grads(ds, w_down, all_coef, origin, start, gate_pre, up_proj)
        parts = back(grad_gate, grad_up, w_gate, w_up, groups, pieces)
        summed = exchange(sum_line([narrow(v, fold) for v in parts]))
        return summed.reshape(-1, feat), grad_gate, grad_up

    sum1, gg1, gu1 = chunk(x1s, d1s, 0)
    sum2, gg2, gu2 = chunk(x2s, d2s, first)
    g_gate, g_up = weight_grads(
        x1s + x2s, jnp.concatenate([gg1, gg2], axis=0), jnp.concatenate([gu1, gu2], axis=0)
    )
    return scatter(onehot, sum1, sum2), g_gate, g_up


def solution(mesh):
    return jax.shard_map(
        per_device,
        mesh=mesh,
        in_specs=(
            P("dp", "expert"),
            P("dp", "expert"),
            P(("dp", "expert"), None),
            P(("dp", "expert"), None),
            P("expert", None, "dp"),
            P("expert", None, "dp"),
            P("expert", "dp", None),
        ),
        out_specs=(P("dp", "expert"), P("expert", None, "dp"), P("expert", None, "dp")),
        check_vma=False,
    )
```

time: 290 us -> 280 us (0.966)
  waiting for transfers between devices: 165 us -> 67.5 us
  Pallas kernels: 0 us -> 65 us
  starting transfers between devices: 21.5 us -> 82.5 us
  matrix products: 44.2 us -> 0 us
  blocking collectives: 9.44 us -> 44.8 us
  local copies, waits for them, and re-layouts: 22.5 us -> 5.69 us
  other arithmetic: 25.6 us -> 10.8 us
    all_to_all x4, waiting for transfers between devices: 165 us -> 3.74 us  [exchange(): lax.all_to_all(values, 'expert', split_axis=0, concat_axis=0, tiled=True)]
    ppermute x0 -> x36, starting transfers between devices: none -> 67.5 us  [the longest x6 25.2 us: sum_line(): got_r = [lax.ppermute(out_r, 'dp', [(i, i + 1) for i in range(s)])]]
    pallas_call x0 -> x9, Pallas kernels: none -> 65 us  [the longest x2 19.5 us: back(): pl.pallas_call(back_kernel, grid=(pieces,), in_specs=[g_spec, g_spec, w_s...]
    ppermute x0 -> x36, waiting for transfers between devices: none -> 63.7 us  [the longest x12 47.6 us: gather_line(): l[s] = lax.ppermute(l[s - 1], 'dp', left[s])]
    dot_general x12 -> x0, matrix products: 44.2 us -> none  [the longest x1 7.15 us: expert_pass(): lax.dot_general(token_rows, grad_up, first_dims, preferred_element_type=j...]
    reduce_sum x5 -> x0, other arithmetic: 24.3 us -> none  [the longest x2 19.5 us: slot_tables(): slot_of = jnp.sum(matches * before[:, :, None, :], axis=3)]
    all_to_all x0 -> x2, blocking collectives: none -> 18.1 us  [exchange(): lax.all_to_all(values, 'expert', split_axis=0, concat_axis=0, tiled=True)]
    all_gather x1 -> x2, blocking collectives: 9.44 us -> 26.6 us  [the longest x1 16.3 us: per_device(): all_coef = lax.all_gather(own_coef, 'dp', axis=0)]
  transfers between devices with their start and end apart: 4 -> 40, of which waited for: 3 -> 11; matrix products, arithmetic and copies ran while one was open for 18% -> 3% of each run, Pallas kernels for 0% -> 22%
where the time goes in v1:
time: 280 us; the launch traced here: 278 us
  starting transfers between devices  82.5 us (29%)
  waiting for transfers between devices  67.5 us (24%)
  Pallas kernels  65 us (23%)
  blocking collectives  44.8 us (16%)
  other arithmetic  10.8 us (4%)
  local copies, waits for them, and re-layouts  5.69 us (2%)
    ppermute x12, waiting for transfers between devices, gather_line(): l[s] = lax.ppermute(l[s - 1], 'dp', left[s])  47.6 us
    ppermute x6, starting transfers between devices, sum_line(): got_r = [lax.ppermute(out_r, 'dp', [(i, i + 1) for i in range(s)])]  25.2 us
    ppermute x12, starting transfers between devices, gather_line(): r[s] = lax.ppermute(r[s - 1], 'dp', right[s])  21.5 us
    pallas_call x2, Pallas kernels, back(): pl.pallas_call(back_kernel, grid=(pieces,), in_specs=[g_spec, g_spec, w_s...  19.5 us
    all_to_all x2, blocking collectives, exchange(): lax.all_to_all(values, 'expert', split_axis=0, concat_axis=0, tiled=True)  18.1 us
    pallas_call x2, Pallas kernels, up(): pl.pallas_call(functools.partial(up_kernel, len(x)), grid=(pieces,), in_s...  17.3 us
    all_gather x1, blocking collectives, per_device(): all_coef = lax.all_gather(own_coef, 'dp', axis=0)  16.3 us
    pallas_call x2, Pallas kernels, hidden_grads(): pl.pallas_call(functools.partial(hidden_kernel, len(dy), start), grid_spe...  15.6 us
  transfers between devices with their start and end apart: 40, of which 11 were waited for; matrix products, arithmetic and copies ran while one was open for 3% of the time, Pallas kernels for 22%

profile of v1, /device:TPU:0, one launch (start us, length us, event | category | flops | bytes accessed | tf_op | source)
XLA Modules:
  0.0 277.6 jit_solution(11454899716347168310)
XLA Ops:
  2.0 10.3 %all_gather.7 = bf16[1024,16]{0,1:T(8,128)(2,1)S(1)} all-gather(bf16[128,16]{0,1:T(8,128)(2,1)S(1)} %pad_maximum_fusion.2), channel_id=1, replica_groups=mesh['expert'=8,'dp'=4] {'expert'}, dimensions={0}, use_global_device_ids=true | all-gather | bytes 36864 | tf_op jit(solution)/shard_map/all_gather | solution.py:314
  15.3 2.8 %compact.1 = (bf16[8,32,896]{2,1,0:T(8,128)(2,1)}, bf16[8,32,896]{2,1,0:T(8,128)(2,1)}, bf16[8,16,896]{2,1,0:T(8,128)(2,1)S(1)}, bf16[8,16,896]{2,1,0:T(8,128)(2...) custom-call(bf16[16,1024]{1,0:T(8,128)(2,1)S(1)} %bitcast.5, bf16[1024,896]{1,0:T(8,128)(2,1)S(1)} %copy-done.5, ...), custom_call_target="tpu_custom_call" | custom-call | flops 1409286144 | bytes 5046272 | tf_op jit(solution)/shard_map/compact/pallas_call | solution.py:73
  19.0 9.1 %all_to_all.30.refs_0_.refs_4_ = bf16[8,16,896]{2,1,0:T(8,128)(2,1)S(1)} all-to-all(bf16[8,16,896]{2,1,0:T(8,128)(2,1)S(1)} %get-tuple-element.40), channel_id=1, replica_groups=mesh['expert'=8,'dp'=4] {'expert'}, dimensions={0} | all-to-all | bytes 458752 | tf_op jit(solution)/shard_map/all_to_all | solution.py:320
  28.2 9.0 %all_to_all.31.refs_0_ = bf16[8,16,896]{2,1,0:T(8,128)(2,1)S(1)} all-to-all(bf16[8,16,896]{2,1,0:T(8,128)(2,1)S(1)} %get-tuple-element.39), channel_id=1, replica_groups=mesh['expert'=8,'dp'=4] {'expert'}, dimensions={0} | all-to-all | bytes 458752 | tf_op jit(solution)/shard_map/all_to_all | solution.py:320
  37.1 3.5 %all-to-all-start.1 = ((bf16[8,32,896]{2,1,0:T(8,128)(2,1)}), bf16[8,32,896]{2,1,0:T(8,128)(2,1)S(1)}, u32[]{:S(2)}, u32[]{:S(2)}) async-start(bf16[8,32,896]{2,1,0:T(8,128)(2,1)} %get-tuple-element.30), calls=%async_computation.1 | async-start | bytes 917504 | tf_op jit(solution)/shard_map/all_to_all | solution.py:320
  41.9 4.6 %collective-permute-start.24 = (bf16[8,16,896]{2,1,0:T(8,128)(2,1)S(1)}, bf16[8,16,896]{2,1,0:T(8,128)(2,1)S(1)}, u32[]{:S(2)}, u32[]{:S(2)}) collective-permute-start(bf16[8,16,896]{2,1,0:T(8,128)(2,1)S(1)} %all_to_all.30.refs_0_.refs_4_), channel_id=1, source_target_pairs={{0,1},{1,2},{2,3},{4,5},{5,6},{6,7},{8,9},{9,10},{10,11},{12,13},{... | collective-permute-start | bytes 688136 | tf_op jit(solution)/shard_map/ppermute | solution.py:260
  46.5 3.1 %all-to-all-done.1.refs_0_ = bf16[8,32,896]{2,1,0:T(8,128)(2,1)S(1)} async-done(((bf16[8,32,896]{2,1,0:T(8,128)(2,1)}), bf16[8,32,896]{2,1,0:T(8,128)(2,1)S(1)}, u32[]{:S(2)}, u32[]{:S(2)}) %all-to-all-start.1) | async-done | bytes 458784 | tf_op jit(solution)/shard_map/all_to_all | solution.py:320
  49.6 3.5 %all-to-all-start = ((bf16[8,32,896]{2,1,0:T(8,128)(2,1)}), bf16[8,32,896]{2,1,0:T(8,128)(2,1)S(1)}, u32[]{:S(2)}, u32[]{:S(2)}) async-start(bf16[8,32,896]{2,1,0:T(8,128)(2,1)} %get-tuple-element.28), calls=%async_computation | async-start | bytes 917504 | tf_op jit(solution)/shard_map/all_to_all | solution.py:320
  54.4 5.3 %collective-permute-start.18 = (bf16[8,16,896]{2,1,0:T(8,128)(2,1)S(1)}, bf16[8,16,896]{2,1,0:T(8,128)(2,1)}, u32[]{:S(2)}, u32[]{:S(2)}) collective-permute-start(bf16[8,16,896]{2,1,0:T(8,128)(2,1)S(1)} %all_to_all.31.refs_0_), channel_id=1, source_target_pairs={{0,1},{1,2},{2,3},{4,5},{5,6},{6,7},{8,9},{9,10},{10,11},{12,13},{... | collective-permute-start | bytes 688136 | tf_op jit(solution)/shard_map/ppermute | solution.py:260
  62.3 16.3 %all_gather.8.refs_5_ = bf16[4,48,128]{2,1,0:T(8,128)(2,1)S(1)} all-gather(bf16[1,48,128]{2,1,0:T(8,128)(2,1)S(1)} %constant_dynamic-slice_fusion), channel_id=1, replica_groups=mesh['expert'=8,'dp'=4] {'dp'}, dimensions={0}, use_global_device_ids=true | all-gather | bytes 61440 | tf_op jit(solution)/shard_map/all_gather | solution.py:324
  86.7 20.4 %collective-permute-done.20 = bf16[8,16,896]{2,1,0:T(8,128)(2,1)S(1)} collective-permute-done((bf16[8,16,896]{2,1,0:T(8,128)(2,1)S(1)}, bf16[8,16,896]{2,1,0:T(8,128)(2,1)S(1)}, u32[]{:S(2)}, u32[]{:S(2)}) %collective-permute-start.20) | collective-permute-done | bytes 229408 | tf_op jit(solution)/shard_map/ppermute | solution.py:261
  107.1 3.1 %collective-permute-start = (bf16[8,32,896]{2,1,0:T(8,128)(2,1)S(1)}, bf16[8,32,896]{2,1,0:T(8,128)(2,1)S(1)}, u32[]{:S(2)}, u32[]{:S(2)}) collective-permute-start(bf16[8,32,896]{2,1,0:T(8,128)(2,1)S(1)} %all-to-all-done.refs_0_), channel_id=1, source_target_pairs={{0,1},{1,2},{2,3},{4,5},{5,6},{6,7},{8,9},{9,10},{10,11},{12,13},{... | collective-permute-start | bytes 1376264 | tf_op jit(solution)/shard_map/ppermute | solution.py:260
  111.5 7.4 %collective-permute-done.27 = bf16[8,16,896]{2,1,0:T(8,128)(2,1)S(1)} collective-permute-done((bf16[8,16,896]{2,1,0:T(8,128)(2,1)}, bf16[8,16,896]{2,1,0:T(8,128)(2,1)S(1)}, u32[]{:S(2)}, u32[]{:S(2)}) %collective-permute-start.27) | collective-permute-done | bytes 229408 | tf_op jit(solution)/shard_map/ppermute | solution.py:261
  120.3 6.6 %collective-permute-done.21 = bf16[8,16,896]{2,1,0:T(8,128)(2,1)S(1)} collective-permute-done((bf16[8,16,896]{2,1,0:T(8,128)(2,1)S(1)}, bf16[8,16,896]{2,1,0:T(8,128)(2,1)S(1)}, u32[]{:S(2)}, u32[]{:S(2)}) %collective-permute-start.21) | collective-permute-done | bytes 229408 | tf_op jit(solution)/shard_map/ppermute | solution.py:261
  134.3 8.6 %up.3 = (f32[64,512]{1,0:T(8,128)S(1)}, f32[64,512]{1,0:T(8,128)S(1)}) custom-call(bf16[8,16,896]{2,1,0:T(8,128)(2,1)S(1)} %all_to_all.30.refs_0_.refs_4_, bf16[8,16,896]{2,1,0:T(8,128)(2,1)S(1)} %broadcast_select_fusion.10.refs_1_.refs_5_, bf16[8,16,896]{2,1,0:T(8,128)(2,1)S(1)} %broadcast_select_fusion.8.refs_2_.refs_6_, ...), custom_call_target="tpu_custom_call" | custom-call | flops 939524096 | bytes 14680064 | tf_op jit(solution)/shard_map/up/pallas_call | solution.py:110
  142.9 7.7 %hidden_grads.3 = (bf16[64,512]{1,0:T(8,128)(2,1)S(1)}, bf16[64,512]{1,0:T(8,128)(2,1)S(1)}) custom-call(s32[4]{0:T(128)S(1)} %compare_select_fusion.origin, bf16[8,16,896]{2,1,0:T(8,128)(2,1)S(1)} %all_to_all.31.refs_0_, bf16[8,16,896]{2,1,0:T(8,128)(2,1)S(1)} %broadcast_select_fusion.11.refs_1_, bf16[8,16,896]{2,1,0:T(8,128)(2,1)S(1)} %broadcast_select_fusion.9.refs_2_, ...), custom_call_target="tpu_custom_call" | custom-call | flops 469762048 | bytes 7340032 | tf_op jit(solution)/shard_map/hidden_grads/pallas_call | solution.py:153
  150.6 9.7 %back.3 = (bf16[8,16,896]{2,1,0:T(8,128)(2,1)S(1)}, bf16[8,16,896]{2,1,0:T(8,128)(2,1)S(1)}, bf16[8,16,896]{2,1,0:T(8,128)(2,1)S(1)}, bf16[8,16,896]{2,1,0:T(8,128)(2,1)S(1)}) custom-call(bf16[64,512]{1,0:T(8,128)(2,1)S(1)} %get-tuple-element.43.grad_gate, bf16[64,512]{1,0:T(8,128)(2,1)S(1)} %get-tuple-element.44.grad_up, bf16[1,7168,512]{2,1,0:T(8,128)(2,1)} %w_gate.3, ...), custom_call_target="tpu_custom_call" | custom-call | flops 939524096 | bytes 14680064 | tf_op jit(solution)/shard_map/back/pallas_call | solution.py:189
  160.4 8.5 %collective-permute-start.30 = (bf16[8,16,896]{2,1,0:T(8,128)(2,1)S(1)}, bf16[8,16,896]{2,1,0:T(8,128)(2,1)S(1)}, u32[]{:S(2)}, u32[]{:S(2)}) collective-permute-start(bf16[8,16,896]{2,1,0:T(8,128)(2,1)S(1)} %get-tuple-element.48), channel_id=1, source_target_pairs={{0,1},{4,5},{8,9},{12,13},{16,17},{20,21},{24,25},{28,29}} | collective-permute-start | bytes 688136 | tf_op jit(solution)/shard_map/ppermute | solution.py:281
  173.7 8.4 %collective-permute-done.9 = bf16[8,32,896]{2,1,0:T(8,128)(2,1)S(1)} collective-permute-done((bf16[8,32,896]{2,1,0:T(8,128)(2,1)S(1)}, bf16[8,32,896]{2,1,0:T(8,128)(2,1)S(1)}, u32[]{:S(2)}, u32[]{:S(2)}) %collective-permute-start.9) | collective-permute-done | bytes 458784 | tf_op jit(solution)/shard_map/ppermute | solution.py:261
  182.3 4.8 %collective-permute-done.3 = bf16[8,32,896]{2,1,0:T(8,128)(2,1)S(1)} collective-permute-done((bf16[8,32,896]{2,1,0:T(8,128)(2,1)S(1)}, bf16[8,32,896]{2,1,0:T(8,128)(2,1)S(1)}, u32[]{:S(2)}, u32[]{:S(2)}) %collective-permute-start.3) | collective-permute-done | bytes 458784 | tf_op jit(solution)/shard_map/ppermute | solution.py:261
  187.1 8.7 %up.2 = (f32[128,512]{1,0:T(8,128)S(1)}, f32[128,512]{1,0:T(8,128)S(1)}) custom-call(bf16[8,32,896]{2,1,0:T(8,128)(2,1)S(1)} %all-to-all-done.1.refs_0_, bf16[8,32,896]{2,1,0:T(8,128)(2,1)S(1)} %broadcast_select_fusion.4.refs_1_, bf16[8,32,896]{2,1,0:T(8,128)(2,1)S(1)} %broadcast_select_fusion.2.refs_2_, ...), custom_call_target="tpu_custom_call" | custom-call | flops 1879048192 | bytes 14680064 | tf_op jit(solution)/shard_map/up/pallas_call | solution.py:110
  195.8 7.9 %hidden_grads.2 = (bf16[128,512]{1,0:T(8,128)(2,1)S(1)}, bf16[128,512]{1,0:T(8,128)(2,1)S(1)}) custom-call(s32[4]{0:T(128)S(1)} %compare_select_fusion.origin, bf16[8,32,896]{2,1,0:T(8,128)(2,1)S(1)} %all-to-all-done.refs_0_, bf16[8,32,896]{2,1,0:T(8,128)(2,1)S(1)} %broadcast_select_fusion.5.refs_1_, bf16[8,32,896]{2,1,0:T(8,128)(2,1)S(1)} %broadcast_select_fusion.3.refs_2_, ...), custom_call_target="tpu_custom_call" | custom-call | flops 939524096 | bytes 7340032 | tf_op jit(solution)/shard_map/hidden_grads/pallas_call | solution.py:153
  204.4 9.8 %back.2 = (bf16[8,32,896]{2,1,0:T(8,128)(2,1)S(1)}, bf16[8,32,896]{2,1,0:T(8,128)(2,1)S(1)}, bf16[8,32,896]{2,1,0:T(8,128)(2,1)S(1)}, bf16[8,32,896]{2,1,0:T(8,128)(2,1)S(1)}) custom-call(bf16[128,512]{1,0:T(8,128)(2,1)S(1)} %get-tuple-element.33.grad_gate, bf16[128,512]{1,0:T(8,128)(2,1)S(1)} %get-tuple-element.34.grad_up, bf16[1,7168,512]{2,1,0:T(8,128)(2,1)} %w_gate.3, ...), custom_call_target="tpu_custom_call" | custom-call | flops 1879048192 | bytes 14680064 | tf_op jit(solution)/shard_map/back/pallas_call | solution.py:189
  218.5 7.8 %collective-permute-done.12 = bf16[8,32,896]{2,1,0:T(8,128)(2,1)S(1)} collective-permute-done((bf16[8,32,896]{2,1,0:T(8,128)(2,1)S(1)}, bf16[8,32,896]{2,1,0:T(8,128)(2,1)S(1)}, u32[]{:S(2)}, u32[]{:S(2)}) %collective-permute-start.12) | collective-permute-done | bytes 458784 | tf_op jit(solution)/shard_map/ppermute | solution.py:281
  226.5 4.4 %collective-permute-start.13 = (bf16[8,32,896]{2,1,0:T(8,128)(2,1)S(1)}, bf16[8,32,896]{2,1,0:T(8,128)(2,1)S(1)}, u32[]{:S(2)}, u32[]{:S(2)}) collective-permute-start(bf16[8,32,896]{2,1,0:T(8,128)(2,1)S(1)} %get-tuple-element.51), channel_id=1, source_target_pairs={{0,1},{1,2},{4,5},{5,6},{8,9},{9,10},{12,13},{13,14},{16,17},{17,1... | collective-permute-start | bytes 1376264 | tf_op jit(solution)/shard_map/ppermute | solution.py:281
  231.2 4.4 %collective-permute-start.32 = (bf16[8,16,896]{2,1,0:T(8,128)(2,1)S(1)}, bf16[8,16,896]{2,1,0:T(8,128)(2,1)S(1)}, u32[]{:S(2)}, u32[]{:S(2)}) collective-permute-start(bf16[8,16,896]{2,1,0:T(8,128)(2,1)S(1)} %add_convert_fusion.5), channel_id=1, source_target_pairs={{0,1},{1,2},{2,3},{4,5},{5,6},{6,7},{8,9},{9,10},{10,11},{12,13},{... | collective-permute-start | bytes 688136 | tf_op jit(solution)/shard_map/ppermute | solution.py:281
  237.7 3.5 %collective-permute-done.13 = bf16[8,32,896]{2,1,0:T(8,128)(2,1)S(1)} collective-permute-done((bf16[8,32,896]{2,1,0:T(8,128)(2,1)S(1)}, bf16[8,32,896]{2,1,0:T(8,128)(2,1)S(1)}, u32[]{:S(2)}, u32[]{:S(2)}) %collective-permute-start.13) | collective-permute-done | bytes 458784 | tf_op jit(solution)/shard_map/ppermute | solution.py:281
  242.1 5.2 %collective-permute-start.14 = (bf16[8,32,896]{2,1,0:T(8,128)(2,1)}, bf16[8,32,896]{2,1,0:T(8,128)(2,1)}, u32[]{:S(2)}, u32[]{:S(2)}) collective-permute-start(bf16[8,32,896]{2,1,0:T(8,128)(2,1)} %add_convert_fusion.2), channel_id=1, source_target_pairs={{0,1},{1,2},{2,3},{4,5},{5,6},{6,7},{8,9},{9,10},{10,11},{12,13},{... | collective-permute-start | bytes 1376264 | tf_op jit(solution)/shard_map/ppermute | solution.py:281
  250.3 4.0 %all-to-all-start.5 = ((bf16[8,16,896]{2,1,0:T(8,128)(2,1)}), bf16[8,16,896]{2,1,0:T(8,128)(2,1)S(1)}, u32[]{:S(2)}, u32[]{:S(2)}) async-start(bf16[8,16,896]{2,1,0:T(8,128)(2,1)} %add_convert_fusion.3), calls=%async_computation.5 | async-start | bytes 458752 | tf_op jit(solution)/shard_map/all_to_all | solution.py:320
  254.3 4.5 %collective-permute-done.17 = bf16[8,32,896]{2,1,0:T(8,128)(2,1)} collective-permute-done((bf16[8,32,896]{2,1,0:T(8,128)(2,1)}, bf16[8,32,896]{2,1,0:T(8,128)(2,1)}, u32[]{:S(2)}, u32[]{:S(2)}) %collective-permute-start.17) | collective-permute-done | bytes 458784 | tf_op jit(solution)/shard_map/ppermute | solution.py:282
  261.0 4.0 %all-to-all-start.2 = ((bf16[8,32,896]{2,1,0:T(8,128)(2,1)}), bf16[8,32,896]{2,1,0:T(8,128)(2,1)S(1)}, u32[]{:S(2)}, u32[]{:S(2)}) async-start(bf16[8,32,896]{2,1,0:T(8,128)(2,1)} %add_convert_fusion), calls=%async_computation.2 | async-start | bytes 917504 | tf_op jit(solution)/shard_map/all_to_all | solution.py:320
  266.0 7.4 %weight_grads.1 = (bf16[1,7168,512]{2,1,0:T(8,128)(2,1)}, bf16[1,7168,512]{2,1,0:T(8,128)(2,1)}) custom-call(bf16[8,32,896]{2,1,0:T(8,128)(2,1)S(1)} %all-to-all-done.1.refs_0_, bf16[8,32,896]{2,1,0:T(8,128)(2,1)S(1)} %broadcast_select_fusion.4.refs_1_, bf16[8,32,896]{2,1,0:T(8,128)(2,1)S(1)} %broadcast_select_fusion.2.refs_2_, ...), custom_call_target="tpu_custom_call" | custom-call | flops 2818572288 | bytes 14680064 | tf_op jit(solution)/shard_map/weight_grads/pallas_call | solution.py:214
  (110 shorter events, 52.1 us)
Async XLA Ops:
  37.1 12.5 %all-to-all-start.1 = ((bf16[8,32,896]{2,1,0:T(8,128)(2,1)}), bf16[8,32,896]{2,1,0:T(8,128)(2,1)S(1)}, u32[]{:S(2)}, u32[]{:S(2)}) async-start(bf16[8,32,896]{2,1,0:T(8,128)(2,1)} %get-tuple-element.30), calls=%async_computation.1 | async-start | bytes 917504 | tf_op jit(solution)/shard_map/all_to_all | solution.py:320
  40.6 19.1 %collective-permute-start.25 = (bf16[8,16,896]{2,1,0:T(8,128)(2,1)S(1)}, bf16[8,16,896]{2,1,0:T(8,128)(2,1)S(1)}, u32[]{:S(2)}, u32[]{:S(2)}) collective-permute-start(bf16[8,16,896]{2,1,0:T(8,128)(2,1)S(1)} %all_to_all.30.refs_0_.refs_4_), channel_id=1, source_target_pairs={{1,0},{2,1},{3,2},{5,4},{6,5},{7,6},{9,8},{10,9},{11,10},{13,12},{... | collective-permute-start | bytes 688136 | tf_op jit(solution)/shard_map/ppermute | solution.py:261
  41.9 19.0 %collective-permute-start.24 = (bf16[8,16,896]{2,1,0:T(8,128)(2,1)S(1)}, bf16[8,16,896]{2,1,0:T(8,128)(2,1)S(1)}, u32[]{:S(2)}, u32[]{:S(2)}) collective-permute-start(bf16[8,16,896]{2,1,0:T(8,128)(2,1)S(1)} %all_to_all.30.refs_0_.refs_4_), channel_id=1, source_target_pairs={{0,1},{1,2},{2,3},{4,5},{5,6},{6,7},{8,9},{9,10},{10,11},{12,13},{... | collective-permute-start | bytes 688136 | tf_op jit(solution)/shard_map/ppermute | solution.py:260
  49.6 32.8 %all-to-all-start = ((bf16[8,32,896]{2,1,0:T(8,128)(2,1)}), bf16[8,32,896]{2,1,0:T(8,128)(2,1)S(1)}, u32[]{:S(2)}, u32[]{:S(2)}) async-start(bf16[8,32,896]{2,1,0:T(8,128)(2,1)} %get-tuple-element.28), calls=%async_computation | async-start | bytes 917504 | tf_op jit(solution)/shard_map/all_to_all | solution.py:320
  53.1 28.0 %collective-permute-start.19 = (bf16[8,16,896]{2,1,0:T(8,128)(2,1)S(1)}, bf16[8,16,896]{2,1,0:T(8,128)(2,1)S(1)}, u32[]{:S(2)}, u32[]{:S(2)}) collective-permute-start(bf16[8,16,896]{2,1,0:T(8,128)(2,1)S(1)} %all_to_all.31.refs_0_), channel_id=1, source_target_pairs={{1,0},{2,1},{3,2},{5,4},{6,5},{7,6},{9,8},{10,9},{11,10},{13,12},{... | collective-permute-start | bytes 688136 | tf_op jit(solution)/shard_map/ppermute | solution.py:261
  54.4 28.0 %collective-permute-start.18 = (bf16[8,16,896]{2,1,0:T(8,128)(2,1)S(1)}, bf16[8,16,896]{2,1,0:T(8,128)(2,1)}, u32[]{:S(2)}, u32[]{:S(2)}) collective-permute-start(bf16[8,16,896]{2,1,0:T(8,128)(2,1)S(1)} %all_to_all.31.refs_0_), channel_id=1, source_target_pairs={{0,1},{1,2},{2,3},{4,5},{5,6},{6,7},{8,9},{9,10},{10,11},{12,13},{... | collective-permute-start | bytes 688136 | tf_op jit(solution)/shard_map/ppermute | solution.py:260
  59.7 24.0 %collective-permute-start.26 = (bf16[8,16,896]{2,1,0:T(8,128)(2,1)S(1)}, bf16[8,16,896]{2,1,0:T(8,128)(2,1)}, u32[]{:S(2)}, u32[]{:S(2)}) collective-permute-start(bf16[8,16,896]{2,1,0:T(8,128)(2,1)S(1)} %collective-permute-done.25), channel_id=1, source_target_pairs={{1,0},{2,1},{5,4},{6,5},{9,8},{10,9},{13,12},{14,13},{17,16},{18,1... | collective-permute-start | bytes 688136 | tf_op jit(solution)/shard_map/ppermute | solution.py:261
  61.0 24.0 %collective-permute-start.28 = (bf16[8,16,896]{2,1,0:T(8,128)(2,1)S(1)}, bf16[8,16,896]{2,1,0:T(8,128)(2,1)}, u32[]{:S(2)}, u32[]{:S(2)}) collective-permute-start(bf16[8,16,896]{2,1,0:T(8,128)(2,1)S(1)} %collective-permute-done.24), channel_id=1, source_target_pairs={{1,2},{2,3},{5,6},{6,7},{9,10},{10,11},{13,14},{14,15},{17,18},{18... | collective-permute-start | bytes 688136 | tf_op jit(solution)/shard_map/ppermute | solution.py:260
  78.7 48.9 %collective-permute-start.6 = (bf16[8,32,896]{2,1,0:T(8,128)(2,1)S(1)}, bf16[8,32,896]{2,1,0:T(8,128)(2,1)S(1)}, u32[]{:S(2)}, u32[]{:S(2)}) collective-permute-start(bf16[8,32,896]{2,1,0:T(8,128)(2,1)S(1)} %all-to-all-done.1.refs_0_), channel_id=1, source_target_pairs={{0,1},{1,2},{2,3},{4,5},{5,6},{6,7},{8,9},{9,10},{10,11},{12,13},{... | collective-permute-start | bytes 1376264 | tf_op jit(solution)/shard_map/ppermute | solution.py:260
  81.1 47.2 %collective-permute-start.7 = (bf16[8,32,896]{2,1,0:T(8,128)(2,1)S(1)}, bf16[8,32,896]{2,1,0:T(8,128)(2,1)S(1)}, u32[]{:S(2)}, u32[]{:S(2)}) collective-permute-start(bf16[8,32,896]{2,1,0:T(8,128)(2,1)S(1)} %all-to-all-done.1.refs_0_), channel_id=1, source_target_pairs={{1,0},{2,1},{3,2},{5,4},{6,5},{7,6},{9,8},{10,9},{11,10},{13,12},{... | collective-permute-start | bytes 1376264 | tf_op jit(solution)/shard_map/ppermute | solution.py:261
  82.4 46.6 %collective-permute-start.1 = (bf16[8,32,896]{2,1,0:T(8,128)(2,1)S(1)}, bf16[8,32,896]{2,1,0:T(8,128)(2,1)S(1)}, u32[]{:S(2)}, u32[]{:S(2)}) collective-permute-start(bf16[8,32,896]{2,1,0:T(8,128)(2,1)S(1)} %all-to-all-done.refs_0_), channel_id=1, source_target_pairs={{1,0},{2,1},{3,2},{5,4},{6,5},{7,6},{9,8},{10,9},{11,10},{13,12},{... | collective-permute-start | bytes 1376264 | tf_op jit(solution)/shard_map/ppermute | solution.py:261
  83.7 23.4 %collective-permute-start.20 = (bf16[8,16,896]{2,1,0:T(8,128)(2,1)S(1)}, bf16[8,16,896]{2,1,0:T(8,128)(2,1)S(1)}, u32[]{:S(2)}, u32[]{:S(2)}) collective-permute-start(bf16[8,16,896]{2,1,0:T(8,128)(2,1)S(1)} %collective-permute-done.19), channel_id=1, source_target_pairs={{1,0},{2,1},{5,4},{6,5},{9,8},{10,9},{13,12},{14,13},{17,16},{18,1... | collective-permute-start | bytes 688136 | tf_op jit(solution)/shard_map/ppermute | solution.py:261
  85.0 25.1 %collective-permute-start.22 = (bf16[8,16,896]{2,1,0:T(8,128)(2,1)}, bf16[8,16,896]{2,1,0:T(8,128)(2,1)S(1)}, u32[]{:S(2)}, u32[]{:S(2)}) collective-permute-start(bf16[8,16,896]{2,1,0:T(8,128)(2,1)} %collective-permute-done.18), channel_id=1, source_target_pairs={{1,2},{2,3},{5,6},{6,7},{9,10},{10,11},{13,14},{14,15},{17,18},{18... | collective-permute-start | bytes 688136 | tf_op jit(solution)/shard_map/ppermute | solution.py:260
  107.1 23.2 %collective-permute-start = (bf16[8,32,896]{2,1,0:T(8,128)(2,1)S(1)}, bf16[8,32,896]{2,1,0:T(8,128)(2,1)S(1)}, u32[]{:S(2)}, u32[]{:S(2)}) collective-permute-start(bf16[8,32,896]{2,1,0:T(8,128)(2,1)S(1)} %all-to-all-done.refs_0_), channel_id=1, source_target_pairs={{0,1},{1,2},{2,3},{4,5},{5,6},{6,7},{8,9},{9,10},{10,11},{12,13},{... | collective-permute-start | bytes 1376264 | tf_op jit(solution)/shard_map/ppermute | solution.py:260
  128.3 40.6 %collective-permute-start.10 = (bf16[8,32,896]{2,1,0:T(8,128)(2,1)S(1)}, bf16[8,32,896]{2,1,0:T(8,128)(2,1)S(1)}, u32[]{:S(2)}, u32[]{:S(2)}) collective-permute-start(bf16[8,32,896]{2,1,0:T(8,128)(2,1)S(1)} %collective-permute-done.6), channel_id=1, source_target_pairs={{1,2},{2,3},{5,6},{6,7},{9,10},{10,11},{13,14},{14,15},{17,18},{18... | collective-permute-start | bytes 1376264 | tf_op jit(solution)/shard_map/ppermute | solution.py:260
  129.0 40.5 %collective-permute-start.8 = (bf16[8,32,896]{2,1,0:T(8,128)(2,1)S(1)}, bf16[8,32,896]{2,1,0:T(8,128)(2,1)S(1)}, u32[]{:S(2)}, u32[]{:S(2)}) collective-permute-start(bf16[8,32,896]{2,1,0:T(8,128)(2,1)S(1)} %collective-permute-done.7), channel_id=1, source_target_pairs={{1,0},{2,1},{5,4},{6,5},{9,8},{10,9},{13,12},{14,13},{17,16},{18,1... | collective-permute-start | bytes 1376264 | tf_op jit(solution)/shard_map/ppermute | solution.py:261
  130.3 40.0 %collective-permute-start.2 = (bf16[8,32,896]{2,1,0:T(8,128)(2,1)S(1)}, bf16[8,32,896]{2,1,0:T(8,128)(2,1)S(1)}, u32[]{:S(2)}, u32[]{:S(2)}) collective-permute-start(bf16[8,32,896]{2,1,0:T(8,128)(2,1)S(1)} %collective-permute-done.1), channel_id=1, source_target_pairs={{1,0},{2,1},{5,4},{6,5},{9,8},{10,9},{13,12},{14,13},{17,16},{18,1... | collective-permute-start | bytes 1376264 | tf_op jit(solution)/shard_map/ppermute | solution.py:261
  131.6 40.0 %collective-permute-start.4 = (bf16[8,32,896]{2,1,0:T(8,128)(2,1)S(1)}, bf16[8,32,896]{2,1,0:T(8,128)(2,1)S(1)}, u32[]{:S(2)}, u32[]{:S(2)}) collective-permute-start(bf16[8,32,896]{2,1,0:T(8,128)(2,1)S(1)} %collective-permute-done), channel_id=1, source_target_pairs={{1,2},{2,3},{5,6},{6,7},{9,10},{10,11},{13,14},{14,15},{17,18},{18... | collective-permute-start | bytes 1376264 | tf_op jit(solution)/shard_map/ppermute | solution.py:260
  160.4 56.0 %collective-permute-start.30 = (bf16[8,16,896]{2,1,0:T(8,128)(2,1)S(1)}, bf16[8,16,896]{2,1,0:T(8,128)(2,1)S(1)}, u32[]{:S(2)}, u32[]{:S(2)}) collective-permute-start(bf16[8,16,896]{2,1,0:T(8,128)(2,1)S(1)} %get-tuple-element.48), channel_id=1, source_target_pairs={{0,1},{4,5},{8,9},{12,13},{16,17},{20,21},{24,25},{28,29}} | collective-permute-start | bytes 688136 | tf_op jit(solution)/shard_map/ppermute | solution.py:281
  168.8 47.5 %collective-permute-start.33 = (bf16[8,16,896]{2,1,0:T(8,128)(2,1)S(1)}, bf16[8,16,896]{2,1,0:T(8,128)(2,1)S(1)}, u32[]{:S(2)}, u32[]{:S(2)}) collective-permute-start(bf16[8,16,896]{2,1,0:T(8,128)(2,1)S(1)} %get-tuple-element.46), channel_id=1, source_target_pairs={{3,2},{7,6},{11,10},{15,14},{19,18},{23,22},{27,26},{31,30}} | collective-permute-start | bytes 688136 | tf_op jit(solution)/shard_map/ppermute | solution.py:282
  170.3 11.9 %collective-permute-start.9 = (bf16[8,32,896]{2,1,0:T(8,128)(2,1)S(1)}, bf16[8,32,896]{2,1,0:T(8,128)(2,1)S(1)}, u32[]{:S(2)}, u32[]{:S(2)}) collective-permute-start(bf16[8,32,896]{2,1,0:T(8,128)(2,1)S(1)} %collective-permute-done.8), channel_id=1, source_target_pairs={{1,0},{5,4},{9,8},{13,12},{17,16},{21,20},{25,24},{29,28}} | collective-permute-start | bytes 1376264 | tf_op jit(solution)/shard_map/ppermute | solution.py:261
  172.4 14.7 %collective-permute-start.3 = (bf16[8,32,896]{2,1,0:T(8,128)(2,1)S(1)}, bf16[8,32,896]{2,1,0:T(8,128)(2,1)S(1)}, u32[]{:S(2)}, u32[]{:S(2)}) collective-permute-start(bf16[8,32,896]{2,1,0:T(8,128)(2,1)S(1)} %collective-permute-done.2), channel_id=1, source_target_pairs={{1,0},{5,4},{9,8},{13,12},{17,16},{21,20},{25,24},{29,28}} | collective-permute-start | bytes 1376264 | tf_op jit(solution)/shard_map/ppermute | solution.py:261
  214.2 12.1 %collective-permute-start.12 = (bf16[8,32,896]{2,1,0:T(8,128)(2,1)S(1)}, bf16[8,32,896]{2,1,0:T(8,128)(2,1)S(1)}, u32[]{:S(2)}, u32[]{:S(2)}) collective-permute-start(bf16[8,32,896]{2,1,0:T(8,128)(2,1)S(1)} %get-tuple-element.38), channel_id=1, source_target_pairs={{0,1},{4,5},{8,9},{12,13},{16,17},{20,21},{24,25},{28,29}} | collective-permute-start | bytes 1376264 | tf_op jit(solution)/shard_map/ppermute | solution.py:281
  216.5 14.7 %collective-permute-start.31 = (bf16[8,16,896]{2,1,0:T(8,128)(2,1)S(1)}, bf16[8,16,896]{2,1,0:T(8,128)(2,1)S(1)}, u32[]{:S(2)}, u32[]{:S(2)}) collective-permute-start(bf16[8,16,896]{2,1,0:T(8,128)(2,1)S(1)} %get-tuple-element.53), channel_id=1, source_target_pairs={{0,1},{1,2},{4,5},{5,6},{8,9},{9,10},{12,13},{13,14},{16,17},{17,1... | collective-permute-start | bytes 688136 | tf_op jit(solution)/shard_map/ppermute | solution.py:281
  217.8 18.5 %collective-permute-start.34 = (bf16[8,16,896]{2,1,0:T(8,128)(2,1)S(1)}, bf16[8,16,896]{2,1,0:T(8,128)(2,1)S(1)}, u32[]{:S(2)}, u32[]{:S(2)}) collective-permute-start(bf16[8,16,896]{2,1,0:T(8,128)(2,1)S(1)} %get-tuple-element.54), channel_id=1, source_target_pairs={{2,1},{3,2},{6,5},{7,6},{10,9},{11,10},{14,13},{15,14},{18,17},{19... | collective-permute-start | bytes 688136 | tf_op jit(solution)/shard_map/ppermute | solution.py:282
  226.5 14.8 %collective-permute-start.13 = (bf16[8,32,896]{2,1,0:T(8,128)(2,1)S(1)}, bf16[8,32,896]{2,1,0:T(8,128)(2,1)S(1)}, u32[]{:S(2)}, u32[]{:S(2)}) collective-permute-start(bf16[8,32,896]{2,1,0:T(8,128)(2,1)S(1)} %get-tuple-element.51), channel_id=1, source_target_pairs={{0,1},{1,2},{4,5},{5,6},{8,9},{9,10},{12,13},{13,14},{16,17},{17,1... | collective-permute-start | bytes 1376264 | tf_op jit(solution)/shard_map/ppermute | solution.py:281
  231.2 18.2 %collective-permute-start.32 = (bf16[8,16,896]{2,1,0:T(8,128)(2,1)S(1)}, bf16[8,16,896]{2,1,0:T(8,128)(2,1)S(1)}, u32[]{:S(2)}, u32[]{:S(2)}) collective-permute-start(bf16[8,16,896]{2,1,0:T(8,128)(2,1)S(1)} %add_convert_fusion.5), channel_id=1, source_target_pairs={{0,1},{1,2},{2,3},{4,5},{5,6},{6,7},{8,9},{9,10},{10,11},{12,13},{... | collective-permute-start | bytes 688136 | tf_op jit(solution)/shard_map/ppermute | solution.py:281
  235.7 11.7 %collective-permute-start.16 = (bf16[8,32,896]{2,1,0:T(8,128)(2,1)S(1)}, bf16[8,32,896]{2,1,0:T(8,128)(2,1)S(1)}, u32[]{:S(2)}, u32[]{:S(2)}) collective-permute-start(bf16[8,32,896]{2,1,0:T(8,128)(2,1)S(1)} %get-tuple-element.52), channel_id=1, source_target_pairs={{2,1},{3,2},{6,5},{7,6},{10,9},{11,10},{14,13},{15,14},{18,17},{19... | collective-permute-start | bytes 1376264 | tf_op jit(solution)/shard_map/ppermute | solution.py:282
  236.4 13.1 %collective-permute-start.35 = (bf16[8,16,896]{2,1,0:T(8,128)(2,1)S(1)}, bf16[8,16,896]{2,1,0:T(8,128)(2,1)S(1)}, u32[]{:S(2)}, u32[]{:S(2)}) collective-permute-start(bf16[8,16,896]{2,1,0:T(8,128)(2,1)S(1)} %add_convert_fusion.4), channel_id=1, source_target_pairs={{1,0},{2,1},{3,2},{5,4},{6,5},{7,6},{9,8},{10,9},{11,10},{13,12},{... | collective-permute-start | bytes 688136 | tf_op jit(solution)/shard_map/ppermute | solution.py:282
  242.1 12.2 %collective-permute-start.14 = (bf16[8,32,896]{2,1,0:T(8,128)(2,1)}, bf16[8,32,896]{2,1,0:T(8,128)(2,1)}, u32[]{:S(2)}, u32[]{:S(2)}) collective-permute-start(bf16[8,32,896]{2,1,0:T(8,128)(2,1)} %add_convert_fusion.2), channel_id=1, source_target_pairs={{0,1},{1,2},{2,3},{4,5},{5,6},{6,7},{8,9},{9,10},{10,11},{12,13},{... | collective-permute-start | bytes 1376264 | tf_op jit(solution)/shard_map/ppermute | solution.py:281
  250.3 10.7 %all-to-all-start.5 = ((bf16[8,16,896]{2,1,0:T(8,128)(2,1)}), bf16[8,16,896]{2,1,0:T(8,128)(2,1)S(1)}, u32[]{:S(2)}, u32[]{:S(2)}) async-start(bf16[8,16,896]{2,1,0:T(8,128)(2,1)} %add_convert_fusion.3), calls=%async_computation.5 | async-start | bytes 458752 | tf_op jit(solution)/shard_map/all_to_all | solution.py:320
  261.0 13.1 %all-to-all-start.2 = ((bf16[8,32,896]{2,1,0:T(8,128)(2,1)}), bf16[8,32,896]{2,1,0:T(8,128)(2,1)S(1)}, u32[]{:S(2)}, u32[]{:S(2)}) async-start(bf16[8,32,896]{2,1,0:T(8,128)(2,1)} %add_convert_fusion), calls=%async_computation.2 | async-start | bytes 917504 | tf_op jit(solution)/shard_map/all_to_all | solution.py:320
  (20 other events, 259.7 us)

commit v2 on v0

v2 whole, which is shorter than its diff:
```python
import functools
import math

import jax
import jax.numpy as jnp
from jax import lax
from jax.experimental import pallas as pl
from jax.experimental.pallas import tpu as pltpu
from jax.sharding import PartitionSpec as P

BF = jnp.bfloat16
F32 = jnp.float32
VMEM_LIMIT = 58 * 1024 * 1024
TILE = 16
AHEAD = 3
ROWS_DIMS = (((1,), (1,)), ((), ()))
FIRST_DIMS = (((0,), (0,)), ((), ()))


def params(*semantics):
    return pltpu.CompilerParams(
        vmem_limit_bytes=VMEM_LIMIT, dimension_semantics=semantics or None
    )


def cost(flops, moved):
    return pl.CostEstimate(flops=int(flops), bytes_accessed=int(moved), transcendentals=0)


def label_kernel(experts, routes, gates, out):
    top = routes.shape[0]
    out[:top, :] = jnp.minimum(routes[...], experts).astype(F32).astype(BF)
    out[top:, :] = gates[...]


def label(routes, gates, experts):
    top, tokens = routes.shape
    return pl.pallas_call(
        functools.partial(label_kernel, experts),
        out_shape=jax.ShapeDtypeStruct((2 * top, tokens), BF),
        name="label",
    )(routes, gates)


def compact_kernel(
    experts, table, x_hbm, dy_hbm, x_out, dy_out, gates, onehot, x_buf, dy_buf, sems
):
    blocks, labels, own = table.shape
    top = labels // 2
    loads = [
        pltpu.make_async_copy(x_hbm, x_buf, sems.at[0]),
        pltpu.make_async_copy(dy_hbm, dy_buf, sems.at[1]),
    ]
    for load in loads:
        load.start()
    ids = lax.broadcasted_iota(jnp.int32, (experts, 1), 0).astype(F32)
    earlier = (
        lax.broadcasted_iota(jnp.int32, (own, own), 0)
        < lax.broadcasted_iota(jnp.int32, (own, own), 1)
    )
    earlier = jnp.where(earlier, 1.0, 0.0).astype(BF)
    codes, weights = [], []
    for b in range(blocks):
        part = table[b].astype(F32)
        match = jnp.zeros((experts, own), F32)
        weight = jnp.zeros((experts, own), F32)
        for k in range(top):
            hit = part[k : k + 1, :] == ids
            match = match + jnp.where(hit, 1.0, 0.0)
            weight = weight + jnp.where(hit, part[top + k : top + k + 1, :], 0.0)
        rank = jnp.dot(match.astype(BF), earlier, preferred_element_type=F32)
        codes.append(jnp.where(match > 0.0, rank * blocks + b, -1.0))
        weights.append(weight)
    code = jnp.concatenate(codes, axis=1)
    weight = jnp.concatenate(weights, axis=1)
    _, per_expert, feat = x_out.shape
    slots = lax.broadcasted_iota(jnp.int32, (per_expert, 1), 0).astype(F32)
    lanes = lax.broadcasted_iota(jnp.int32, (per_expert, feat), 1)
    diagonal = lanes == lax.broadcasted_iota(jnp.int32, (per_expert, feat), 0)
    for e in range(experts):
        placed = jnp.where(slots == code[e : e + 1, :], 1.0, 0.0)
        coef = jnp.sum(placed * weight[e : e + 1, :], axis=1, keepdims=True)
        coef = jnp.sum(jnp.where(diagonal, coef, 0.0), axis=0, keepdims=True)
        gates[e] = jnp.broadcast_to(coef, (TILE, feat)).astype(BF)
        onehot[e * per_expert : (e + 1) * per_expert, :] = placed.astype(BF)
    for load, src, out in zip(loads, (x_buf, dy_buf), (x_out, dy_out)):
        load.wait()
        rows = jnp.dot(onehot[...], src[...], preferred_element_type=F32).astype(BF)
        rows = rows.reshape(experts, per_expert, feat)
        out[...] = rows


def compact(table, x, dy, experts, per_expert):
    tokens, feat = x.shape
    rows = experts * per_expert
    out = jax.ShapeDtypeStruct((experts, per_expert, feat), BF)
    return pl.pallas_call(
        functools.partial(compact_kernel, experts),
        in_specs=in_vmem(1) + [IN_HBM] * 2,
        out_shape=(
            out,
            out,
            jax.ShapeDtypeStruct((experts, TILE, feat), BF),
            jax.ShapeDtypeStruct((rows, tokens), BF),
        ),
        scratch_shapes=[
            pltpu.VMEM((tokens, feat), BF),
            pltpu.VMEM((tokens, feat), BF),
            pltpu.SemaphoreType.DMA((2,)),
        ],
        compiler_params=params(),
        cost_estimate=cost(4 * rows * tokens * feat, 4 * tokens * feat + 4 * rows * feat),
        name="compact",
    )(table, x, dy)


def in_vmem(count):
    return [pl.BlockSpec(memory_space=pltpu.VMEM)] * count


SCALAR = pl.BlockSpec(memory_space=pltpu.SMEM)
IN_HBM = pl.BlockSpec(memory_space=pl.ANY)


class Queue:
    def __init__(self, groups, ahead):
        self.groups = groups
        self.started = 0
        self.waited = 0
        self.ahead = ahead

    def wait(self):
        while self.started < min(len(self.groups), self.waited + 1 + self.ahead):
            for start, _ in self.groups[self.started]:
                start()
            self.started += 1
        for _, wait in self.groups[self.waited]:
            wait()
        self.waited += 1


def plain(copy):
    return (copy.start, copy.wait)


def column(row, rows):
    shape = (rows, row.shape[1])
    same = lax.broadcasted_iota(jnp.int32, shape, 1) == lax.broadcasted_iota(jnp.int32, shape, 0)
    return jnp.sum(jnp.where(same, row, 0.0), axis=1, keepdims=True)


def block_copies(refs, sources, me, copies):
    out = []
    for k, places in enumerate(sources):
        found = {}
        for j, place in enumerate(places):
            found.setdefault(place, []).append(j)
        options = [(copies(refs[place], k), devices) for place, devices in found.items()]

        def start(options=options):
            if len(options) == 1:
                options[0][0].start()
                return
            for copy, devices in options:
                pl.when(functools.reduce(jnp.logical_or, [me == j for j in devices]))(copy.start)

        out.append((start, options[0][0].wait))
    return out


def line_copies(refs, sources, me, buffer, sems):
    pieces, total, _ = buffer.shape
    rows = total // len(sources)
    return [
        block_copies(
            refs,
            sources,
            me,
            lambda ref, k, f=f: pltpu.make_async_copy(
                ref.at[pl.ds(f * rows, rows), :],
                buffer.at[f, pl.ds(k * rows, rows), :],
                sems.at[f],
            ),
        )
        for f in range(pieces)
    ]


def weight_copies(weights, buffer, sems, pieces, by_rows):
    size = buffer.shape[0 if by_rows else 1] // pieces
    out = []
    for f in range(pieces):
        here = pl.ds(f * size, size)
        at = (here, slice(None)) if by_rows else (slice(None), here)
        out.append(plain(pltpu.make_async_copy(weights.at[(0, *at)], buffer.at[at], sems.at[f])))
    return out


def up_kernel(count, sources, coef_at, me, *refs):
    x, coefs, refs = refs[:count], refs[count : 2 * count], refs[2 * count :]
    w_gate, w_up, gate_pre, up_proj, coef, rows_out = refs[:6]
    x_buf, coef_buf, gate_buf, up_buf, sems, coef_sem = refs[6:]
    pieces, total, feat = x_buf.shape
    blocks = len(sources)
    rows = total // blocks
    x_loads = line_copies(x, sources, me[0], x_buf, sems.at[0])
    gate_loads = weight_copies(w_gate, gate_buf, sems.at[1], pieces, True)
    up_loads = weight_copies(w_up, up_buf, sems.at[2], pieces, True)
    coef_loads = block_copies(
        coefs,
        sources,
        me[0],
        lambda ref, k: pltpu.make_async_copy(
            ref.at[pl.ds(coef_at, TILE), :], coef_buf.at[k], coef_sem.at[0]
        ),
    )
    queue = Queue(
        [[*x_loads[f], gate_loads[f], up_loads[f]] for f in range(pieces)] + [coef_loads], AHEAD
    )
    stores = []
    for f in range(pieces):
        queue.wait()
        stores.append(pltpu.make_async_copy(x_buf.at[f], rows_out.at[f], sems.at[3, f]))
        stores[-1].start()
        here = slice(f * feat, (f + 1) * feat)
        gate = jnp.dot(x_buf[f], gate_buf[here, :], preferred_element_type=F32)
        proj = jnp.dot(x_buf[f], up_buf[here, :], preferred_element_type=F32)
        if f == 0:
            gate_pre[...] = gate
            up_proj[...] = proj
        else:
            gate_pre[...] += gate
            up_proj[...] += proj
    queue.wait()
    for k in range(blocks):
        values = column(coef_buf[k][:1, :].astype(F32), rows)
        coef[k * rows : (k + 1) * rows, :] = jnp.broadcast_to(values, (rows, 128))
    for store in stores:
        store.wait()


def up(me, sources, x, coefs, coef_at, w_gate, w_up):
    feat = x[0].shape[1]
    _, model, hidden = w_gate.shape
    pieces = model // feat
    blocks = len(sources)
    total = x[0].shape[0] // pieces * blocks
    total -= total % (blocks * TILE)
    out = jax.ShapeDtypeStruct((total, hidden), F32)
    return pl.pallas_call(
        functools.partial(up_kernel, len(x), sources, coef_at),
        in_specs=[SCALAR] + [IN_HBM] * (2 * len(x) + 2),
        out_specs=in_vmem(3) + [IN_HBM],
        out_shape=(
            out,
            out,
            jax.ShapeDtypeStruct((total, 128), F32),
            jax.ShapeDtypeStruct((pieces, total, feat), BF),
        ),
        scratch_shapes=[
            pltpu.VMEM((pieces, total, feat), BF),
            pltpu.VMEM((blocks, TILE, coefs[0].shape[1]), BF),
            pltpu.VMEM((model, hidden), BF),
            pltpu.VMEM((model, hidden), BF),
            pltpu.SemaphoreType.DMA((4, pieces)),
            pltpu.SemaphoreType.DMA((1,)),
        ],
        compiler_params=params(),
        cost_estimate=cost(4 * total * model * hidden, 4 * model * hidden),
        name="up",
    )(me, *x, *coefs, w_gate, w_up)


def back_kernel(count, sources, me, *refs):
    dy, refs = refs[:count], refs[count:]
    w_down, w_gate, w_up, coef, gate_pre, up_proj, grad_gate, grad_up, parts = refs[:9]
    dy_buf, down_buf, gate_buf, up_buf, out_buf, sems, out_sems = refs[9:]
    pieces, total, feat = dy_buf.shape
    blocks = len(sources)
    rows = total // blocks
    dy_loads = line_copies(dy, sources, me[0], dy_buf, sems.at[0])
    down_loads = weight_copies(w_down, down_buf, sems.at[1], pieces, False)
    gate_loads = weight_copies(w_gate, gate_buf, sems.at[2], pieces, True)
    up_loads = weight_copies(w_up, up_buf, sems.at[3], pieces, True)
    queue = Queue(
        [[*dy_loads[f], down_loads[f]] for f in range(pieces)]
        + [[gate_loads[f], up_loads[f]] for f in range(pieces)],
        AHEAD,
    )
    value = None
    for f in range(pieces):
        queue.wait()
        here = slice(f * feat, (f + 1) * feat)
        part = lax.dot_general(dy_buf[f], down_buf[:, here], ROWS_DIMS, preferred_element_type=F32)
        value = part if value is None else value + part
    grad_hidden = coef[:, :1] * value
    pre = gate_pre[...]
    sigma = jax.nn.sigmoid(pre)
    grad_gate[...] = (
        grad_hidden * up_proj[...] * sigma * (1.0 + pre * (1.0 - sigma))
    ).astype(BF)
    grad_up[...] = (grad_hidden * (pre * sigma)).astype(BF)
    stores = []
    for f in range(pieces):
        queue.wait()
        here = slice(f * feat, (f + 1) * feat)
        value = lax.dot_general(
            grad_gate[...], gate_buf[here, :], ROWS_DIMS, preferred_element_type=F32
        )
        value += lax.dot_general(
            grad_up[...], up_buf[here, :], ROWS_DIMS, preferred_element_type=F32
        )
        out_buf[f] = value.astype(BF)
        for k in range(blocks):
            stores.append(
                pltpu.make_async_copy(
                    out_buf.at[f, pl.ds(k * rows, rows), :],
                    parts.at[f * blocks + k],
                    out_sems.at[f],
                )
            )
            stores[-1].start()
    for store in stores:
        store.wait()


def back(me, dy, sources, coef, weights, gate_pre, up_proj):
    feat = dy[0].shape[1]
    _, model, hidden = weights[1].shape
    pieces = model // feat
    blocks = len(sources)
    total = gate_pre.shape[0]
    grads = jax.ShapeDtypeStruct((total, hidden), BF)
    return pl.pallas_call(
        functools.partial(back_kernel, len(dy), sources),
        in_specs=[SCALAR] + [IN_HBM] * (len(dy) + 3) + in_vmem(3),
        out_specs=in_vmem(2) + [IN_HBM],
        out_shape=[
            grads,
            grads,
            jax.ShapeDtypeStruct((pieces * blocks, total // blocks, feat), BF),
        ],
        scratch_shapes=[
            pltpu.VMEM((pieces, total, feat), BF),
            pltpu.VMEM((hidden, model), BF),
            pltpu.VMEM((model, hidden), BF),
            pltpu.VMEM((model, hidden), BF),
            pltpu.VMEM((pieces, total, feat), BF),
            pltpu.SemaphoreType.DMA((4, pieces)),
            pltpu.SemaphoreType.DMA((pieces,)),
        ],
        compiler_params=params(),
        cost_estimate=cost(6 * total * model * hidden, 6 * model * hidden),
        name="back",
    )(me, *dy, *weights, coef, gate_pre, up_proj)


def weights_kernel(count, *refs):
    x, (gates, ups, g_gate, g_up) = refs[:count], refs[count:]
    rows = jnp.concatenate([r[0] for r in x], axis=0)
    g_gate[0] = lax.dot_general(rows, gates[...], FIRST_DIMS, preferred_element_type=F32).astype(BF)
    g_up[0] = lax.dot_general(rows, ups[...], FIRST_DIMS, preferred_element_type=F32).astype(BF)


def weight_grads(x, grad_gate, grad_up):
    pieces, _, feat = x[0].shape
    total, hidden = grad_gate.shape
    g_spec = pl.BlockSpec((total, hidden), lambda f: (0, 0))
    o_spec = pl.BlockSpec((1, feat, hidden), lambda f: (0, f, 0))
    out = jax.ShapeDtypeStruct((1, pieces * feat, hidden), BF)
    return pl.pallas_call(
        functools.partial(weights_kernel, len(x)),
        grid=(pieces,),
        in_specs=[pl.BlockSpec((1,) + v.shape[1:], lambda f: (f, 0, 0)) for v in x]
        + [g_spec, g_spec],
        out_specs=(o_spec, o_spec),
        out_shape=(out, out),
        compiler_params=params("arbitrary"),
        cost_estimate=cost(4 * total * pieces * feat * hidden, 4 * pieces * feat * hidden),
        name="weight_grads",
    )(*x, grad_gate, grad_up)


def scatter_kernel(experts, onehot_hbm, parts, out, onehot, buffer, high, low, sems):
    groups = parts.shape[0] // experts
    rows = parts.shape[1]
    queue = Queue(
        [
            [
                plain(
                    pltpu.make_async_copy(
                        parts.at[pl.ds(e * groups, groups)],
                        buffer.at[pl.ds(e * groups, groups)],
                        sems.at[e],
                    )
                )
            ]
            for e in range(experts)
        ]
        + [[plain(pltpu.make_async_copy(onehot_hbm, onehot, sems.at[experts]))]],
        experts,
    )
    for e in range(experts):
        queue.wait()
        here = slice(e * rows, (e + 1) * rows)
        total = buffer[e * groups].astype(F32)
        for g in range(1, groups):
            total += buffer[e * groups + g].astype(F32)
        high[here, :] = total.astype(BF)
        low[here, :] = (total - high[here, :].astype(F32)).astype(BF)
    queue.wait()
    value = lax.dot_general(onehot[...], high[...], FIRST_DIMS, preferred_element_type=F32)
    value += lax.dot_general(onehot[...], low[...], FIRST_DIMS, preferred_element_type=F32)
    out[...] = value.astype(BF)


def scatter(onehot, parts, experts):
    rows, tokens = onehot.shape
    feat = parts.shape[2]
    return pl.pallas_call(
        functools.partial(scatter_kernel, experts),
        in_specs=[IN_HBM] * 2,
        out_shape=jax.ShapeDtypeStruct((tokens, feat), BF),
        scratch_shapes=[
            pltpu.VMEM(onehot.shape, BF),
            pltpu.VMEM(parts.shape, BF),
            pltpu.VMEM((rows, feat), BF),
            pltpu.VMEM((rows, feat), BF),
            pltpu.SemaphoreType.DMA((experts + 1,)),
        ],
        compiler_params=params(),
        cost_estimate=cost(4 * rows * tokens * feat, 2 * rows * tokens + 4 * tokens * feat),
        name="scatter",
    )(onehot, parts)


def together(*groups):
    flat = lax.optimization_barrier([v for g in groups for v in g])
    out = []
    for g in groups:
        out.append(flat[: len(g)])
        flat = flat[len(g) :]
    return out


def send(value, pairs):
    return lax.ppermute(value, "dp", pairs)


class Gather:
    def __init__(self, value):
        self.right = [value]
        self.left = [value]

    def step(self):
        n = lax.axis_size("dp")
        s = len(self.right)
        right, left = self.right[-1], self.left[-1]
        self.right.append(send(right, [(i, i + 1) for i in range(s - 1, n - 1)]))
        self.left.append(send(left, [(i, i - 1) for i in range(1, n - s + 1)]))

    @property
    def last(self):
        return [self.right[-1], self.left[-1]]

    @last.setter
    def last(self, values):
        self.right[-1], self.left[-1] = values

    def arrays(self):
        return self.right + self.left[1:]

    @staticmethod
    def sources(n):
        def place(me, at):
            return me - at if at <= me else n - 1 + at - me

        return tuple(
            tuple(place(me, block) for me in range(n)) for block in range(n)
        )


def widen(values, fold, blocks):
    if fold == 1:
        return values
    count, rows, feat = values.shape
    values = values.reshape(count // (fold * blocks), fold, blocks, rows, feat)
    values = jnp.transpose(values, (0, 2, 3, 1, 4))
    return values.reshape(count // fold, rows, fold * feat)


def narrow(values, fold, blocks):
    if fold == 1:
        return values
    count, rows, feat = values.shape
    values = values.reshape(count // blocks, blocks, rows, fold, feat // fold)
    values = jnp.transpose(values, (0, 3, 1, 2, 4))
    return values.reshape(count * fold, rows, feat // fold)


def per_device(attn_rows, out_grad, routes, gates, w_gate, w_up, w_down):
    experts = lax.axis_size("expert")
    groups = lax.axis_size("dp")
    own, top = routes.shape
    feat = attn_rows.shape[1]
    capacity = 3 * own // 64
    rows = capacity * experts
    fold = 128 // math.gcd(feat, 128)
    pieces = experts // fold
    me = lax.axis_index("dp").astype(jnp.int32)[None]
    sources = Gather.sources(groups)

    def exchange(values, axes):
        return lax.all_to_all(values, axes, split_axis=0, concat_axis=0, tiled=True)

    table = lax.all_gather(label(routes.T, gates.T, experts), "expert", axis=0)
    x, d, coef, onehot = compact(table, attn_rows, out_grad, experts, rows)

    x = exchange(x, "expert")
    coef = lax.dynamic_index_in_dim(coef, lax.axis_index("expert"), 0, keepdims=False)
    (x,), (d,) = together([x], [d])
    gx = Gather(jnp.concatenate([x.reshape(-1, feat), coef], axis=0))
    gx.step()
    d = exchange(d, "expert")
    gx.last, (d,) = together(gx.last, [d])
    gd = Gather(d.reshape(-1, feat))
    for _ in range(groups - 2):
        gx.step()
        gd.step()
    gx.last, gd.last = together(gx.last, gd.last)
    gd.step()
    xs, dy, coefs, coef_at = gx.arrays(), gd.arrays(), gx.arrays(), experts * rows
    if fold > 1:
        xs, dy = [
            [
                widen(v[:coef_at].reshape(experts, rows, feat), fold, 1).reshape(-1, fold * feat)
                for v in arrays
            ]
            for arrays in (xs, dy)
        ]
        coefs = [v[coef_at:] for v in coefs]
        coef_at = 0
    gate_pre, up_proj, coef, x_rows = up(me, sources, xs, coefs, coef_at, w_gate, w_up)
    grad_gate, grad_up, parts = back(
        me, dy, sources, coef, (w_down, w_gate, w_up), gate_pre, up_proj
    )
    parts = exchange(narrow(parts, fold, groups), ("expert", "dp"))
    g_gate, g_up = weight_grads([x_rows], grad_gate, grad_up)
    return scatter(onehot, parts, experts), g_gate, g_up


def solution(mesh):
    return jax.shard_map(
        per_device,
        mesh=mesh,
        in_specs=(
            P("dp", "expert"),
            P("dp", "expert"),
            P(("dp", "expert"), None),
            P(("dp", "expert"), None),
            P("expert", None, "dp"),
            P("expert", None, "dp"),
            P("expert", "dp", None),
        ),
        out_specs=(P("dp", "expert"), P("expert", None, "dp"), P("expert", None, "dp")),
        check_vma=False,
    )
```

time: 290 us -> 230 us (0.79)
  Pallas kernels: 0 us -> 44.7 us
  matrix products: 44.2 us -> 0 us
  waiting for transfers between devices: 165 us -> 122 us
  other arithmetic: 25.6 us -> 0.06 us
  local copies, waits for them, and re-layouts: 22.5 us -> 3.13 us
  blocking collectives: 9.44 us -> 26.1 us
  starting transfers between devices: 21.5 us -> 31 us
    all_to_all x4 -> x2, waiting for transfers between devices: 165 us -> 62.9 us  [exchange(): return lax.all_to_all(values, axes, split_axis=0, concat_axis=0, tiled=True)]
    ppermute x0 -> x12, waiting for transfers between devices: none -> 59.5 us  [send(): return lax.ppermute(value, 'dp', pairs)]
    pallas_call x0 -> x6, Pallas kernels: none -> 44.7 us  [the longest x1 14.2 us: back(): pl.pallas_call(functools.partial(back_kernel, len(dy), sources), in_specs...]
    dot_general x12 -> x0, matrix products: 44.2 us -> none  [the longest x1 7.15 us: expert_pass(): lax.dot_general(token_rows, grad_up, first_dims, preferred_element_type=j...]
    ppermute x0 -> x12, starting transfers between devices: none -> 24.5 us  [send(): return lax.ppermute(value, 'dp', pairs)]
    reduce_sum x5 -> x0, other arithmetic: 24.3 us -> none  [the longest x2 19.5 us: slot_tables(): slot_of = jnp.sum(matches * before[:, :, None, :], axis=3)]
    all_to_all x4 -> x2, starting transfers between devices: 21.5 us -> 6.48 us  [exchange(): return lax.all_to_all(values, axes, split_axis=0, concat_axis=0, tiled=True)]
    all_to_all x0 -> x1, blocking collectives: none -> 13.9 us  [exchange(): return lax.all_to_all(values, axes, split_axis=0, concat_axis=0, tiled=True)]
  transfers between devices with their start and end apart: 4 -> 14, of which waited for: 3 -> 6; matrix products, arithmetic and copies ran while one was open for 18% -> 0% of each run, Pallas kernels for 0% -> 8%
where the time goes in v2:
time: 230 us; the launch traced here: 228 us
  waiting for transfers between devices  122 us (53%)
  Pallas kernels  44.7 us (19%)
  starting transfers between devices  31 us (13%)
  blocking collectives  26.1 us (11%)
  local copies, waits for them, and re-layouts  3.13 us (1%)
    all_to_all x2, waiting for transfers between devices, exchange(): return lax.all_to_all(values, axes, split_axis=0, concat_axis=0, tiled=True)  62.9 us
    ppermute x12, waiting for transfers between devices, send(): return lax.ppermute(value, 'dp', pairs)  59.5 us
    ppermute x12, starting transfers between devices, send(): return lax.ppermute(value, 'dp', pairs)  24.5 us
    pallas_call x1, Pallas kernels, back(): pl.pallas_call(functools.partial(back_kernel, len(dy), sources), in_specs...  14.2 us
    all_to_all x1, blocking collectives, exchange(): return lax.all_to_all(values, axes, split_axis=0, concat_axis=0, tiled=True)  13.9 us
    all_gather x1, blocking collectives, per_device(): table = lax.all_gather(label(routes.T, gates.T, experts), 'expert', axis=0)  12.2 us
    pallas_call x1, Pallas kernels, weight_grads(): pl.pallas_call(functools.partial(weights_kernel, len(x)), grid=(pieces,),...  9.52 us
    pallas_call x1, Pallas kernels, up(): pl.pallas_call(functools.partial(up_kernel, len(x), sources, coef_at), in...  9.04 us
  transfers between devices with their start and end apart: 14, of which 6 were waited for; matrix products, arithmetic and copies ran while one was open for 0% of the time, Pallas kernels for 8%

profile of v2, /device:TPU:0, one launch (start us, length us, event | category | flops | bytes accessed | tf_op | source)
XLA Modules:
  0.0 228.5 jit_solution(6894888926938781565)
XLA Ops:
  0.6 1.3 label.1
  1.9 12.2 %all-gather = bf16[128,128]{1,0:T(8,128)(2,1)} all-gather(bf16[16,128]{1,0:T(8,128)(2,1)} %label.1), channel_id=2, replica_groups=mesh['expert'=8,'dp'=4] {'expert'}, dimensions={0}, use_global_device_ids=true | all-gather | bytes 36864 | tf_op jit(solution)/shard_map/all_gather | solution.py:516
  14.1 5.2 %compact.1 = (bf16[8,48,896]{2,1,0:T(8,128)(2,1)}, bf16[8,48,896]{2,1,0:T(8,128)(2,1)}, bf16[8,16,896]{2,1,0:T(8,128)(2,1)}, bf16[384,1024]{1,0:T(8,128)(2,1)}) custom-call(bf16[8,16,128]{2,1,0:T(8,128)(2,1)} %bitcast.12, bf16[1024,896]{1,0:T(8,128)(2,1)} %x_hbm.1, bf16[1024,896]{1,0:T(8,128)(2,1)} %dy_hbm.1), custom_call_target="tpu_custom_call" | custom-call | flops 1409286144 | bytes 5046272 | tf_op jit(solution)/shard_map/compact/pallas_call | solution.py:97
  19.3 3.7 %all-to-all-start = ((bf16[8,48,896]{2,1,0:T(8,128)(2,1)}), bf16[8,48,896]{2,1,0:T(8,128)(2,1)S(1)}, u32[]{:S(2)}, u32[]{:S(2)}) async-start(bf16[8,48,896]{2,1,0:T(8,128)(2,1)} %get-tuple-element.26), calls=%async_computation | async-start | bytes 1376256 | tf_op jit(solution)/shard_map/all_to_all | solution.py:514
  23.0 0.8 dynamic-slice_bitcast_fusion
  23.8 10.7 %all-to-all-done = bf16[8,48,896]{2,1,0:T(8,128)(2,1)S(1)} async-done(((bf16[8,48,896]{2,1,0:T(8,128)(2,1)}), bf16[8,48,896]{2,1,0:T(8,128)(2,1)S(1)}, u32[]{:S(2)}, u32[]{:S(2)}) %all-to-all-start) | async-done | bytes 688160 | tf_op jit(solution)/shard_map/all_to_all | solution.py:514
  34.4 0.1 pad_maximum_fusion.refs_0_.refs_7_
  34.5 1.3 collective-permute-start.1
  35.8 4.6 %collective-permute-start = (bf16[400,896]{1,0:T(8,128)(2,1)S(1)}, bf16[400,896]{1,0:T(8,128)(2,1)S(1)}, u32[]{:S(2)}, u32[]{:S(2)}) collective-permute-start(bf16[400,896]{1,0:T(8,128)(2,1)S(1)} %pad_maximum_fusion.refs_0_.refs_7_), channel_id=1, source_target_pairs={{0,1},{1,2},{2,3},{4,5},{5,6},{6,7},{8,9},{9,10},{10,11},{12,13},{... | collective-permute-start | bytes 2150408 | tf_op jit(solution)/shard_map/ppermute | solution.py:447
  40.4 13.9 %all_to_all.15 = bf16[8,48,896]{2,1,0:T(8,128)(2,1)S(1)} all-to-all(bf16[8,48,896]{2,1,0:T(8,128)(2,1)S(1)} %copy-done.11), channel_id=1, replica_groups=mesh['expert'=8,'dp'=4] {'expert'}, dimensions={0} | all-to-all | bytes 1376256 | tf_op jit(solution)/shard_map/all_to_all | solution.py:514
  54.3 0.7 collective-permute-start.3
  55.1 1.3 collective-permute-start.5
  56.4 1.3 collective-permute-start.8
  57.7 7.6 %collective-permute-start.2 = (bf16[384,896]{1,0:T(8,128)(2,1)S(1)}, bf16[384,896]{1,0:T(8,128)(2,1)S(1)}, u32[]{:S(2)}, u32[]{:S(2)}) collective-permute-start(bf16[384,896]{1,0:T(8,128)(2,1)S(1)} %bitcast.9), channel_id=1, source_target_pairs={{0,1},{1,2},{2,3},{4,5},{5,6},{6,7},{8,9},{9,10},{10,11},{12,13},{... | collective-permute-start | bytes 2064392 | tf_op jit(solution)/shard_map/ppermute | solution.py:447
  65.3 0.7 collective-permute-start.4
  66.0 12.3 %collective-permute-done.5.refs_5_.refs_12_ = bf16[400,896]{1,0:T(8,128)(2,1)S(1)} collective-permute-done((bf16[400,896]{1,0:T(8,128)(2,1)S(1)}, bf16[400,896]{1,0:T(8,128)(2,1)S(1)}, u32[]{:S(2)}, u32[]{:S(2)}) %collective-permute-start.5) | collective-permute-done | bytes 716832 | tf_op jit(solution)/shard_map/ppermute | solution.py:447
  78.3 1.3 collective-permute-start.6
  79.6 13.5 %collective-permute-done.8.refs_4_ = bf16[384,896]{1,0:T(8,128)(2,1)S(1)} collective-permute-done((bf16[384,896]{1,0:T(8,128)(2,1)S(1)}, bf16[384,896]{1,0:T(8,128)(2,1)S(1)}, u32[]{:S(2)}, u32[]{:S(2)}) %collective-permute-start.8) | collective-permute-done | bytes 688160 | tf_op jit(solution)/shard_map/ppermute | solution.py:447
  93.0 1.3 collective-permute-start.9
  94.4 1.5 collective-permute-start.7
  95.9 26.0 %collective-permute-done.9.refs_5_ = bf16[384,896]{1,0:T(8,128)(2,1)} collective-permute-done((bf16[384,896]{1,0:T(8,128)(2,1)S(1)}, bf16[384,896]{1,0:T(8,128)(2,1)}, u32[]{:S(2)}, u32[]{:S(2)}) %collective-permute-start.9) | collective-permute-done | bytes 688160 | tf_op jit(solution)/shard_map/ppermute | solution.py:447
  121.9 0.8 copy-done.6
  122.7 1.5 collective-permute-start.10
  124.3 1.5 collective-permute-start.11
  125.8 9.0 %up.1 = (f32[192,512]{1,0:T(8,128)}, f32[192,512]{1,0:T(8,128)}, f32[192,128]{1,0:T(8,128)}, bf16[8,192,896]{2,1,0:T(8,128)(2,1)}) custom-call(s32[1]{0:T(128)} %bitcast.3.me, bf16[400,896]{1,0:T(8,128)(2,1)} %copy-done.1, bf16[400,896]{1,0:T(8,128)(2,1)} %copy-done.3, bf16[400,896]{1,0:T(8,128)(2,1)} %copy-done.4, bf16[400,896]{1,0:T(8,128)(2,1)} %copy-done.6, ...), custom_call_target="tpu_custom_call" | custom-call | flops 2818572288 | bytes 14680064 | tf_op jit(solution)/shard_map/up/pallas_call | solution.py:250
  134.8 7.7 %collective-permute-done.11.refs_6_ = bf16[384,896]{1,0:T(8,128)(2,1)} collective-permute-done((bf16[384,896]{1,0:T(8,128)(2,1)}, bf16[384,896]{1,0:T(8,128)(2,1)}, u32[]{:S(2)}, u32[]{:S(2)}) %collective-permute-start.11) | collective-permute-done | bytes 688160 | tf_op jit(solution)/shard_map/ppermute | solution.py:447
  142.5 14.2 %back.1 = (bf16[192,512]{1,0:T(8,128)(2,1)}, bf16[192,512]{1,0:T(8,128)(2,1)}, bf16[32,48,896]{2,1,0:T(8,128)(2,1)}) custom-call(s32[1]{0:T(128)} %bitcast.3.me, bf16[384,896]{1,0:T(8,128)(2,1)} %bitcast.10, bf16[384,896]{1,0:T(8,128)(2,1)} %copy-done.10, bf16[384,896]{1,0:T(8,128)(2,1)} %collective-permute-done.7.refs_2_, ...), custom_call_target="tpu_custom_call" | custom-call | flops 4227858432 | bytes 22020096 | tf_op jit(solution)/shard_map/back/pallas_call | solution.py:334
  156.7 2.8 %all-to-all-start.2 = ((bf16[32,48,896]{2,1,0:T(8,128)(2,1)}), bf16[32,48,896]{2,1,0:T(8,128)(2,1)S(1)}, u32[]{:S(2)}, u32[]{:S(2)}) async-start(bf16[32,48,896]{2,1,0:T(8,128)(2,1)} %get-tuple-element.41), calls=%async_computation.2 | async-start | bytes 5505024 | tf_op jit(solution)/shard_map/all_to_all | solution.py:514
  159.5 9.5 %weight_grads.1 = (bf16[1,7168,512]{2,1,0:T(8,128)(2,1)}, bf16[1,7168,512]{2,1,0:T(8,128)(2,1)}) custom-call(bf16[8,192,896]{2,1,0:T(8,128)(2,1)} %get-tuple-element.42.refs_0_, bf16[192,512]{1,0:T(8,128)(2,1)} %get-tuple-element.43.refs_1_, bf16[192,512]{1,0:T(8,128)(2,1)} %get-tuple-element.44.refs_2_), custom_call_target="tpu_custom_call" | custom-call | flops 2818572288 | bytes 14680064 | tf_op jit(solution)/shard_map/weight_grads/pallas_call | solution.py:371
  169.0 52.3 %all-to-all-done.2.parts = bf16[32,48,896]{2,1,0:T(8,128)(2,1)S(1)} async-done(((bf16[32,48,896]{2,1,0:T(8,128)(2,1)}), bf16[32,48,896]{2,1,0:T(8,128)(2,1)S(1)}, u32[]{:S(2)}, u32[]{:S(2)}) %all-to-all-start.2) | async-done | bytes 2752544 | tf_op jit(solution)/shard_map/all_to_all | solution.py:514
  221.3 1.5 copy-done
  222.8 5.5 %scatter.1 = bf16[1024,896]{1,0:T(8,128)(2,1)} custom-call(bf16[384,1024]{1,0:T(8,128)(2,1)} %get-tuple-element.25.onehot_hbm, bf16[32,48,896]{2,1,0:T(8,128)(2,1)} %copy-done), custom_call_target="tpu_custom_call" | custom-call | flops 1409286144 | bytes 4456448 | tf_op jit(solution)/shard_map/scatter/pallas_call | solution.py:420
  (30 shorter events, 0.1 us)
Async XLA Ops:
  19.3 21.1 %copy-start.11 = (bf16[8,48,896]{2,1,0:T(8,128)(2,1)S(1)}, bf16[8,48,896]{2,1,0:T(8,128)(2,1)}, u32[]{:S(2)}) copy-start(bf16[8,48,896]{2,1,0:T(8,128)(2,1)} %get-tuple-element.30) | copy-start | bytes 2064388
  19.3 15.1 %all-to-all-start = ((bf16[8,48,896]{2,1,0:T(8,128)(2,1)}), bf16[8,48,896]{2,1,0:T(8,128)(2,1)S(1)}, u32[]{:S(2)}, u32[]{:S(2)}) async-start(bf16[8,48,896]{2,1,0:T(8,128)(2,1)} %get-tuple-element.26), calls=%async_computation | async-start | bytes 1376256 | tf_op jit(solution)/shard_map/all_to_all | solution.py:514
  34.5 91.2 %copy-start.1 = (bf16[400,896]{1,0:T(8,128)(2,1)}, bf16[400,896]{1,0:T(8,128)(2,1)S(1)}, u32[]{:S(2)}) copy-start(bf16[400,896]{1,0:T(8,128)(2,1)S(1)} %pad_maximum_fusion.refs_0_.refs_7_) | copy-start | bytes 2150404
  34.5 19.8 %collective-permute-start.1 = (bf16[400,896]{1,0:T(8,128)(2,1)S(1)}, bf16[400,896]{1,0:T(8,128)(2,1)S(1)}, u32[]{:S(2)}, u32[]{:S(2)}) collective-permute-start(bf16[400,896]{1,0:T(8,128)(2,1)S(1)} %pad_maximum_fusion.refs_0_.refs_7_), channel_id=1, source_target_pairs={{1,0},{2,1},{3,2},{5,4},{6,5},{7,6},{9,8},{10,9},{11,10},{13,12},{... | collective-permute-start | bytes 2150408 | tf_op jit(solution)/shard_map/ppermute | solution.py:447
  35.8 18.5 %collective-permute-start = (bf16[400,896]{1,0:T(8,128)(2,1)S(1)}, bf16[400,896]{1,0:T(8,128)(2,1)S(1)}, u32[]{:S(2)}, u32[]{:S(2)}) collective-permute-start(bf16[400,896]{1,0:T(8,128)(2,1)S(1)} %pad_maximum_fusion.refs_0_.refs_7_), channel_id=1, source_target_pairs={{0,1},{1,2},{2,3},{4,5},{5,6},{6,7},{8,9},{9,10},{10,11},{12,13},{... | collective-permute-start | bytes 2150408 | tf_op jit(solution)/shard_map/ppermute | solution.py:447
  54.3 80.5 %copy-start.8 = (bf16[8,48,896]{2,1,0:T(8,128)(2,1)}, bf16[8,48,896]{2,1,0:T(8,128)(2,1)S(1)}, u32[]{:S(2)}) copy-start(bf16[8,48,896]{2,1,0:T(8,128)(2,1)S(1)} %all_to_all.15) | copy-start | bytes 2064388
  54.3 71.4 %copy-start.2 = (bf16[400,896]{1,0:T(8,128)(2,1)}, bf16[400,896]{1,0:T(8,128)(2,1)S(1)}, u32[]{:S(2)}) copy-start(bf16[400,896]{1,0:T(8,128)(2,1)S(1)} %collective-permute-done.1.refs_4_.refs_11_) | copy-start | bytes 2150404
  54.3 71.4 %copy-start.3 = (bf16[400,896]{1,0:T(8,128)(2,1)}, bf16[400,896]{1,0:T(8,128)(2,1)S(1)}, u32[]{:S(2)}) copy-start(bf16[400,896]{1,0:T(8,128)(2,1)S(1)} %collective-permute-done.refs_1_.refs_8_) | copy-start | bytes 2150404
  54.3 10.9 %collective-permute-start.3 = (bf16[400,896]{1,0:T(8,128)(2,1)S(1)}, bf16[400,896]{1,0:T(8,128)(2,1)S(1)}, u32[]{:S(2)}, u32[]{:S(2)}) collective-permute-start(bf16[400,896]{1,0:T(8,128)(2,1)S(1)} %collective-permute-done.refs_1_.refs_8_), channel_id=1, source_target_pairs={{1,2},{2,3},{5,6},{6,7},{9,10},{10,11},{13,14},{14,15},{17,18},{18... | collective-permute-start | bytes 2150408 | tf_op jit(solution)/shard_map/ppermute | solution.py:447
  55.1 23.2 %collective-permute-start.5 = (bf16[400,896]{1,0:T(8,128)(2,1)S(1)}, bf16[400,896]{1,0:T(8,128)(2,1)S(1)}, u32[]{:S(2)}, u32[]{:S(2)}) collective-permute-start(bf16[400,896]{1,0:T(8,128)(2,1)S(1)} %collective-permute-done.1.refs_4_.refs_11_), channel_id=1, source_target_pairs={{1,0},{2,1},{5,4},{6,5},{9,8},{10,9},{13,12},{14,13},{17,16},{18,1... | collective-permute-start | bytes 2150408 | tf_op jit(solution)/shard_map/ppermute | solution.py:447
  56.4 36.7 %collective-permute-start.8 = (bf16[384,896]{1,0:T(8,128)(2,1)S(1)}, bf16[384,896]{1,0:T(8,128)(2,1)S(1)}, u32[]{:S(2)}, u32[]{:S(2)}) collective-permute-start(bf16[384,896]{1,0:T(8,128)(2,1)S(1)} %bitcast.8), channel_id=1, source_target_pairs={{1,0},{2,1},{3,2},{5,4},{6,5},{7,6},{9,8},{10,9},{11,10},{13,12},{... | collective-permute-start | bytes 2064392 | tf_op jit(solution)/shard_map/ppermute | solution.py:447
  57.7 36.7 %collective-permute-start.2 = (bf16[384,896]{1,0:T(8,128)(2,1)S(1)}, bf16[384,896]{1,0:T(8,128)(2,1)S(1)}, u32[]{:S(2)}, u32[]{:S(2)}) collective-permute-start(bf16[384,896]{1,0:T(8,128)(2,1)S(1)} %bitcast.9), channel_id=1, source_target_pairs={{0,1},{1,2},{2,3},{4,5},{5,6},{6,7},{8,9},{9,10},{10,11},{12,13},{... | collective-permute-start | bytes 2064392 | tf_op jit(solution)/shard_map/ppermute | solution.py:447
  65.3 60.5 %copy-start.4 = (bf16[400,896]{1,0:T(8,128)(2,1)}, bf16[400,896]{1,0:T(8,128)(2,1)S(1)}, u32[]{:S(2)}) copy-start(bf16[400,896]{1,0:T(8,128)(2,1)S(1)} %collective-permute-done.3.refs_2_.refs_9_) | copy-start | bytes 2150404
  65.3 56.6 %collective-permute-start.4 = (bf16[400,896]{1,0:T(8,128)(2,1)S(1)}, bf16[400,896]{1,0:T(8,128)(2,1)S(1)}, u32[]{:S(2)}, u32[]{:S(2)}) collective-permute-start(bf16[400,896]{1,0:T(8,128)(2,1)S(1)} %collective-permute-done.3.refs_2_.refs_9_), channel_id=1, source_target_pairs={{2,3},{6,7},{10,11},{14,15},{18,19},{22,23},{26,27},{30,31}} | collective-permute-start | bytes 2150408 | tf_op jit(solution)/shard_map/ppermute | solution.py:447
  78.3 43.6 %copy-start.5 = (bf16[400,896]{1,0:T(8,128)(2,1)}, bf16[400,896]{1,0:T(8,128)(2,1)S(1)}, u32[]{:S(2)}) copy-start(bf16[400,896]{1,0:T(8,128)(2,1)S(1)} %collective-permute-done.5.refs_5_.refs_12_) | copy-start | bytes 2150404
  78.3 43.6 %collective-permute-start.6 = (bf16[400,896]{1,0:T(8,128)(2,1)S(1)}, bf16[400,896]{1,0:T(8,128)(2,1)S(1)}, u32[]{:S(2)}, u32[]{:S(2)}) collective-permute-start(bf16[400,896]{1,0:T(8,128)(2,1)S(1)} %collective-permute-done.5.refs_5_.refs_12_), channel_id=1, source_target_pairs={{1,0},{5,4},{9,8},{13,12},{17,16},{21,20},{25,24},{29,28}} | collective-permute-start | bytes 2150408 | tf_op jit(solution)/shard_map/ppermute | solution.py:447
  93.0 31.2 %copy-start.9 = (bf16[384,896]{1,0:T(8,128)(2,1)}, bf16[384,896]{1,0:T(8,128)(2,1)S(1)}, u32[]{:S(2)}) copy-start(bf16[384,896]{1,0:T(8,128)(2,1)S(1)} %collective-permute-done.8.refs_4_) | copy-start | bytes 2064388
  93.0 28.8 %collective-permute-start.9 = (bf16[384,896]{1,0:T(8,128)(2,1)S(1)}, bf16[384,896]{1,0:T(8,128)(2,1)}, u32[]{:S(2)}, u32[]{:S(2)}) collective-permute-start(bf16[384,896]{1,0:T(8,128)(2,1)S(1)} %collective-permute-done.8.refs_4_), channel_id=1, source_target_pairs={{1,0},{2,1},{5,4},{6,5},{9,8},{10,9},{13,12},{14,13},{17,16},{18,1... | collective-permute-start | bytes 2064392 | tf_op jit(solution)/shard_map/ppermute | solution.py:447
  94.3 29.9 %copy-start.10 = (bf16[384,896]{1,0:T(8,128)(2,1)}, bf16[384,896]{1,0:T(8,128)(2,1)S(1)}, u32[]{:S(2)}) copy-start(bf16[384,896]{1,0:T(8,128)(2,1)S(1)} %collective-permute-done.2.refs_1_) | copy-start | bytes 2064388
  94.4 27.5 %collective-permute-start.7 = (bf16[384,896]{1,0:T(8,128)(2,1)S(1)}, bf16[384,896]{1,0:T(8,128)(2,1)}, u32[]{:S(2)}, u32[]{:S(2)}) collective-permute-start(bf16[384,896]{1,0:T(8,128)(2,1)S(1)} %collective-permute-done.2.refs_1_), channel_id=1, source_target_pairs={{1,2},{2,3},{5,6},{6,7},{9,10},{10,11},{13,14},{14,15},{17,18},{18... | collective-permute-start | bytes 2064392 | tf_op jit(solution)/shard_map/ppermute | solution.py:447
  121.9 0.9 copy-start.6
  122.7 1.5 copy-start.7
  122.7 12.1 %collective-permute-start.10 = (bf16[384,896]{1,0:T(8,128)(2,1)}, bf16[384,896]{1,0:T(8,128)(2,1)}, u32[]{:S(2)}, u32[]{:S(2)}) collective-permute-start(bf16[384,896]{1,0:T(8,128)(2,1)} %collective-permute-done.7.refs_2_), channel_id=1, source_target_pairs={{2,3},{6,7},{10,11},{14,15},{18,19},{22,23},{26,27},{30,31}} | collective-permute-start | bytes 2064392 | tf_op jit(solution)/shard_map/ppermute | solution.py:447
  124.3 18.3 %collective-permute-start.11 = (bf16[384,896]{1,0:T(8,128)(2,1)}, bf16[384,896]{1,0:T(8,128)(2,1)}, u32[]{:S(2)}, u32[]{:S(2)}) collective-permute-start(bf16[384,896]{1,0:T(8,128)(2,1)} %collective-permute-done.9.refs_5_), channel_id=1, source_target_pairs={{1,0},{5,4},{9,8},{13,12},{17,16},{21,20},{25,24},{29,28}} | collective-permute-start | bytes 2064392 | tf_op jit(solution)/shard_map/ppermute | solution.py:447
  156.7 64.6 %all-to-all-start.2 = ((bf16[32,48,896]{2,1,0:T(8,128)(2,1)}), bf16[32,48,896]{2,1,0:T(8,128)(2,1)S(1)}, u32[]{:S(2)}, u32[]{:S(2)}) async-start(bf16[32,48,896]{2,1,0:T(8,128)(2,1)} %get-tuple-element.41), calls=%async_computation.2 | async-start | bytes 5505024 | tf_op jit(solution)/shard_map/all_to_all | solution.py:514
  221.3 1.5 copy-start

commit v3 on v2

v3 whole, which is shorter than its diff:
```python
import functools
import math

import jax
import jax.numpy as jnp
from jax import lax
from jax.experimental import pallas as pl
from jax.experimental.pallas import tpu as pltpu
from jax.sharding import PartitionSpec as P

BF = jnp.bfloat16
F32 = jnp.float32
TILE = 16
AHEAD = 8
ROWS_DIMS = (((1,), (1,)), ((), ()))
FIRST_DIMS = (((0,), (0,)), ((), ()))


def params(*semantics, limit=58):
    return pltpu.CompilerParams(
        vmem_limit_bytes=limit * 1024 * 1024, dimension_semantics=semantics or None
    )


def cost(flops, moved):
    return pl.CostEstimate(flops=int(flops), bytes_accessed=int(moved), transcendentals=0)


def label(routes, gates, experts):
    top = routes.shape[0]
    named = jnp.pad(jnp.minimum(routes, experts).astype(F32), ((0, top), (0, 0)))
    return (named + jnp.pad(gates.astype(F32), ((top, 0), (0, 0)))).astype(BF)


def compact_kernel(
    experts, first, second, table, x_hbm, dy_hbm, early, late, gates, onehot, x_buf, dy_buf, sems
):
    blocks, labels, own = table.shape
    top = labels // 2
    feat = x_hbm.shape[1]
    loads = [
        pltpu.make_async_copy(x_hbm, x_buf, sems.at[0]),
        pltpu.make_async_copy(dy_hbm, dy_buf, sems.at[1]),
    ]
    for load in loads:
        load.start()
    ids = lax.broadcasted_iota(jnp.int32, (experts, 1), 0).astype(F32)
    earlier = (
        lax.broadcasted_iota(jnp.int32, (own, own), 0)
        < lax.broadcasted_iota(jnp.int32, (own, own), 1)
    )
    earlier = jnp.where(earlier, 1.0, 0.0).astype(BF)
    codes, weights = [], []
    for b in range(blocks):
        part = table[b].astype(F32)
        match = jnp.zeros((experts, own), F32)
        weight = jnp.zeros((experts, own), F32)
        for k in range(top):
            hit = part[k : k + 1, :] == ids
            match = match + jnp.where(hit, 1.0, 0.0)
            weight = weight + jnp.where(hit, part[top + k : top + k + 1, :], 0.0)
        rank = jnp.dot(match.astype(BF), earlier, preferred_element_type=F32)
        codes.append(jnp.where(match > 0.0, rank * blocks + b, -1.0))
        weights.append(weight)
    code = jnp.concatenate(codes, axis=1)
    weight = jnp.concatenate(weights, axis=1)
    per_expert = first + second
    slots = lax.broadcasted_iota(jnp.int32, (per_expert, 1), 0).astype(F32)
    lanes = lax.broadcasted_iota(jnp.int32, (per_expert, feat), 1)
    diagonal = lanes == lax.broadcasted_iota(jnp.int32, (per_expert, feat), 0)
    for e in range(experts):
        placed = jnp.where(slots == code[e : e + 1, :], 1.0, 0.0)
        coef = jnp.sum(placed * weight[e : e + 1, :], axis=1, keepdims=True)
        coef = jnp.sum(jnp.where(diagonal, coef, 0.0), axis=0, keepdims=True)
        gates[e] = jnp.broadcast_to(coef, (TILE, feat)).astype(BF)
        onehot[e * per_expert : (e + 1) * per_expert, :] = placed.astype(BF)
    for k, (load, src) in enumerate(zip(loads, (x_buf, dy_buf))):
        load.wait()
        rows = jnp.dot(onehot[...], src[...], preferred_element_type=F32).astype(BF)
        rows = rows.reshape(experts, per_expert, feat)
        early[:, k * first : (k + 1) * first] = rows[:, :first]
        late[:, k * second : (k + 1) * second] = rows[:, first:]


def compact(table, x, dy, experts, first, second):
    tokens, feat = x.shape
    rows = experts * (first + second)
    return pl.pallas_call(
        functools.partial(compact_kernel, experts, first, second),
        in_specs=in_vmem(1) + [IN_HBM] * 2,
        out_shape=(
            jax.ShapeDtypeStruct((experts, 2 * first, feat), BF),
            jax.ShapeDtypeStruct((experts, 2 * second, feat), BF),
            jax.ShapeDtypeStruct((experts, TILE, feat), BF),
            jax.ShapeDtypeStruct((rows, tokens), BF),
        ),
        scratch_shapes=[
            pltpu.VMEM((tokens, feat), BF),
            pltpu.VMEM((tokens, feat), BF),
            pltpu.SemaphoreType.DMA((2,)),
        ],
        compiler_params=params(),
        cost_estimate=cost(4 * rows * tokens * feat, 4 * tokens * feat + 4 * rows * feat),
        name="compact",
    )(table, x, dy)


def in_vmem(count):
    return [pl.BlockSpec(memory_space=pltpu.VMEM)] * count


SCALAR = pl.BlockSpec(memory_space=pltpu.SMEM)
IN_HBM = pl.BlockSpec(memory_space=pl.ANY)


def column(row, rows):
    shape = (rows, row.shape[1])
    same = lax.broadcasted_iota(jnp.int32, shape, 1) == lax.broadcasted_iota(jnp.int32, shape, 0)
    return jnp.sum(jnp.where(same, row, 0.0), axis=1, keepdims=True)


class Queue:
    def __init__(self, groups, ahead):
        self.groups = groups
        self.started = 0
        self.waited = 0
        self.ahead = ahead

    def wait(self):
        while self.started < min(len(self.groups), self.waited + 1 + self.ahead):
            for start, _ in self.groups[self.started]:
                start()
            self.started += 1
        for _, wait in self.groups[self.waited]:
            wait()
        self.waited += 1


def plain(copy):
    return (copy.start, copy.wait)


def column(row, rows):
    shape = (rows, row.shape[1])
    same = lax.broadcasted_iota(jnp.int32, shape, 1) == lax.broadcasted_iota(jnp.int32, shape, 0)
    return jnp.sum(jnp.where(same, row, 0.0), axis=1, keepdims=True)


def block_copies(refs, choices, end, copies):
    out = []
    for k, choice in enumerate(choices):
        copy = copies(refs[choice[0]], k)
        if len(choice) == 1:
            out.append(plain(copy))
            continue
        other = copies(refs[choice[1]], k)

        def start(copy=copy, other=other):
            pl.when(end == 0)(copy.start)
            pl.when(end != 0)(other.start)

        out.append((start, copy.wait))
    return out


def block_copies(refs, sources, me, copies):
    out = []
    for k, places in enumerate(sources):
        found = {}
        for j, place in enumerate(places):
            found.setdefault(place, []).append(j)
        options = [(copies(refs[place], k), devices) for place, devices in found.items()]

        def start(options=options):
            if len(options) == 1:
                options[0][0].start()
                return
            for copy, devices in options:
                pl.when(functools.reduce(jnp.logical_or, [me == j for j in devices]))(copy.start)

        out.append((start, options[0][0].wait))
    return out


def weight_copies(weights, buffer, sems, pieces, by_rows):
    size = buffer.shape[0 if by_rows else 1] // pieces
    out = []
    for f in range(pieces):
        here = pl.ds(f * size, size)
        at = (here, slice(None)) if by_rows else (slice(None), here)
        out.append(plain(pltpu.make_async_copy(weights.at[(0, *at)], buffer.at[at], sems.at[f])))
    return out


def expert_kernel(counts, sources, coef_sources, start, coef_at, me, *refs):
    blocks = len(sources)
    arrays, refs = refs[: counts[0]], refs[counts[0] :]
    coefs, refs = refs[: counts[1]], refs[counts[1] :]
    w_down, w_gate, w_up, rows_out, grad_gate, grad_up = refs[:6]
    parts, refs = refs[6 : 6 + blocks], refs[6 + blocks :]
    x_buf, dy_buf, coef_buf, down_buf, gate_buf, up_buf, gate_pre, up_proj, out_buf = refs[:-3]
    sems, coef_sem, out_sems = refs[-3:]
    pieces, total, feat = x_buf.shape
    rows = total // blocks

    def load(buffer, second, sem):
        return [
            block_copies(
                arrays,
                sources,
                me[0],
                lambda ref, k, f=f: pltpu.make_async_copy(
                    ref.at[pl.ds((2 * f + second) * rows, rows), :],
                    buffer.at[f, pl.ds(k * rows, rows), :],
                    sem.at[f],
                ),
            )
            for f in range(pieces)
        ]

    coef_loads = block_copies(
        coefs,
        coef_sources,
        me[0],
        lambda ref, k: pltpu.make_async_copy(
            ref.at[pl.ds(coef_at, TILE), :], coef_buf.at[k], coef_sem.at[0]
        ),
    )
    x_loads = load(x_buf, 0, sems.at[0])
    dy_loads = load(dy_buf, 1, sems.at[1])
    down_loads = weight_copies(w_down, down_buf, sems.at[2], pieces, False)
    gate_loads = weight_copies(w_gate, gate_buf, sems.at[3], pieces, True)
    up_loads = weight_copies(w_up, up_buf, sems.at[4], pieces, True)
    queue = Queue(
        [[*dy_loads[f], down_loads[f]] for f in range(pieces)]
        + [coef_loads]
        + [[*x_loads[f], gate_loads[f], up_loads[f]] for f in range(pieces)],
        AHEAD,
    )
    value = None
    for f in range(pieces):
        queue.wait()
        here = slice(f * feat, (f + 1) * feat)
        part = lax.dot_general(dy_buf[f], down_buf[:, here], ROWS_DIMS, preferred_element_type=F32)
        value = part if value is None else value + part
    queue.wait()
    coef = [column(coef_buf[k][:1, :].astype(F32), start + rows)[start:] for k in range(blocks)]
    grad_hidden = jnp.concatenate(coef, axis=0) * value
    stores = []
    for f in range(pieces):
        queue.wait()
        stores.append(pltpu.make_async_copy(x_buf.at[f], rows_out.at[f], out_sems.at[0, f]))
        stores[-1].start()
        here = slice(f * feat, (f + 1) * feat)
        gate = jnp.dot(x_buf[f], gate_buf[here, :], preferred_element_type=F32)
        proj = jnp.dot(x_buf[f], up_buf[here, :], preferred_element_type=F32)
        if f == 0:
            gate_pre[...] = gate
            up_proj[...] = proj
        else:
            gate_pre[...] += gate
            up_proj[...] += proj
    pre = gate_pre[...]
    sigma = jax.nn.sigmoid(pre)
    grad_gate[...] = (
        grad_hidden * up_proj[...] * sigma * (1.0 + pre * (1.0 - sigma))
    ).astype(BF)
    grad_up[...] = (grad_hidden * (pre * sigma)).astype(BF)
    for f in range(pieces):
        here = slice(f * feat, (f + 1) * feat)
        value = lax.dot_general(
            grad_gate[...], gate_buf[here, :], ROWS_DIMS, preferred_element_type=F32
        )
        value += lax.dot_general(
            grad_up[...], up_buf[here, :], ROWS_DIMS, preferred_element_type=F32
        )
        out_buf[f] = value.astype(BF)
        for k in range(blocks):
            stores.append(
                pltpu.make_async_copy(
                    out_buf.at[f, pl.ds(k * rows, rows), :],
                    parts[k].at[f],
                    out_sems.at[1, f],
                )
            )
            stores[-1].start()
    for store in stores:
        store.wait()


def expert_pass(me, sources, arrays, coef_sources, coefs, coef_at, weights, start, rows):
    feat = arrays[0].shape[1]
    _, model, hidden = weights[1].shape
    pieces = model // feat
    blocks = len(sources)
    total = rows * blocks
    grads = jax.ShapeDtypeStruct((total, hidden), BF)
    big = (pieces, total, feat)
    results = pl.pallas_call(
        functools.partial(
            expert_kernel, (len(arrays), len(coefs)), sources, coef_sources, start, coef_at
        ),
        in_specs=[SCALAR] + [IN_HBM] * (len(arrays) + len(coefs) + 3),
        out_specs=[IN_HBM] + in_vmem(2) + [IN_HBM] * blocks,
        out_shape=[
            jax.ShapeDtypeStruct(big, BF),
            grads,
            grads,
        ]
        + [jax.ShapeDtypeStruct((pieces, rows, feat), BF)] * blocks,
        scratch_shapes=[
            pltpu.VMEM(big, BF),
            pltpu.VMEM(big, BF),
            pltpu.VMEM((blocks, TILE, coefs[0].shape[1]), BF),
            pltpu.VMEM((hidden, model), BF),
            pltpu.VMEM((model, hidden), BF),
            pltpu.VMEM((model, hidden), BF),
            pltpu.VMEM((total, hidden), F32),
            pltpu.VMEM((total, hidden), F32),
            pltpu.VMEM(big, BF),
            pltpu.SemaphoreType.DMA((5, pieces)),
            pltpu.SemaphoreType.DMA((1,)),
            pltpu.SemaphoreType.DMA((2, pieces)),
        ],
        compiler_params=params(),
        cost_estimate=cost(10 * total * model * hidden, 6 * model * hidden),
        name="expert",
    )(me, *arrays, *coefs, *weights)
    return results[0], results[1:3], results[3:]


def weights_kernel(count, *refs):
    x, gates, ups = refs[:count], refs[count : 2 * count], refs[2 * count : 3 * count]
    g_gate, g_up = refs[3 * count :]
    rows = jnp.concatenate([r[0] for r in x], axis=0)
    for grads, out in ((gates, g_gate), (ups, g_up)):
        values = jnp.concatenate([r[...] for r in grads], axis=0)
        out[0] = lax.dot_general(
            rows, values, FIRST_DIMS, preferred_element_type=F32
        ).astype(BF)


def weight_grads(x, gates, ups):
    pieces, _, feat = x[0].shape
    hidden = gates[0].shape[1]
    total = sum(v.shape[1] for v in x)
    g_specs = [pl.BlockSpec(v.shape, lambda f: (0, 0)) for v in gates]
    o_spec = pl.BlockSpec((1, feat, hidden), lambda f: (0, f, 0))
    out = jax.ShapeDtypeStruct((1, pieces * feat, hidden), BF)
    return pl.pallas_call(
        functools.partial(weights_kernel, len(x)),
        grid=(pieces,),
        in_specs=[pl.BlockSpec((1,) + v.shape[1:], lambda f: (f, 0, 0)) for v in x]
        + g_specs * 2,
        out_specs=(o_spec, o_spec),
        out_shape=(out, out),
        compiler_params=params("arbitrary"),
        cost_estimate=cost(4 * total * pieces * feat * hidden, 4 * pieces * feat * hidden),
        name="weight_grads",
    )(*x, *gates, *ups)


def scatter_kernel(onehot, rows, out):
    rows = rows[...].reshape(onehot.shape[0], out.shape[1])
    value = lax.dot_general(onehot[...], rows, FIRST_DIMS, preferred_element_type=F32)
    out[...] = value.astype(BF)


def scatter(onehot, values):
    rows, tokens = onehot.shape
    feat = values.shape[2]
    return pl.pallas_call(
        scatter_kernel,
        out_shape=jax.ShapeDtypeStruct((tokens, feat), BF),
        compiler_params=params(limit=16),
        cost_estimate=cost(2 * rows * tokens * feat, 2 * rows * tokens + 4 * tokens * feat),
        name="scatter",
    )(onehot, values)


def together(*groups):
    flat = lax.optimization_barrier([v for g in groups for v in g])
    out = []
    for g in groups:
        out.append(flat[: len(g)])
        flat = flat[len(g) :]
    return out


FOUR = 4
TWO_ON = [(i, (i + 2) % FOUR) for i in range(FOUR)]
PAIRS = [(i, i ^ 1) for i in range(FOUR)]
MIDDLE = [(1, 2), (2, 1)]
OUTWARD = [(1, 0), (2, 3)]
INWARD = [(0, 1), (3, 2)]


def send(value, pairs):
    return lax.ppermute(value, "dp", pairs)


def shift(n, k):
    return [(i, (i + k) % n) for i in range(n)]


def origin(n, block, me):
    return me ^ (0, 2, 1, 3)[block] if n == FOUR else (me - block) % n


class Steps:
    def __init__(self, value):
        self.right = [value]
        self.left = [value]

    def step(self):
        n = lax.axis_size("dp")
        s = len(self.right)
        right, left = self.right[-1], self.left[-1]
        self.right.append(send(right, [(i, i + 1) for i in range(s - 1, n - 1)]))
        self.left.append(send(left, [(i, i - 1) for i in range(1, n - s + 1)]))

    @property
    def last(self):
        return [self.right[-1], self.left[-1]]

    @last.setter
    def last(self, values):
        self.right[-1], self.left[-1] = values

    @property
    def got(self):
        return self.right + self.left[1:]

    @staticmethod
    def sources(n):
        def place(me, at):
            return me - at if at <= me else n - 1 + at - me

        return tuple(tuple(place(j, origin(n, k, j)) for j in range(n)) for k in range(n))


class Gather:
    def __init__(self, value):
        self.got = [value]

    def middle(self):
        if lax.axis_size("dp") == FOUR:
            self.got.append(send(self.got[0], MIDDLE))

    def first(self):
        own, n = self.got[0], lax.axis_size("dp")
        if n == FOUR:
            self.got += [send(own, TWO_ON), send(own, PAIRS)]
        else:
            self.got += [send(own, shift(n, k)) for k in range(1, n)]

    def second(self):
        if lax.axis_size("dp") == FOUR:
            self.got.append(send(self.got[2], OUTWARD))

    @staticmethod
    def sources(n):
        if n == FOUR:
            return ((0,) * n, (2,) * n, (3,) * n, (4, 1, 1, 4))
        return tuple((k,) * n for k in range(n))


def add(*values):
    total = values[0].astype(F32)
    for v in values[1:]:
        total = total + v.astype(F32)
    return total.astype(BF)


class Sum:
    def __init__(self, parts):
        self.parts = parts
        self.got = []

    def first(self):
        n = len(self.parts)
        if n == FOUR:
            self.got = [send(self.parts[3], INWARD), send(self.parts[3], MIDDLE)]
        else:
            self.got = [send(self.parts[k], shift(n, n - k)) for k in range(1, n)]

    def second(self):
        if len(self.parts) == FOUR:
            inward, middle = self.got
            two_on = send(add(self.parts[1], inward), TWO_ON)
            self.got = [two_on, send(self.parts[2], PAIRS), middle]

    def result(self):
        return add(self.parts[0], *self.got)


def widen(values, fold):
    pieces, rows, feat = values.shape
    values = values.reshape(pieces // fold, fold, rows, feat)
    values = jnp.swapaxes(values, 1, 2) if fold > 1 else values
    return values.reshape(pieces // fold * rows, fold * feat)


def narrow(values, fold):
    if fold == 1:
        return values
    pieces, rows, feat = values.shape
    values = values.reshape(pieces, rows, fold, feat // fold)
    return jnp.swapaxes(values, 1, 2).reshape(pieces * fold, rows, feat // fold)


def per_device(attn_rows, out_grad, routes, gates, w_gate, w_up, w_down):
    experts = lax.axis_size("expert")
    groups = lax.axis_size("dp")
    own, top = routes.shape
    feat = attn_rows.shape[1]
    capacity = 3 * own // 64
    late = capacity // 3
    first, second = (capacity - late) * experts, late * experts
    rows = first + second
    fold = 128 // math.gcd(feat, 128)
    pieces = experts // fold
    here = lax.axis_index("dp").astype(jnp.int32)
    me = here[None]
    weights = (w_down, w_gate, w_up)

    def exchange(values):
        return lax.all_to_all(values, "expert", split_axis=0, concat_axis=0, tiled=True)

    table = lax.all_gather(label(routes.T, gates.T, experts), "expert", axis=0)
    early, late, coef, onehot = compact(table, attn_rows, out_grad, experts, first, second)
    early = exchange(early)
    coef = lax.dynamic_index_in_dim(coef, lax.axis_index("expert"), 0, keepdims=False)
    (early, coef), (late,) = together([early, coef], [late])
    one = Steps(jnp.concatenate([early.reshape(-1, feat), coef], axis=0))
    one.step()
    late = exchange(late)
    one.last, (late,) = together(one.last, [late])
    for _ in range(groups - 3):
        one.step()
    one.last, (late,) = together(one.last, [late])
    two = Gather(late.reshape(-1, feat))
    one.step()
    two.middle()
    one.last, two.got = together(one.last, two.got)
    two.first()
    coef_at = 2 * experts * first
    coefs = one.got if fold == 1 else [v[coef_at:] for v in one.got]
    coef_sources = Steps.sources(groups)

    def run(sources, arrays, start, count):
        if fold > 1:
            size = 2 * experts * count
            arrays = [
                widen(v[:size].reshape(experts, 2 * count, feat), fold) for v in arrays
            ]
        at = coef_at if fold == 1 else 0
        x_rows, grads, parts = expert_pass(
            me, sources, arrays, coef_sources, coefs, at, weights, start, count
        )
        return x_rows, grads, [narrow(v, fold) for v in parts]

    xs1, grads1, parts1 = run(coef_sources, one.got, 0, first)
    two.got, parts1 = together(two.got, parts1)
    two.second()
    back1 = Sum(parts1)
    back1.first()
    two.got, back1.got = together(two.got, back1.got)
    back1.second()
    xs2, grads2, parts2 = run(Gather.sources(groups), two.got, first, second)
    back1.got, parts2 = together(back1.got, parts2)
    back2 = Sum(parts2)
    back2.first()
    g_gate, g_up = weight_grads([xs1, xs2], *[list(pair) for pair in zip(grads1, grads2)])
    back2.second()
    total = jnp.concatenate([back1.result(), back2.result()], axis=1)
    return scatter(onehot, exchange(total)), g_gate, g_up


def solution(mesh):
    return jax.shard_map(
        per_device,
        mesh=mesh,
        in_specs=(
            P("dp", "expert"),
            P("dp", "expert"),
            P(("dp", "expert"), None),
            P(("dp", "expert"), None),
            P("expert", None, "dp"),
            P("expert", None, "dp"),
            P("expert", "dp", None),
        ),
        out_specs=(P("dp", "expert"), P("expert", None, "dp"), P("expert", None, "dp")),
        check_vma=False,
    )
```

time: 230 us -> 208 us (0.904)
  waiting for transfers between devices: 122 us -> 82.6 us
  starting transfers between devices: 31 us -> 44.3 us
  other arithmetic: 0.06 us -> 4.84 us
  Pallas kernels: 44.7 us -> 49 us
    all_to_all x2, waiting for transfers between devices: 62.9 us -> 14.6 us  [exchange(): lax.all_to_all(values, 'expert', split_axis=0, concat_axis=0, tiled=True)]
    ppermute x12 -> x18, starting transfers between devices: 24.5 us -> 33.4 us  [send(): return lax.ppermute(value, 'dp', pairs)]
    ppermute x12 -> x18, waiting for transfers between devices: 59.5 us -> 68 us  [send(): return lax.ppermute(value, 'dp', pairs)]
    all_to_all x2, starting transfers between devices: 6.48 us -> 10.9 us  [exchange(): lax.all_to_all(values, 'expert', split_axis=0, concat_axis=0, tiled=True)]
    convert_element_type x0 -> x6, other arithmetic: none -> 3.85 us  [the longest x4 2.47 us: add(): return total.astype(BF)]
    pallas_call x5 -> x4, Pallas kernels: 35.2 us -> 38.8 us  [the longest x2 31 us: expert_pass(): pl.pallas_call(functools.partial(expert_kernel, (len(arrays), len(coefs))...]
  transfers between devices with their start and end apart: 14 -> 20, of which waited for: 6 -> 11; matrix products, arithmetic and copies ran while one was open for 0% -> 2% of each run, Pallas kernels for 8% -> 20%
where the time goes in v3:
time: 208 us; the launch traced here: 207 us
  waiting for transfers between devices  82.6 us (40%)
  Pallas kernels  49 us (24%)
  starting transfers between devices  44.3 us (21%)
  blocking collectives  23.9 us (11%)
  other arithmetic  4.84 us (2%)
    ppermute x18, waiting for transfers between devices, send(): return lax.ppermute(value, 'dp', pairs)  68 us
    ppermute x18, starting transfers between devices, send(): return lax.ppermute(value, 'dp', pairs)  33.4 us
    pallas_call x2, Pallas kernels, expert_pass(): pl.pallas_call(functools.partial(expert_kernel, (len(arrays), len(coefs))...  31 us
    all_to_all x2, waiting for transfers between devices, exchange(): lax.all_to_all(values, 'expert', split_axis=0, concat_axis=0, tiled=True)  14.6 us
    all_to_all x1, blocking collectives, exchange(): lax.all_to_all(values, 'expert', split_axis=0, concat_axis=0, tiled=True)  12.4 us
    all_gather x1, blocking collectives, per_device(): table = lax.all_gather(label(routes.T, gates.T, experts), 'expert', axis=0)  11.5 us
    all_to_all x2, starting transfers between devices, exchange(): lax.all_to_all(values, 'expert', split_axis=0, concat_axis=0, tiled=True)  10.9 us
    pallas_call x1, Pallas kernels, weight_grads(): pl.pallas_call(functools.partial(weights_kernel, len(x)), grid=(pieces,),...  10.1 us
  transfers between devices with their start and end apart: 20, of which 11 were waited for; matrix products, arithmetic and copies ran while one was open for 2% of the time, Pallas kernels for 20%

profile of v3, /device:TPU:0, one launch (start us, length us, event | category | flops | bytes accessed | tf_op | source)
XLA Modules:
  0.0 207.3 jit_solution(3364189118720433625)
XLA Ops:
  2.0 11.5 %all-gather = bf16[128,128]{1,0:T(8,128)(2,1)} all-gather(bf16[16,128]{1,0:T(8,128)(2,1)S(1)} %add_convert_fusion.4), channel_id=2, replica_groups=mesh['expert'=8,'dp'=4] {'expert'}, dimensions={0}, use_global_device_ids=true | all-gather | bytes 36864 | tf_op jit(solution)/shard_map/all_gather | solution.py:530
  13.5 5.4 %compact.1 = (bf16[8,64,896]{2,1,0:T(8,128)(2,1)}, bf16[8,32,896]{2,1,0:T(8,128)(2,1)}, bf16[8,16,896]{2,1,0:T(8,128)(2,1)}, bf16[384,1024]{1,0:T(8,128)(2,1)}) custom-call(bf16[8,16,128]{2,1,0:T(8,128)(2,1)} %bitcast.14, bf16[1024,896]{1,0:T(8,128)(2,1)} %x_hbm.1, bf16[1024,896]{1,0:T(8,128)(2,1)} %dy_hbm.1), custom_call_target="tpu_custom_call" | custom-call | flops 1409286144 | bytes 5046272 | tf_op jit(solution)/shard_map/compact/pallas_call | solution.py:88
  18.9 3.6 %all-to-all-start = ((bf16[8,64,896]{2,1,0:T(8,128)(2,1)}), bf16[8,64,896]{2,1,0:T(8,128)(2,1)S(1)}, u32[]{:S(2)}, u32[]{:S(2)}) async-start(bf16[8,64,896]{2,1,0:T(8,128)(2,1)} %get-tuple-element.59), calls=%async_computation | async-start | bytes 1835008 | tf_op jit(solution)/shard_map/all_to_all | solution.py:528
  23.2 13.2 %all-to-all-done = bf16[8,64,896]{2,1,0:T(8,128)(2,1)S(1)} async-done(((bf16[8,64,896]{2,1,0:T(8,128)(2,1)}), bf16[8,64,896]{2,1,0:T(8,128)(2,1)S(1)}, u32[]{:S(2)}, u32[]{:S(2)}) %all-to-all-start) | async-done | bytes 917536 | tf_op jit(solution)/shard_map/all_to_all | solution.py:528
  36.5 1.3 collective-permute-start.1
  37.8 4.6 %collective-permute-start = (bf16[528,896]{1,0:T(8,128)(2,1)S(1)}, bf16[528,896]{1,0:T(8,128)(2,1)S(1)}, u32[]{:S(2)}, u32[]{:S(2)}) collective-permute-start(bf16[528,896]{1,0:T(8,128)(2,1)S(1)} %pad_maximum_fusion.refs_0_.refs_7_.refs_5_), channel_id=1, source_target_pairs={{0,1},{1,2},{2,3},{4,5},{5,6},{6,7},{8,9},{9,10},{10,11},{12,13},{... | collective-permute-start | bytes 2838536 | tf_op jit(solution)/shard_map/ppermute | solution.py:399
  42.4 12.4 %all_to_all.15 = bf16[8,32,896]{2,1,0:T(8,128)(2,1)S(1)} all-to-all(bf16[8,32,896]{2,1,0:T(8,128)(2,1)} %get-tuple-element.64), channel_id=1, replica_groups=mesh['expert'=8,'dp'=4] {'expert'}, dimensions={0} | all-to-all | bytes 917504 | tf_op jit(solution)/shard_map/all_to_all | solution.py:528
  54.8 3.4 %collective-permute-done.1.refs_4_.refs_11_.refs_9_ = bf16[528,896]{1,0:T(8,128)(2,1)S(1)} collective-permute-done((bf16[528,896]{1,0:T(8,128)(2,1)S(1)}, bf16[528,896]{1,0:T(8,128)(2,1)S(1)}, u32[]{:S(2)}, u32[]{:S(2)}) %collective-permute-start.1) | collective-permute-done | bytes 946208 | tf_op jit(solution)/shard_map/ppermute | solution.py:399
  58.2 1.2 collective-permute-done.refs_1_.refs_8_.refs_6_
  60.1 1.3 collective-permute-start.3
  61.5 22.5 %collective-permute-done.3.refs_5_.refs_12_.refs_10_ = bf16[528,896]{1,0:T(8,128)(2,1)S(1)} collective-permute-done((bf16[528,896]{1,0:T(8,128)(2,1)S(1)}, bf16[528,896]{1,0:T(8,128)(2,1)S(1)}, u32[]{:S(2)}, u32[]{:S(2)}) %collective-permute-start.3) | collective-permute-done | bytes 946208 | tf_op jit(solution)/shard_map/ppermute | solution.py:399
  84.7 1.3 collective-permute-start.5
  86.7 24.1 %collective-permute-done.5.refs_6_.refs_13_.refs_11_ = bf16[528,896]{1,0:T(8,128)(2,1)S(1)} collective-permute-done((bf16[528,896]{1,0:T(8,128)(2,1)S(1)}, bf16[528,896]{1,0:T(8,128)(2,1)S(1)}, u32[]{:S(2)}, u32[]{:S(2)}) %collective-permute-start.5) | collective-permute-done | bytes 946208 | tf_op jit(solution)/shard_map/ppermute | solution.py:399
  112.6 15.9 %expert.2 = (bf16[8,128,896]{2,1,0:T(8,128)(2,1)}, bf16[128,512]{1,0:T(8,128)(2,1)}, bf16[128,512]{1,0:T(8,128)(2,1)}, bf16[8,32,896]{2,1,0:T(8,128)(2,1)}, bf16...) custom-call(s32[1]{0:T(128)} %bitcast.6.me, bf16[528,896]{1,0:T(8,128)(2,1)} %copy-done.1, ...), custom_call_target="tpu_custom_call" | custom-call | flops 4697620480 | bytes 22020096 | tf_op jit(solution)/shard_map/expert/pallas_call | solution.py:299
  128.6 1.3 collective-permute-start.9
  130.6 7.7 %collective-permute-start.10 = (bf16[8,32,896]{2,1,0:T(8,128)(2,1)}, bf16[8,32,896]{2,1,0:T(8,128)(2,1)S(1)}, u32[]{:S(2)}, u32[]{:S(2)}) collective-permute-start(bf16[8,32,896]{2,1,0:T(8,128)(2,1)} %get-tuple-element.85), channel_id=1, source_target_pairs={{0,1},{3,2},{4,5},{7,6},{8,9},{11,10},{12,13},{15,14},{16,17},{19,... | collective-permute-start | bytes 1376264 | tf_op jit(solution)/shard_map/ppermute | solution.py:399
  138.4 3.1 %collective-permute-done.9.refs_4_ = bf16[256,896]{1,0:T(8,128)(2,1)S(1)} collective-permute-done((bf16[256,896]{1,0:T(8,128)(2,1)}, bf16[256,896]{1,0:T(8,128)(2,1)S(1)}, u32[]{:S(2)}, u32[]{:S(2)}) %collective-permute-start.9) | collective-permute-done | bytes 458784 | tf_op jit(solution)/shard_map/ppermute | solution.py:399
  141.5 3.0 %collective-permute-done.10 = bf16[8,32,896]{2,1,0:T(8,128)(2,1)S(1)} collective-permute-done((bf16[8,32,896]{2,1,0:T(8,128)(2,1)}, bf16[8,32,896]{2,1,0:T(8,128)(2,1)S(1)}, u32[]{:S(2)}, u32[]{:S(2)}) %collective-permute-start.10) | collective-permute-done | bytes 458784 | tf_op jit(solution)/shard_map/ppermute | solution.py:399
  144.5 1.1 add_convert_fusion.1
  145.6 5.8 %collective-permute-start.12 = (bf16[8,32,896]{2,1,0:T(8,128)(2,1)S(1)}, bf16[8,32,896]{2,1,0:T(8,128)(2,1)S(1)}, u32[]{:S(2)}, u32[]{:S(2)}) collective-permute-start(bf16[8,32,896]{2,1,0:T(8,128)(2,1)S(1)} %add_convert_fusion.1), channel_id=1, source_target_pairs={{0,2},{1,3},{2,0},{3,1},{4,6},{5,7},{6,4},{7,5},{8,10},{9,11},{10,... | collective-permute-start | bytes 1376264 | tf_op jit(solution)/shard_map/ppermute | solution.py:399
  151.4 15.1 %expert.3 = (bf16[8,64,896]{2,1,0:T(8,128)(2,1)}, bf16[64,512]{1,0:T(8,128)(2,1)}, bf16[64,512]{1,0:T(8,128)(2,1)}, bf16[8,16,896]{2,1,0:T(8,128)(2,1)}, bf16[8,...) custom-call(s32[1]{0:T(128)} %bitcast.6.me, bf16[256,896]{1,0:T(8,128)(2,1)} %bitcast.13, ...), custom_call_target="tpu_custom_call" | custom-call | flops 2348810240 | bytes 22020096 | tf_op jit(solution)/shard_map/expert/pallas_call | solution.py:299
  166.5 2.8 %collective-permute-done.12 = bf16[8,32,896]{2,1,0:T(8,128)(2,1)S(1)} collective-permute-done((bf16[8,32,896]{2,1,0:T(8,128)(2,1)S(1)}, bf16[8,32,896]{2,1,0:T(8,128)(2,1)S(1)}, u32[]{:S(2)}, u32[]{:S(2)}) %collective-permute-start.12) | collective-permute-done | bytes 458784 | tf_op jit(solution)/shard_map/ppermute | solution.py:399
  169.3 1.3 collective-permute-start.14
  171.3 1.4 collective-permute-start.16
  172.7 1.7 collective-permute-done.14
  174.5 1.0 add_convert_fusion.3
  175.5 3.1 %collective-permute-start.15 = (bf16[8,16,896]{2,1,0:T(8,128)(2,1)S(1)}, bf16[8,16,896]{2,1,0:T(8,128)(2,1)S(1)}, u32[]{:S(2)}, u32[]{:S(2)}) collective-permute-start(bf16[8,16,896]{2,1,0:T(8,128)(2,1)S(1)} %add_convert_fusion.3), channel_id=1, source_target_pairs={{0,2},{1,3},{2,0},{3,1},{4,6},{5,7},{6,4},{7,5},{8,10},{9,11},{10,... | collective-permute-start | bytes 688136 | tf_op jit(solution)/shard_map/ppermute | solution.py:399
  178.8 6.2 %collective-permute-done.15 = bf16[8,16,896]{2,1,0:T(8,128)(2,1)S(1)} collective-permute-done((bf16[8,16,896]{2,1,0:T(8,128)(2,1)S(1)}, bf16[8,16,896]{2,1,0:T(8,128)(2,1)S(1)}, u32[]{:S(2)}, u32[]{:S(2)}) %collective-permute-start.15) | collective-permute-done | bytes 229408 | tf_op jit(solution)/shard_map/ppermute | solution.py:399
  186.0 7.3 %all-to-all-start.2 = ((bf16[8,48,896]{2,1,0:T(8,128)(2,1)}), bf16[8,48,896]{2,1,0:T(8,128)(2,1)S(1)}, u32[]{:S(2)}, u32[]{:S(2)}) async-start(bf16[8,48,896]{2,1,0:T(8,128)(2,1)} %pad_maximum_fusion.1), calls=%async_computation.2 | async-start | bytes 1376256 | tf_op jit(solution)/shard_map/all_to_all | solution.py:528
  193.4 10.1 %weight_grads.1 = (bf16[1,7168,512]{2,1,0:T(8,128)(2,1)}, bf16[1,7168,512]{2,1,0:T(8,128)(2,1)}) custom-call(bf16[8,128,896]{2,1,0:T(8,128)(2,1)} %get-tuple-element.105.refs_0_, bf16[8,64,896]{2,1,0:T(8,128)(2,1)} %get-tuple-element.106.refs_1_, bf16[128,512]{1,0:T(8,128)(2,1)} %get-tuple-element.107.refs_2_, bf16[64,512]{1,0:T(8,128)(2,1)} %get-tuple-element.108.refs_3_, ...), custom_call_target="tpu_custom_call" | custom-call | flops 2818572288 | bytes 14680064 | tf_op jit(solution)/shard_map/weight_grads/pallas_call | solution.py:350
  203.5 1.4 all-to-all-done.2.rows
  204.9 2.5 %scatter.1 = bf16[1024,896]{1,0:T(8,128)(2,1)} custom-call(bf16[384,1024]{1,0:T(8,128)(2,1)S(1)} %copy-done, bf16[8,48,896]{2,1,0:T(8,128)(2,1)S(1)} %all-to-all-done.2.rows), custom_call_target="tpu_custom_call" | custom-call | flops 704643072 | bytes 4456448 | tf_op jit(solution)/shard_map/scatter/pallas_call | solution.py:372
  (50 shorter events, 8.9 us)
Async XLA Ops:
  18.9 17.5 %all-to-all-start = ((bf16[8,64,896]{2,1,0:T(8,128)(2,1)}), bf16[8,64,896]{2,1,0:T(8,128)(2,1)S(1)}, u32[]{:S(2)}, u32[]{:S(2)}) async-start(bf16[8,64,896]{2,1,0:T(8,128)(2,1)} %get-tuple-element.59), calls=%async_computation | async-start | bytes 1835008 | tf_op jit(solution)/shard_map/all_to_all | solution.py:528
  36.5 76.1 %copy-start.1 = (bf16[528,896]{1,0:T(8,128)(2,1)}, bf16[528,896]{1,0:T(8,128)(2,1)S(1)}, u32[]{:S(2)}) copy-start(bf16[528,896]{1,0:T(8,128)(2,1)S(1)} %pad_maximum_fusion.refs_0_.refs_7_.refs_5_) | copy-start | bytes 2838532
  36.5 21.7 %collective-permute-start.1 = (bf16[528,896]{1,0:T(8,128)(2,1)S(1)}, bf16[528,896]{1,0:T(8,128)(2,1)S(1)}, u32[]{:S(2)}, u32[]{:S(2)}) collective-permute-start(bf16[528,896]{1,0:T(8,128)(2,1)S(1)} %pad_maximum_fusion.refs_0_.refs_7_.refs_5_), channel_id=1, source_target_pairs={{1,0},{2,1},{3,2},{5,4},{6,5},{7,6},{9,8},{10,9},{11,10},{13,12},{... | collective-permute-start | bytes 2838536 | tf_op jit(solution)/shard_map/ppermute | solution.py:399
  37.8 21.6 %collective-permute-start = (bf16[528,896]{1,0:T(8,128)(2,1)S(1)}, bf16[528,896]{1,0:T(8,128)(2,1)S(1)}, u32[]{:S(2)}, u32[]{:S(2)}) collective-permute-start(bf16[528,896]{1,0:T(8,128)(2,1)S(1)} %pad_maximum_fusion.refs_0_.refs_7_.refs_5_), channel_id=1, source_target_pairs={{0,1},{1,2},{2,3},{4,5},{5,6},{6,7},{8,9},{9,10},{10,11},{12,13},{... | collective-permute-start | bytes 2838536 | tf_op jit(solution)/shard_map/ppermute | solution.py:399
  54.8 73.7 %copy-start.8 = (bf16[8,32,896]{2,1,0:T(8,128)(2,1)}, bf16[8,32,896]{2,1,0:T(8,128)(2,1)S(1)}, u32[]{:S(2)}) copy-start(bf16[8,32,896]{2,1,0:T(8,128)(2,1)S(1)} %all_to_all.15) | copy-start | bytes 1376260
  58.2 54.4 %copy-start.2 = (bf16[528,896]{1,0:T(8,128)(2,1)}, bf16[528,896]{1,0:T(8,128)(2,1)S(1)}, u32[]{:S(2)}) copy-start(bf16[528,896]{1,0:T(8,128)(2,1)S(1)} %collective-permute-done.1.refs_4_.refs_11_.refs_9_) | copy-start | bytes 2838532
  59.4 53.2 %copy-start.3 = (bf16[528,896]{1,0:T(8,128)(2,1)}, bf16[528,896]{1,0:T(8,128)(2,1)S(1)}, u32[]{:S(2)}) copy-start(bf16[528,896]{1,0:T(8,128)(2,1)S(1)} %collective-permute-done.refs_1_.refs_8_.refs_6_) | copy-start | bytes 2838532
  59.4 2.0 collective-permute-start.2
  60.1 23.8 %collective-permute-start.3 = (bf16[528,896]{1,0:T(8,128)(2,1)S(1)}, bf16[528,896]{1,0:T(8,128)(2,1)S(1)}, u32[]{:S(2)}, u32[]{:S(2)}) collective-permute-start(bf16[528,896]{1,0:T(8,128)(2,1)S(1)} %collective-permute-done.1.refs_4_.refs_11_.refs_9_), channel_id=1, source_target_pairs={{1,0},{2,1},{5,4},{6,5},{9,8},{10,9},{13,12},{14,13},{17,16},{18,1... | collective-permute-start | bytes 2838536 | tf_op jit(solution)/shard_map/ppermute | solution.py:399
  61.4 22.5 %copy-start.4 = (bf16[528,896]{1,0:T(8,128)(2,1)}, bf16[528,896]{1,0:T(8,128)(2,1)S(1)}, u32[]{:S(2)}) copy-start(bf16[528,896]{1,0:T(8,128)(2,1)S(1)} %collective-permute-done.2.refs_2_.refs_9_.refs_7_) | copy-start | bytes 2838532
  84.0 2.8 %copy-start.5 = (bf16[528,896]{1,0:T(8,128)(2,1)}, bf16[528,896]{1,0:T(8,128)(2,1)S(1)}, u32[]{:S(2)}) copy-start(bf16[528,896]{1,0:T(8,128)(2,1)S(1)} %collective-permute-done.3.refs_5_.refs_12_.refs_10_) | copy-start | bytes 2838532
  84.0 2.7 %collective-permute-start.4 = (bf16[528,896]{1,0:T(8,128)(2,1)S(1)}, bf16[528,896]{1,0:T(8,128)(2,1)S(1)}, u32[]{:S(2)}, u32[]{:S(2)}) collective-permute-start(bf16[528,896]{1,0:T(8,128)(2,1)S(1)} %collective-permute-done.2.refs_2_.refs_9_.refs_7_), channel_id=1, source_target_pairs={{2,3},{6,7},{10,11},{14,15},{18,19},{22,23},{26,27},{30,31}} | collective-permute-start | bytes 2838536 | tf_op jit(solution)/shard_map/ppermute | solution.py:399
  84.7 26.1 %collective-permute-start.5 = (bf16[528,896]{1,0:T(8,128)(2,1)S(1)}, bf16[528,896]{1,0:T(8,128)(2,1)S(1)}, u32[]{:S(2)}, u32[]{:S(2)}) collective-permute-start(bf16[528,896]{1,0:T(8,128)(2,1)S(1)} %collective-permute-done.3.refs_5_.refs_12_.refs_10_), channel_id=1, source_target_pairs={{1,0},{5,4},{9,8},{13,12},{17,16},{21,20},{25,24},{29,28}} | collective-permute-start | bytes 2838536 | tf_op jit(solution)/shard_map/ppermute | solution.py:399
  86.0 0.7 collective-permute-start.6
  86.7 24.1 %copy-start.9 = (bf16[256,896]{1,0:T(8,128)(2,1)}, bf16[256,896]{1,0:T(8,128)(2,1)S(1)}, u32[]{:S(2)}) copy-start(bf16[256,896]{1,0:T(8,128)(2,1)S(1)} %collective-permute-done.6.refs_1_) | copy-start | bytes 1376260
  86.7 24.1 %copy-start.6 = (bf16[528,896]{1,0:T(8,128)(2,1)}, bf16[528,896]{1,0:T(8,128)(2,1)S(1)}, u32[]{:S(2)}) copy-start(bf16[528,896]{1,0:T(8,128)(2,1)S(1)} %collective-permute-done.4.refs_3_.refs_10_.refs_8_) | copy-start | bytes 2838532
  110.8 17.8 %collective-permute-start.8 = (bf16[256,896]{1,0:T(8,128)(2,1)S(1)}, bf16[256,896]{1,0:T(8,128)(2,1)}, u32[]{:S(2)}, u32[]{:S(2)}) collective-permute-start(bf16[256,896]{1,0:T(8,128)(2,1)S(1)} %bitcast.11), channel_id=1, source_target_pairs={{0,1},{1,0},{2,3},{3,2},{4,5},{5,4},{6,7},{7,6},{8,9},{9,8},{10,11... | collective-permute-start | bytes 1376264 | tf_op jit(solution)/shard_map/ppermute | solution.py:399
  111.7 16.8 %collective-permute-start.7 = (bf16[256,896]{1,0:T(8,128)(2,1)S(1)}, bf16[256,896]{1,0:T(8,128)(2,1)}, u32[]{:S(2)}, u32[]{:S(2)}) collective-permute-start(bf16[256,896]{1,0:T(8,128)(2,1)S(1)} %bitcast.12), channel_id=1, source_target_pairs={{0,2},{1,3},{2,0},{3,1},{4,6},{5,7},{6,4},{7,5},{8,10},{9,11},{10,... | collective-permute-start | bytes 1376264 | tf_op jit(solution)/shard_map/ppermute | solution.py:399
  128.6 12.9 %collective-permute-start.9 = (bf16[256,896]{1,0:T(8,128)(2,1)}, bf16[256,896]{1,0:T(8,128)(2,1)S(1)}, u32[]{:S(2)}, u32[]{:S(2)}) collective-permute-start(bf16[256,896]{1,0:T(8,128)(2,1)} %collective-permute-done.7.refs_2_), channel_id=1, source_target_pairs={{1,0},{2,3},{5,4},{6,7},{9,8},{10,11},{13,12},{14,15},{17,16},{18,... | collective-permute-start | bytes 1376264 | tf_op jit(solution)/shard_map/ppermute | solution.py:399
  129.9 11.6 %collective-permute-start.11 = (bf16[8,32,896]{2,1,0:T(8,128)(2,1)}, bf16[8,32,896]{2,1,0:T(8,128)(2,1)S(1)}, u32[]{:S(2)}, u32[]{:S(2)}) collective-permute-start(bf16[8,32,896]{2,1,0:T(8,128)(2,1)} %get-tuple-element.85), channel_id=1, source_target_pairs={{1,2},{2,1},{5,6},{6,5},{9,10},{10,9},{13,14},{14,13},{17,18},{18,... | collective-permute-start | bytes 1376264 | tf_op jit(solution)/shard_map/ppermute | solution.py:399
  130.6 13.9 %collective-permute-start.10 = (bf16[8,32,896]{2,1,0:T(8,128)(2,1)}, bf16[8,32,896]{2,1,0:T(8,128)(2,1)S(1)}, u32[]{:S(2)}, u32[]{:S(2)}) collective-permute-start(bf16[8,32,896]{2,1,0:T(8,128)(2,1)} %get-tuple-element.85), channel_id=1, source_target_pairs={{0,1},{3,2},{4,5},{7,6},{8,9},{11,10},{12,13},{15,14},{16,17},{19,... | collective-permute-start | bytes 1376264 | tf_op jit(solution)/shard_map/ppermute | solution.py:399
  138.3 28.2 %collective-permute-start.13 = (bf16[8,32,896]{2,1,0:T(8,128)(2,1)}, bf16[8,32,896]{2,1,0:T(8,128)(2,1)S(1)}, u32[]{:S(2)}, u32[]{:S(2)}) collective-permute-start(bf16[8,32,896]{2,1,0:T(8,128)(2,1)} %get-tuple-element.87), channel_id=1, source_target_pairs={{0,1},{1,0},{2,3},{3,2},{4,5},{5,4},{6,7},{7,6},{8,9},{9,8},{10,11... | collective-permute-start | bytes 1376264 | tf_op jit(solution)/shard_map/ppermute | solution.py:399
  141.4 10.0 %copy-start.10 = (bf16[256,896]{1,0:T(8,128)(2,1)}, bf16[256,896]{1,0:T(8,128)(2,1)S(1)}, u32[]{:S(2)}) copy-start(bf16[256,896]{1,0:T(8,128)(2,1)S(1)} %collective-permute-done.9.refs_4_) | copy-start | bytes 1376260
  145.6 32.9 %copy-start.11 = (bf16[8,32,896]{2,1,0:T(8,128)(2,1)S(1)}, bf16[8,32,896]{2,1,0:T(8,128)(2,1)}, u32[]{:S(2)}) copy-start(bf16[8,32,896]{2,1,0:T(8,128)(2,1)} %get-tuple-element.79) | copy-start | bytes 1376260
  145.6 23.7 %collective-permute-start.12 = (bf16[8,32,896]{2,1,0:T(8,128)(2,1)S(1)}, bf16[8,32,896]{2,1,0:T(8,128)(2,1)S(1)}, u32[]{:S(2)}, u32[]{:S(2)}) collective-permute-start(bf16[8,32,896]{2,1,0:T(8,128)(2,1)S(1)} %add_convert_fusion.1), channel_id=1, source_target_pairs={{0,2},{1,3},{2,0},{3,1},{4,6},{5,7},{6,4},{7,5},{8,10},{9,11},{10,... | collective-permute-start | bytes 1376264 | tf_op jit(solution)/shard_map/ppermute | solution.py:399
  166.5 18.5 %copy-start.12 = (bf16[8,16,896]{2,1,0:T(8,128)(2,1)S(1)}, bf16[8,16,896]{2,1,0:T(8,128)(2,1)}, u32[]{:S(2)}) copy-start(bf16[8,16,896]{2,1,0:T(8,128)(2,1)} %get-tuple-element.101) | copy-start | bytes 688132
  169.3 5.1 %collective-permute-start.14 = (bf16[8,16,896]{2,1,0:T(8,128)(2,1)}, bf16[8,16,896]{2,1,0:T(8,128)(2,1)S(1)}, u32[]{:S(2)}, u32[]{:S(2)}) collective-permute-start(bf16[8,16,896]{2,1,0:T(8,128)(2,1)} %get-tuple-element.103), channel_id=1, source_target_pairs={{0,1},{3,2},{4,5},{7,6},{8,9},{11,10},{12,13},{15,14},{16,17},{19,... | collective-permute-start | bytes 688136 | tf_op jit(solution)/shard_map/ppermute | solution.py:399
  170.6 8.1 %collective-permute-start.17 = (bf16[8,16,896]{2,1,0:T(8,128)(2,1)}, bf16[8,16,896]{2,1,0:T(8,128)(2,1)S(1)}, u32[]{:S(2)}, u32[]{:S(2)}) collective-permute-start(bf16[8,16,896]{2,1,0:T(8,128)(2,1)} %get-tuple-element.103), channel_id=1, source_target_pairs={{1,2},{2,1},{5,6},{6,5},{9,10},{10,9},{13,14},{14,13},{17,18},{18,... | collective-permute-start | bytes 688136 | tf_op jit(solution)/shard_map/ppermute | solution.py:399
  171.3 7.4 %collective-permute-start.16 = (bf16[8,16,896]{2,1,0:T(8,128)(2,1)}, bf16[8,16,896]{2,1,0:T(8,128)(2,1)S(1)}, u32[]{:S(2)}, u32[]{:S(2)}) collective-permute-start(bf16[8,16,896]{2,1,0:T(8,128)(2,1)} %get-tuple-element.104), channel_id=1, source_target_pairs={{0,1},{1,0},{2,3},{3,2},{4,5},{5,4},{6,7},{7,6},{8,9},{9,8},{10,11... | collective-permute-start | bytes 688136 | tf_op jit(solution)/shard_map/ppermute | solution.py:399
  175.5 9.5 %collective-permute-start.15 = (bf16[8,16,896]{2,1,0:T(8,128)(2,1)S(1)}, bf16[8,16,896]{2,1,0:T(8,128)(2,1)S(1)}, u32[]{:S(2)}, u32[]{:S(2)}) collective-permute-start(bf16[8,16,896]{2,1,0:T(8,128)(2,1)S(1)} %add_convert_fusion.3), channel_id=1, source_target_pairs={{0,2},{1,3},{2,0},{3,1},{4,6},{5,7},{6,4},{7,5},{8,10},{9,11},{10,... | collective-permute-start | bytes 688136 | tf_op jit(solution)/shard_map/ppermute | solution.py:399
  186.0 18.8 %all-to-all-start.2 = ((bf16[8,48,896]{2,1,0:T(8,128)(2,1)}), bf16[8,48,896]{2,1,0:T(8,128)(2,1)S(1)}, u32[]{:S(2)}, u32[]{:S(2)}) async-start(bf16[8,48,896]{2,1,0:T(8,128)(2,1)} %pad_maximum_fusion.1), calls=%async_computation.2 | async-start | bytes 1376256 | tf_op jit(solution)/shard_map/all_to_all | solution.py:528
  193.4 11.5 %copy-start = (bf16[384,1024]{1,0:T(8,128)(2,1)S(1)}, bf16[384,1024]{1,0:T(8,128)(2,1)}, u32[]{:S(2)}) copy-start(bf16[384,1024]{1,0:T(8,128)(2,1)} %get-tuple-element.58.onehot) | copy-start | bytes 2359300
  (1 other events, 0.9 us)

commit v4 on v3

--- a/solution.py
+++ b/solution.py
@@ -192,9 +192,16 @@
     return out
 
 
+def split_refs(counts, refs):
+    n, apart = counts[0], counts[2]
+    if apart:
+        return (refs[:n], refs[n : 2 * n]), (1, 0), refs[2 * n :]
+    return (refs[:n], refs[:n]), (2, 1), refs[n:]
+
+
 def expert_kernel(counts, sources, coef_sources, start, coef_at, me, *refs):
     blocks = len(sources)
-    arrays, refs = refs[: counts[0]], refs[counts[0] :]
+    (x, dy), (stride, shift), refs = split_refs(counts, refs)
     coefs, refs = refs[: counts[1]], refs[counts[1] :]
     w_down, w_gate, w_up, rows_out, grad_gate, grad_up = refs[:6]
     parts, refs = refs[6 : 6 + blocks], refs[6 + blocks :]
@@ -203,14 +210,14 @@
     pieces, total, feat = x_buf.shape
     rows = total // blocks
 
-    def load(buffer, second, sem):
+    def load(arrays, buffer, shift, sem):
         return [
             block_copies(
                 arrays,
                 sources,
                 me[0],
                 lambda ref, k, f=f: pltpu.make_async_copy(
-                    ref.at[pl.ds((2 * f + second) * rows, rows), :],
+                    ref.at[pl.ds((stride * f + shift) * rows, rows), :],
                     buffer.at[f, pl.ds(k * rows, rows), :],
                     sem.at[f],
                 ),
@@ -226,8 +233,8 @@
             ref.at[pl.ds(coef_at, TILE), :], coef_buf.at[k], coef_sem.at[0]
         ),
     )
-    x_loads = load(x_buf, 0, sems.at[0])
-    dy_loads = load(dy_buf, 1, sems.at[1])
+    x_loads = load(x, x_buf, 0, sems.at[0])
+    dy_loads = load(dy, dy_buf, shift, sems.at[1])
     down_loads = weight_copies(w_down, down_buf, sems.at[2], pieces, False)
     gate_loads = weight_copies(w_gate, gate_buf, sems.at[3], pieces, True)
     up_loads = weight_copies(w_up, up_buf, sems.at[4], pieces, True)
@@ -293,12 +300,14 @@
     _, model, hidden = weights[1].shape
     pieces = model // feat
     blocks = len(sources)
+    apart = len(arrays) > len(coefs) + 1
+    count = len(arrays) // 2 if apart else len(arrays)
     total = rows * blocks
     grads = jax.ShapeDtypeStruct((total, hidden), BF)
     big = (pieces, total, feat)
     results = pl.pallas_call(
         functools.partial(
-            expert_kernel, (len(arrays), len(coefs)), sources, coef_sources, start, coef_at
+            expert_kernel, (count, len(coefs), apart), sources, coef_sources, start, coef_at
         ),
         in_specs=[SCALAR] + [IN_HBM] * (len(arrays) + len(coefs) + 3),
         out_specs=[IN_HBM] + in_vmem(2) + [IN_HBM] * blocks,
@@ -532,27 +541,31 @@
     early = exchange(early)
     coef = lax.dynamic_index_in_dim(coef, lax.axis_index("expert"), 0, keepdims=False)
     (early, coef), (late,) = together([early, coef], [late])
-    one = Steps(jnp.concatenate([early.reshape(-1, feat), coef], axis=0))
-    one.step()
+    x = Steps(early[:, :first].reshape(-1, feat))
+    dy = Steps(jnp.concatenate([early[:, first:].reshape(-1, feat), coef], axis=0))
+    x.step()
+    dy.step()
     late = exchange(late)
-    one.last, (late,) = together(one.last, [late])
+    x.last, (late,) = together(x.last, [late])
     for _ in range(groups - 3):
-        one.step()
-    one.last, (late,) = together(one.last, [late])
+        x.step()
+        dy.step()
+    x.step()
+    dy.last, (late,) = together(dy.last, [late])
     two = Gather(late.reshape(-1, feat))
-    one.step()
+    dy.step()
     two.middle()
-    one.last, two.got = together(one.last, two.got)
+    x.last, dy.last, two.got = together(x.last, dy.last, two.got)
     two.first()
-    coef_at = 2 * experts * first
-    coefs = one.got if fold == 1 else [v[coef_at:] for v in one.got]
+    coef_at = experts * first
+    coefs = dy.got if fold == 1 else [v[coef_at:] for v in dy.got]
     coef_sources = Steps.sources(groups)
 
-    def run(sources, arrays, start, count):
+    def run(sources, arrays, start, count, parts_in):
         if fold > 1:
-            size = 2 * experts * count
+            size = experts * count * parts_in
             arrays = [
-                widen(v[:size].reshape(experts, 2 * count, feat), fold) for v in arrays
+                widen(v[:size].reshape(experts, parts_in * count, feat), fold) for v in arrays
             ]
         at = coef_at if fold == 1 else 0
         x_rows, grads, parts = expert_pass(
@@ -560,14 +573,14 @@
         )
         return x_rows, grads, [narrow(v, fold) for v in parts]
 
-    xs1, grads1, parts1 = run(coef_sources, one.got, 0, first)
+    xs1, grads1, parts1 = run(coef_sources, x.got + dy.got, 0, first, 1)
     two.got, parts1 = together(two.got, parts1)
     two.second()
     back1 = Sum(parts1)
     back1.first()
-    two.got, back1.got = together(two.got, back1.got)
+    two.got, back1.got[:1] = together(two.got, back1.got[:1])
     back1.second()
-    xs2, grads2, parts2 = run(Gather.sources(groups), two.got, first, second)
+    xs2, grads2, parts2 = run(Gather.sources(groups), two.got, first, second, 2)
     back1.got, parts2 = together(back1.got, parts2)
     back2 = Sum(parts2)
     back2.first()

time: 208 us -> 203 us (0.976)
  starting transfers between devices: 44.3 us -> 59.8 us
  blocking collectives: 23.9 us -> 11.5 us
  waiting for transfers between devices: 82.6 us -> 74.4 us
    ppermute x18 -> x24, waiting for transfers between devices: 68 us -> 53 us  [send(): return lax.ppermute(value, 'dp', pairs)]
    all_to_all x1 -> x0, blocking collectives: 12.4 us -> none  [exchange(): lax.all_to_all(values, 'expert', split_axis=0, concat_axis=0, tiled=True)]
    ppermute x18 -> x24, starting transfers between devices: 33.4 us -> 45.7 us  [send(): return lax.ppermute(value, 'dp', pairs)]
    all_to_all x2 -> x3, waiting for transfers between devices: 14.6 us -> 21.4 us  [exchange(): lax.all_to_all(values, 'expert', split_axis=0, concat_axis=0, tiled=True)]
    all_to_all x2 -> x3, starting transfers between devices: 10.9 us -> 14.1 us  [exchange(): lax.all_to_all(values, 'expert', split_axis=0, concat_axis=0, tiled=True)]
  transfers between devices with their start and end apart: 20 -> 27, of which waited for: 11 -> 14; matrix products, arithmetic and copies ran while one was open for 2% -> 2% of each run, Pallas kernels for 20% -> 20%
where the time goes in v4:
time: 203 us; the launch traced here: 202 us
  waiting for transfers between devices  74.4 us (37%)
  starting transfers between devices  59.8 us (29%)
  Pallas kernels  49 us (24%)
  blocking collectives  11.5 us (6%)
  other arithmetic  4.8 us (2%)
    ppermute x24, waiting for transfers between devices, send(): return lax.ppermute(value, 'dp', pairs)  53 us
    ppermute x24, starting transfers between devices, send(): return lax.ppermute(value, 'dp', pairs)  45.7 us
    pallas_call x2, Pallas kernels, expert_pass(): pl.pallas_call(functools.partial(expert_kernel, (count, len(coefs), apart...  31 us
    all_to_all x3, waiting for transfers between devices, exchange(): lax.all_to_all(values, 'expert', split_axis=0, concat_axis=0, tiled=True)  21.4 us
    all_to_all x3, starting transfers between devices, exchange(): lax.all_to_all(values, 'expert', split_axis=0, concat_axis=0, tiled=True)  14.1 us
    all_gather x1, blocking collectives, per_device(): table = lax.all_gather(label(routes.T, gates.T, experts), 'expert', axis=0)  11.5 us
    pallas_call x1, Pallas kernels, weight_grads(): pl.pallas_call(functools.partial(weights_kernel, len(x)), grid=(pieces,),...  10.1 us
    pallas_call x1, Pallas kernels, compact(): pl.pallas_call(functools.partial(compact_kernel, experts, first, second),...  5.37 us
  transfers between devices with their start and end apart: 27, of which 14 were waited for; matrix products, arithmetic and copies ran while one was open for 2% of the time, Pallas kernels for 20%

profile of v4, /device:TPU:0, one launch (start us, length us, event | category | flops | bytes accessed | tf_op | source)
XLA Modules:
  0.0 201.7 jit_solution(14365115583535390585)
XLA Ops:
  2.0 11.5 %all-gather = bf16[128,128]{1,0:T(8,128)(2,1)} all-gather(bf16[16,128]{1,0:T(8,128)(2,1)S(1)} %add_convert_fusion.4), channel_id=2, replica_groups=mesh['expert'=8,'dp'=4] {'expert'}, dimensions={0}, use_global_device_ids=true | all-gather | bytes 36864 | tf_op jit(solution)/shard_map/all_gather | solution.py:539
  13.5 5.4 %compact.1 = (bf16[8,64,896]{2,1,0:T(8,128)(2,1)}, bf16[8,32,896]{2,1,0:T(8,128)(2,1)}, bf16[8,16,896]{2,1,0:T(8,128)(2,1)}, bf16[384,1024]{1,0:T(8,128)(2,1)}) custom-call(bf16[8,16,128]{2,1,0:T(8,128)(2,1)} %bitcast.18, bf16[1024,896]{1,0:T(8,128)(2,1)} %x_hbm.1, bf16[1024,896]{1,0:T(8,128)(2,1)} %dy_hbm.1), custom_call_target="tpu_custom_call" | custom-call | flops 1409286144 | bytes 5046272 | tf_op jit(solution)/shard_map/compact/pallas_call | solution.py:88
  18.9 3.6 %all-to-all-start = ((bf16[8,64,896]{2,1,0:T(8,128)(2,1)}), bf16[8,64,896]{2,1,0:T(8,128)(2,1)S(1)}, u32[]{:S(2)}, u32[]{:S(2)}) async-start(bf16[8,64,896]{2,1,0:T(8,128)(2,1)} %get-tuple-element.60), calls=%async_computation | async-start | bytes 1835008 | tf_op jit(solution)/shard_map/all_to_all | solution.py:537
  23.2 13.2 %all-to-all-done = bf16[8,64,896]{2,1,0:T(8,128)(2,1)S(1)} async-done(((bf16[8,64,896]{2,1,0:T(8,128)(2,1)}), bf16[8,64,896]{2,1,0:T(8,128)(2,1)S(1)}, u32[]{:S(2)}, u32[]{:S(2)}) %all-to-all-start) | async-done | bytes 917536 | tf_op jit(solution)/shard_map/all_to_all | solution.py:537
  36.6 1.3 collective-permute-start.8
  37.9 4.6 %collective-permute-start.6 = (bf16[272,896]{1,0:T(8,128)(2,1)S(1)}, bf16[272,896]{1,0:T(8,128)(2,1)S(1)}, u32[]{:S(2)}, u32[]{:S(2)}) collective-permute-start(bf16[272,896]{1,0:T(8,128)(2,1)S(1)} %pad_maximum_fusion.1.refs_7_.refs_14_.refs_5_), channel_id=1, source_target_pairs={{0,1},{1,2},{2,3},{4,5},{5,6},{6,7},{8,9},{9,10},{10,11},{12,13},{... | collective-permute-start | bytes 1462280 | tf_op jit(solution)/shard_map/ppermute | solution.py:408
  42.4 1.3 collective-permute-start.1
  43.7 5.3 %collective-permute-start = (bf16[256,896]{1,0:T(8,128)(2,1)S(1)}, bf16[256,896]{1,0:T(8,128)(2,1)}, u32[]{:S(2)}, u32[]{:S(2)}) collective-permute-start(bf16[256,896]{1,0:T(8,128)(2,1)S(1)} %bitcast.11), channel_id=1, source_target_pairs={{0,1},{1,2},{2,3},{4,5},{5,6},{6,7},{8,9},{9,10},{10,11},{12,13},{... | collective-permute-start | bytes 1376264 | tf_op jit(solution)/shard_map/ppermute | solution.py:408
  49.1 3.5 %all-to-all-start.1 = ((bf16[8,32,896]{2,1,0:T(8,128)(2,1)}), bf16[8,32,896]{2,1,0:T(8,128)(2,1)S(1)}, u32[]{:S(2)}, u32[]{:S(2)}) async-start(bf16[8,32,896]{2,1,0:T(8,128)(2,1)} %get-tuple-element.64), calls=%async_computation.1 | async-start | bytes 917504 | tf_op jit(solution)/shard_map/all_to_all | solution.py:537
  52.6 1.3 collective-permute-start.9
  54.7 6.9 %all-to-all-done.1 = bf16[8,32,896]{2,1,0:T(8,128)(2,1)S(1)} async-done(((bf16[8,32,896]{2,1,0:T(8,128)(2,1)}), bf16[8,32,896]{2,1,0:T(8,128)(2,1)S(1)}, u32[]{:S(2)}, u32[]{:S(2)}) %all-to-all-start.1) | async-done | bytes 458784 | tf_op jit(solution)/shard_map/all_to_all | solution.py:537
  62.3 1.3 collective-permute-start.4
  63.6 5.9 %collective-permute-done.9.refs_12_.refs_19_.refs_10_ = bf16[272,896]{1,0:T(8,128)(2,1)S(1)} collective-permute-done((bf16[272,896]{1,0:T(8,128)(2,1)S(1)}, bf16[272,896]{1,0:T(8,128)(2,1)S(1)}, u32[]{:S(2)}, u32[]{:S(2)}) %collective-permute-start.9) | collective-permute-done | bytes 487456 | tf_op jit(solution)/shard_map/ppermute | solution.py:408
  70.2 1.3 collective-permute-start.11
  72.2 8.7 %collective-permute-done.4.refs_5_ = bf16[256,896]{1,0:T(8,128)(2,1)S(1)} collective-permute-done((bf16[256,896]{1,0:T(8,128)(2,1)}, bf16[256,896]{1,0:T(8,128)(2,1)S(1)}, u32[]{:S(2)}, u32[]{:S(2)}) %collective-permute-start.4) | collective-permute-done | bytes 458784 | tf_op jit(solution)/shard_map/ppermute | solution.py:408
  82.9 15.9 %collective-permute-done.5.refs_6_ = bf16[256,896]{1,0:T(8,128)(2,1)S(1)} collective-permute-done((bf16[256,896]{1,0:T(8,128)(2,1)S(1)}, bf16[256,896]{1,0:T(8,128)(2,1)S(1)}, u32[]{:S(2)}, u32[]{:S(2)}) %collective-permute-start.5) | collective-permute-done | bytes 458784 | tf_op jit(solution)/shard_map/ppermute | solution.py:408
  99.8 5.6 %collective-permute-start.13 = (bf16[256,896]{1,0:T(8,128)(2,1)}, bf16[256,896]{1,0:T(8,128)(2,1)}, u32[]{:S(2)}, u32[]{:S(2)}) collective-permute-start(bf16[256,896]{1,0:T(8,128)(2,1)} %bitcast.16), channel_id=1, source_target_pairs={{0,2},{1,3},{2,0},{3,1},{4,6},{5,7},{6,4},{7,5},{8,10},{9,11},{10,... | collective-permute-start | bytes 1376264 | tf_op jit(solution)/shard_map/ppermute | solution.py:408
  105.4 16.0 %expert.2 = (bf16[8,128,896]{2,1,0:T(8,128)(2,1)}, bf16[128,512]{1,0:T(8,128)(2,1)}, bf16[128,512]{1,0:T(8,128)(2,1)}, bf16[8,32,896]{2,1,0:T(8,128)(2,1)}, bf16...) custom-call(s32[1]{0:T(128)} %bitcast.7.me, bf16[256,896]{1,0:T(8,128)(2,1)} %bitcast.12, ...), custom_call_target="tpu_custom_call" | custom-call | flops 4697620480 | bytes 22020096 | tf_op jit(solution)/shard_map/expert/pallas_call | solution.py:308
  121.4 1.9 collective-permute-done.13.refs_2_
  124.6 4.6 %collective-permute-start.16 = (bf16[8,32,896]{2,1,0:T(8,128)(2,1)}, bf16[8,32,896]{2,1,0:T(8,128)(2,1)S(1)}, u32[]{:S(2)}, u32[]{:S(2)}) collective-permute-start(bf16[8,32,896]{2,1,0:T(8,128)(2,1)} %get-tuple-element.88), channel_id=1, source_target_pairs={{0,1},{3,2},{4,5},{7,6},{8,9},{11,10},{12,13},{15,14},{16,17},{19,... | collective-permute-start | bytes 1376264 | tf_op jit(solution)/shard_map/ppermute | solution.py:408
  130.1 3.0 %collective-permute-start.18 = (bf16[8,32,896]{2,1,0:T(8,128)(2,1)}, bf16[8,32,896]{2,1,0:T(8,128)(2,1)S(1)}, u32[]{:S(2)}, u32[]{:S(2)}) collective-permute-start(bf16[8,32,896]{2,1,0:T(8,128)(2,1)} %get-tuple-element.90), channel_id=1, source_target_pairs={{0,1},{1,0},{2,3},{3,2},{4,5},{5,4},{6,7},{7,6},{8,9},{9,8},{10,11... | collective-permute-start | bytes 1376264 | tf_op jit(solution)/shard_map/ppermute | solution.py:408
  133.0 3.5 %collective-permute-done.15.refs_4_ = bf16[256,896]{1,0:T(8,128)(2,1)S(1)} collective-permute-done((bf16[256,896]{1,0:T(8,128)(2,1)}, bf16[256,896]{1,0:T(8,128)(2,1)S(1)}, u32[]{:S(2)}, u32[]{:S(2)}) %collective-permute-start.15) | collective-permute-done | bytes 458784 | tf_op jit(solution)/shard_map/ppermute | solution.py:408
  136.5 3.9 %collective-permute-done.16 = bf16[8,32,896]{2,1,0:T(8,128)(2,1)S(1)} collective-permute-done((bf16[8,32,896]{2,1,0:T(8,128)(2,1)}, bf16[8,32,896]{2,1,0:T(8,128)(2,1)S(1)}, u32[]{:S(2)}, u32[]{:S(2)}) %collective-permute-start.16) | collective-permute-done | bytes 458784 | tf_op jit(solution)/shard_map/ppermute | solution.py:408
  141.5 4.2 %collective-permute-start.17 = (bf16[8,32,896]{2,1,0:T(8,128)(2,1)S(1)}, bf16[8,32,896]{2,1,0:T(8,128)(2,1)S(1)}, u32[]{:S(2)}, u32[]{:S(2)}) collective-permute-start(bf16[8,32,896]{2,1,0:T(8,128)(2,1)S(1)} %add_convert_fusion.1), channel_id=1, source_target_pairs={{0,2},{1,3},{2,0},{3,1},{4,6},{5,7},{6,4},{7,5},{8,10},{9,11},{10,... | collective-permute-start | bytes 1376264 | tf_op jit(solution)/shard_map/ppermute | solution.py:408
  145.8 15.1 %expert.3 = (bf16[8,64,896]{2,1,0:T(8,128)(2,1)}, bf16[64,512]{1,0:T(8,128)(2,1)}, bf16[64,512]{1,0:T(8,128)(2,1)}, bf16[8,16,896]{2,1,0:T(8,128)(2,1)}, bf16[8,...) custom-call(s32[1]{0:T(128)} %bitcast.7.me, bf16[256,896]{1,0:T(8,128)(2,1)} %bitcast.17, ...), custom_call_target="tpu_custom_call" | custom-call | flops 2348810240 | bytes 22020096 | tf_op jit(solution)/shard_map/expert/pallas_call | solution.py:308
  161.6 2.5 %collective-permute-start.20 = (bf16[8,16,896]{2,1,0:T(8,128)(2,1)}, bf16[8,16,896]{2,1,0:T(8,128)(2,1)S(1)}, u32[]{:S(2)}, u32[]{:S(2)}) collective-permute-start(bf16[8,16,896]{2,1,0:T(8,128)(2,1)} %get-tuple-element.105), channel_id=1, source_target_pairs={{0,1},{3,2},{4,5},{7,6},{8,9},{11,10},{12,13},{15,14},{16,17},{19,... | collective-permute-start | bytes 688136 | tf_op jit(solution)/shard_map/ppermute | solution.py:408
  165.5 3.7 %collective-permute-done.20 = bf16[8,16,896]{2,1,0:T(8,128)(2,1)S(1)} collective-permute-done((bf16[8,16,896]{2,1,0:T(8,128)(2,1)}, bf16[8,16,896]{2,1,0:T(8,128)(2,1)S(1)}, u32[]{:S(2)}, u32[]{:S(2)}) %collective-permute-start.20) | collective-permute-done | bytes 229408 | tf_op jit(solution)/shard_map/ppermute | solution.py:408
  171.7 8.0 %collective-permute-done.21 = bf16[8,16,896]{2,1,0:T(8,128)(2,1)S(1)} collective-permute-done((bf16[8,16,896]{2,1,0:T(8,128)(2,1)S(1)}, bf16[8,16,896]{2,1,0:T(8,128)(2,1)S(1)}, u32[]{:S(2)}, u32[]{:S(2)}) %collective-permute-start.21) | collective-permute-done | bytes 229408 | tf_op jit(solution)/shard_map/ppermute | solution.py:408
  180.7 7.1 %all-to-all-start.2 = ((bf16[8,48,896]{2,1,0:T(8,128)(2,1)}), bf16[8,48,896]{2,1,0:T(8,128)(2,1)S(1)}, u32[]{:S(2)}, u32[]{:S(2)}) async-start(bf16[8,48,896]{2,1,0:T(8,128)(2,1)} %pad_maximum_fusion), calls=%async_computation.2 | async-start | bytes 1376256 | tf_op jit(solution)/shard_map/all_to_all | solution.py:537
  187.7 10.1 %weight_grads.1 = (bf16[1,7168,512]{2,1,0:T(8,128)(2,1)}, bf16[1,7168,512]{2,1,0:T(8,128)(2,1)}) custom-call(bf16[8,128,896]{2,1,0:T(8,128)(2,1)} %get-tuple-element.107.refs_0_, bf16[8,64,896]{2,1,0:T(8,128)(2,1)} %get-tuple-element.108.refs_1_, bf16[128,512]{1,0:T(8,128)(2,1)} %get-tuple-element.109.refs_2_, bf16[64,512]{1,0:T(8,128)(2,1)} %get-tuple-element.110.refs_3_, ...), custom_call_target="tpu_custom_call" | custom-call | flops 2818572288 | bytes 14680064 | tf_op jit(solution)/shard_map/weight_grads/pallas_call | solution.py:359
  197.9 1.4 all-to-all-done.2.rows
  199.2 2.5 %scatter.1 = bf16[1024,896]{1,0:T(8,128)(2,1)} custom-call(bf16[384,1024]{1,0:T(8,128)(2,1)S(1)} %copy-done, bf16[8,48,896]{2,1,0:T(8,128)(2,1)S(1)} %all-to-all-done.2.rows), custom_call_target="tpu_custom_call" | custom-call | flops 704643072 | bytes 4456448 | tf_op jit(solution)/shard_map/scatter/pallas_call | solution.py:381
  (74 shorter events, 16.9 us)
Async XLA Ops:
  18.9 17.5 %all-to-all-start = ((bf16[8,64,896]{2,1,0:T(8,128)(2,1)}), bf16[8,64,896]{2,1,0:T(8,128)(2,1)S(1)}, u32[]{:S(2)}, u32[]{:S(2)}) async-start(bf16[8,64,896]{2,1,0:T(8,128)(2,1)} %get-tuple-element.60), calls=%async_computation | async-start | bytes 1835008 | tf_op jit(solution)/shard_map/all_to_all | solution.py:537
  36.5 68.8 %copy-start.1 = (bf16[272,896]{1,0:T(8,128)(2,1)}, bf16[272,896]{1,0:T(8,128)(2,1)S(1)}, u32[]{:S(2)}) copy-start(bf16[272,896]{1,0:T(8,128)(2,1)S(1)} %pad_maximum_fusion.1.refs_7_.refs_14_.refs_5_) | copy-start | bytes 1462276
  36.6 16.0 %collective-permute-start.8 = (bf16[272,896]{1,0:T(8,128)(2,1)S(1)}, bf16[272,896]{1,0:T(8,128)(2,1)S(1)}, u32[]{:S(2)}, u32[]{:S(2)}) collective-permute-start(bf16[272,896]{1,0:T(8,128)(2,1)S(1)} %pad_maximum_fusion.1.refs_7_.refs_14_.refs_5_), channel_id=1, source_target_pairs={{1,0},{2,1},{3,2},{5,4},{6,5},{7,6},{9,8},{10,9},{11,10},{13,12},{... | collective-permute-start | bytes 1462280 | tf_op jit(solution)/shard_map/ppermute | solution.py:408
  37.9 16.1 %collective-permute-start.6 = (bf16[272,896]{1,0:T(8,128)(2,1)S(1)}, bf16[272,896]{1,0:T(8,128)(2,1)S(1)}, u32[]{:S(2)}, u32[]{:S(2)}) collective-permute-start(bf16[272,896]{1,0:T(8,128)(2,1)S(1)} %pad_maximum_fusion.1.refs_7_.refs_14_.refs_5_), channel_id=1, source_target_pairs={{0,1},{1,2},{2,3},{4,5},{5,6},{6,7},{8,9},{9,10},{10,11},{12,13},{... | collective-permute-start | bytes 1462280 | tf_op jit(solution)/shard_map/ppermute | solution.py:408
  42.4 19.1 %collective-permute-start.1 = (bf16[256,896]{1,0:T(8,128)(2,1)S(1)}, bf16[256,896]{1,0:T(8,128)(2,1)}, u32[]{:S(2)}, u32[]{:S(2)}) collective-permute-start(bf16[256,896]{1,0:T(8,128)(2,1)S(1)} %bitcast.10), channel_id=1, source_target_pairs={{1,0},{2,1},{3,2},{5,4},{6,5},{7,6},{9,8},{10,9},{11,10},{13,12},{... | collective-permute-start | bytes 1376264 | tf_op jit(solution)/shard_map/ppermute | solution.py:408
  43.7 17.8 %collective-permute-start = (bf16[256,896]{1,0:T(8,128)(2,1)S(1)}, bf16[256,896]{1,0:T(8,128)(2,1)}, u32[]{:S(2)}, u32[]{:S(2)}) collective-permute-start(bf16[256,896]{1,0:T(8,128)(2,1)S(1)} %bitcast.11), channel_id=1, source_target_pairs={{0,1},{1,2},{2,3},{4,5},{5,6},{6,7},{8,9},{9,10},{10,11},{12,13},{... | collective-permute-start | bytes 1376264 | tf_op jit(solution)/shard_map/ppermute | solution.py:408
  49.1 12.5 %all-to-all-start.1 = ((bf16[8,32,896]{2,1,0:T(8,128)(2,1)}), bf16[8,32,896]{2,1,0:T(8,128)(2,1)S(1)}, u32[]{:S(2)}, u32[]{:S(2)}) async-start(bf16[8,32,896]{2,1,0:T(8,128)(2,1)} %get-tuple-element.64), calls=%async_computation.1 | async-start | bytes 917504 | tf_op jit(solution)/shard_map/all_to_all | solution.py:537
  52.6 52.8 %copy-start.2 = (bf16[272,896]{1,0:T(8,128)(2,1)}, bf16[272,896]{1,0:T(8,128)(2,1)S(1)}, u32[]{:S(2)}) copy-start(bf16[272,896]{1,0:T(8,128)(2,1)S(1)} %collective-permute-done.8.refs_11_.refs_18_.refs_9_) | copy-start | bytes 1462276
  52.6 16.9 %collective-permute-start.9 = (bf16[272,896]{1,0:T(8,128)(2,1)S(1)}, bf16[272,896]{1,0:T(8,128)(2,1)S(1)}, u32[]{:S(2)}, u32[]{:S(2)}) collective-permute-start(bf16[272,896]{1,0:T(8,128)(2,1)S(1)} %collective-permute-done.8.refs_11_.refs_18_.refs_9_), channel_id=1, source_target_pairs={{1,0},{2,1},{5,4},{6,5},{9,8},{10,9},{13,12},{14,13},{17,16},{18,1... | collective-permute-start | bytes 1462280 | tf_op jit(solution)/shard_map/ppermute | solution.py:408
  54.0 51.4 %copy-start.3 = (bf16[272,896]{1,0:T(8,128)(2,1)}, bf16[272,896]{1,0:T(8,128)(2,1)S(1)}, u32[]{:S(2)}) copy-start(bf16[272,896]{1,0:T(8,128)(2,1)S(1)} %collective-permute-done.6.refs_8_.refs_15_.refs_6_) | copy-start | bytes 1462276
  54.0 15.5 %collective-permute-start.7 = (bf16[272,896]{1,0:T(8,128)(2,1)S(1)}, bf16[272,896]{1,0:T(8,128)(2,1)S(1)}, u32[]{:S(2)}, u32[]{:S(2)}) collective-permute-start(bf16[272,896]{1,0:T(8,128)(2,1)S(1)} %collective-permute-done.6.refs_8_.refs_15_.refs_6_), channel_id=1, source_target_pairs={{1,2},{2,3},{5,6},{6,7},{9,10},{10,11},{13,14},{14,15},{17,18},{18... | collective-permute-start | bytes 1462280 | tf_op jit(solution)/shard_map/ppermute | solution.py:408
  61.6 10.0 %collective-permute-start.2 = (bf16[256,896]{1,0:T(8,128)(2,1)}, bf16[256,896]{1,0:T(8,128)(2,1)S(1)}, u32[]{:S(2)}, u32[]{:S(2)}) collective-permute-start(bf16[256,896]{1,0:T(8,128)(2,1)} %collective-permute-done.refs_1_), channel_id=1, source_target_pairs={{1,2},{2,3},{5,6},{6,7},{9,10},{10,11},{13,14},{14,15},{17,18},{18... | collective-permute-start | bytes 1376264 | tf_op jit(solution)/shard_map/ppermute | solution.py:408
  62.3 18.6 %collective-permute-start.4 = (bf16[256,896]{1,0:T(8,128)(2,1)}, bf16[256,896]{1,0:T(8,128)(2,1)S(1)}, u32[]{:S(2)}, u32[]{:S(2)}) collective-permute-start(bf16[256,896]{1,0:T(8,128)(2,1)} %collective-permute-done.1.refs_4_), channel_id=1, source_target_pairs={{1,0},{2,1},{5,4},{6,5},{9,8},{10,9},{13,12},{14,13},{17,16},{18,1... | collective-permute-start | bytes 1376264 | tf_op jit(solution)/shard_map/ppermute | solution.py:408
  69.5 35.9 %copy-start.4 = (bf16[272,896]{1,0:T(8,128)(2,1)}, bf16[272,896]{1,0:T(8,128)(2,1)S(1)}, u32[]{:S(2)}) copy-start(bf16[272,896]{1,0:T(8,128)(2,1)S(1)} %collective-permute-done.9.refs_12_.refs_19_.refs_10_) | copy-start | bytes 1462276
  69.5 35.8 %copy-start.5 = (bf16[272,896]{1,0:T(8,128)(2,1)}, bf16[272,896]{1,0:T(8,128)(2,1)S(1)}, u32[]{:S(2)}) copy-start(bf16[272,896]{1,0:T(8,128)(2,1)S(1)} %collective-permute-done.7.refs_9_.refs_16_.refs_7_) | copy-start | bytes 1462276
  69.5 29.3 %collective-permute-start.10 = (bf16[272,896]{1,0:T(8,128)(2,1)S(1)}, bf16[272,896]{1,0:T(8,128)(2,1)S(1)}, u32[]{:S(2)}, u32[]{:S(2)}) collective-permute-start(bf16[272,896]{1,0:T(8,128)(2,1)S(1)} %collective-permute-done.7.refs_9_.refs_16_.refs_7_), channel_id=1, source_target_pairs={{2,3},{6,7},{10,11},{14,15},{18,19},{22,23},{26,27},{30,31}} | collective-permute-start | bytes 1462280 | tf_op jit(solution)/shard_map/ppermute | solution.py:408
  70.2 28.7 %collective-permute-start.11 = (bf16[272,896]{1,0:T(8,128)(2,1)S(1)}, bf16[272,896]{1,0:T(8,128)(2,1)S(1)}, u32[]{:S(2)}, u32[]{:S(2)}) collective-permute-start(bf16[272,896]{1,0:T(8,128)(2,1)S(1)} %collective-permute-done.9.refs_12_.refs_19_.refs_10_), channel_id=1, source_target_pairs={{1,0},{5,4},{9,8},{13,12},{17,16},{21,20},{25,24},{29,28}} | collective-permute-start | bytes 1462280 | tf_op jit(solution)/shard_map/ppermute | solution.py:408
  71.5 11.4 %collective-permute-start.3 = (bf16[256,896]{1,0:T(8,128)(2,1)S(1)}, bf16[256,896]{1,0:T(8,128)(2,1)S(1)}, u32[]{:S(2)}, u32[]{:S(2)}) collective-permute-start(bf16[256,896]{1,0:T(8,128)(2,1)S(1)} %collective-permute-done.2.refs_2_), channel_id=1, source_target_pairs={{2,3},{6,7},{10,11},{14,15},{18,19},{22,23},{26,27},{30,31}} | collective-permute-start | bytes 1376264 | tf_op jit(solution)/shard_map/ppermute | solution.py:408
  80.9 17.9 %collective-permute-start.5 = (bf16[256,896]{1,0:T(8,128)(2,1)S(1)}, bf16[256,896]{1,0:T(8,128)(2,1)S(1)}, u32[]{:S(2)}, u32[]{:S(2)}) collective-permute-start(bf16[256,896]{1,0:T(8,128)(2,1)S(1)} %collective-permute-done.4.refs_5_), channel_id=1, source_target_pairs={{1,0},{5,4},{9,8},{13,12},{17,16},{21,20},{25,24},{29,28}} | collective-permute-start | bytes 1376264 | tf_op jit(solution)/shard_map/ppermute | solution.py:408
  82.2 16.7 %collective-permute-start.12 = (bf16[256,896]{1,0:T(8,128)(2,1)}, bf16[256,896]{1,0:T(8,128)(2,1)S(1)}, u32[]{:S(2)}, u32[]{:S(2)}) collective-permute-start(bf16[256,896]{1,0:T(8,128)(2,1)} %bitcast.14), channel_id=1, source_target_pairs={{1,2},{2,1},{5,6},{6,5},{9,10},{10,9},{13,14},{14,13},{17,18},{18,... | collective-permute-start | bytes 1376264 | tf_op jit(solution)/shard_map/ppermute | solution.py:408
  98.9 22.5 %collective-permute-start.14 = (bf16[256,896]{1,0:T(8,128)(2,1)}, bf16[256,896]{1,0:T(8,128)(2,1)}, u32[]{:S(2)}, u32[]{:S(2)}) collective-permute-start(bf16[256,896]{1,0:T(8,128)(2,1)} %bitcast.15), channel_id=1, source_target_pairs={{0,1},{1,0},{2,3},{3,2},{4,5},{5,4},{6,7},{7,6},{8,9},{9,8},{10,11... | collective-permute-start | bytes 1376264 | tf_op jit(solution)/shard_map/ppermute | solution.py:408
  99.8 23.5 %collective-permute-start.13 = (bf16[256,896]{1,0:T(8,128)(2,1)}, bf16[256,896]{1,0:T(8,128)(2,1)}, u32[]{:S(2)}, u32[]{:S(2)}) collective-permute-start(bf16[256,896]{1,0:T(8,128)(2,1)} %bitcast.16), channel_id=1, source_target_pairs={{0,2},{1,3},{2,0},{3,1},{4,6},{5,7},{6,4},{7,5},{8,10},{9,11},{10,... | collective-permute-start | bytes 1376264 | tf_op jit(solution)/shard_map/ppermute | solution.py:408
  123.3 13.2 %collective-permute-start.15 = (bf16[256,896]{1,0:T(8,128)(2,1)}, bf16[256,896]{1,0:T(8,128)(2,1)S(1)}, u32[]{:S(2)}, u32[]{:S(2)}) collective-permute-start(bf16[256,896]{1,0:T(8,128)(2,1)} %collective-permute-done.13.refs_2_), channel_id=1, source_target_pairs={{1,0},{2,3},{5,4},{6,7},{9,8},{10,11},{13,12},{14,15},{17,16},{18,... | collective-permute-start | bytes 1376264 | tf_op jit(solution)/shard_map/ppermute | solution.py:408
  124.6 15.8 %collective-permute-start.16 = (bf16[8,32,896]{2,1,0:T(8,128)(2,1)}, bf16[8,32,896]{2,1,0:T(8,128)(2,1)S(1)}, u32[]{:S(2)}, u32[]{:S(2)}) collective-permute-start(bf16[8,32,896]{2,1,0:T(8,128)(2,1)} %get-tuple-element.88), channel_id=1, source_target_pairs={{0,1},{3,2},{4,5},{7,6},{8,9},{11,10},{12,13},{15,14},{16,17},{19,... | collective-permute-start | bytes 1376264 | tf_op jit(solution)/shard_map/ppermute | solution.py:408
  129.2 31.7 %collective-permute-start.19 = (bf16[8,32,896]{2,1,0:T(8,128)(2,1)}, bf16[8,32,896]{2,1,0:T(8,128)(2,1)S(1)}, u32[]{:S(2)}, u32[]{:S(2)}) collective-permute-start(bf16[8,32,896]{2,1,0:T(8,128)(2,1)} %get-tuple-element.88), channel_id=1, source_target_pairs={{1,2},{2,1},{5,6},{6,5},{9,10},{10,9},{13,14},{14,13},{17,18},{18,... | collective-permute-start | bytes 1376264 | tf_op jit(solution)/shard_map/ppermute | solution.py:408
  130.1 30.8 %collective-permute-start.18 = (bf16[8,32,896]{2,1,0:T(8,128)(2,1)}, bf16[8,32,896]{2,1,0:T(8,128)(2,1)S(1)}, u32[]{:S(2)}, u32[]{:S(2)}) collective-permute-start(bf16[8,32,896]{2,1,0:T(8,128)(2,1)} %get-tuple-element.90), channel_id=1, source_target_pairs={{0,1},{1,0},{2,3},{3,2},{4,5},{5,4},{6,7},{7,6},{8,9},{9,8},{10,11... | collective-permute-start | bytes 1376264 | tf_op jit(solution)/shard_map/ppermute | solution.py:408
  141.5 20.1 %collective-permute-start.17 = (bf16[8,32,896]{2,1,0:T(8,128)(2,1)S(1)}, bf16[8,32,896]{2,1,0:T(8,128)(2,1)S(1)}, u32[]{:S(2)}, u32[]{:S(2)}) collective-permute-start(bf16[8,32,896]{2,1,0:T(8,128)(2,1)S(1)} %add_convert_fusion.1), channel_id=1, source_target_pairs={{0,2},{1,3},{2,0},{3,1},{4,6},{5,7},{6,4},{7,5},{8,10},{9,11},{10,... | collective-permute-start | bytes 1376264 | tf_op jit(solution)/shard_map/ppermute | solution.py:408
  161.6 7.6 %collective-permute-start.20 = (bf16[8,16,896]{2,1,0:T(8,128)(2,1)}, bf16[8,16,896]{2,1,0:T(8,128)(2,1)S(1)}, u32[]{:S(2)}, u32[]{:S(2)}) collective-permute-start(bf16[8,16,896]{2,1,0:T(8,128)(2,1)} %get-tuple-element.105), channel_id=1, source_target_pairs={{0,1},{3,2},{4,5},{7,6},{8,9},{11,10},{12,13},{15,14},{16,17},{19,... | collective-permute-start | bytes 688136 | tf_op jit(solution)/shard_map/ppermute | solution.py:408
  164.1 7.5 %collective-permute-start.23 = (bf16[8,16,896]{2,1,0:T(8,128)(2,1)}, bf16[8,16,896]{2,1,0:T(8,128)(2,1)S(1)}, u32[]{:S(2)}, u32[]{:S(2)}) collective-permute-start(bf16[8,16,896]{2,1,0:T(8,128)(2,1)} %get-tuple-element.105), channel_id=1, source_target_pairs={{1,2},{2,1},{5,6},{6,5},{9,10},{10,9},{13,14},{14,13},{17,18},{18,... | collective-permute-start | bytes 688136 | tf_op jit(solution)/shard_map/ppermute | solution.py:408
  164.8 6.9 %collective-permute-start.22 = (bf16[8,16,896]{2,1,0:T(8,128)(2,1)}, bf16[8,16,896]{2,1,0:T(8,128)(2,1)S(1)}, u32[]{:S(2)}, u32[]{:S(2)}) collective-permute-start(bf16[8,16,896]{2,1,0:T(8,128)(2,1)} %get-tuple-element.106), channel_id=1, source_target_pairs={{0,1},{1,0},{2,3},{3,2},{4,5},{5,4},{6,7},{7,6},{8,9},{9,8},{10,11... | collective-permute-start | bytes 688136 | tf_op jit(solution)/shard_map/ppermute | solution.py:408
  170.2 9.4 %collective-permute-start.21 = (bf16[8,16,896]{2,1,0:T(8,128)(2,1)S(1)}, bf16[8,16,896]{2,1,0:T(8,128)(2,1)S(1)}, u32[]{:S(2)}, u32[]{:S(2)}) collective-permute-start(bf16[8,16,896]{2,1,0:T(8,128)(2,1)S(1)} %add_convert_fusion.3), channel_id=1, source_target_pairs={{0,2},{1,3},{2,0},{3,1},{4,6},{5,7},{6,4},{7,5},{8,10},{9,11},{10,... | collective-permute-start | bytes 688136 | tf_op jit(solution)/shard_map/ppermute | solution.py:408
  180.7 18.6 %all-to-all-start.2 = ((bf16[8,48,896]{2,1,0:T(8,128)(2,1)}), bf16[8,48,896]{2,1,0:T(8,128)(2,1)S(1)}, u32[]{:S(2)}, u32[]{:S(2)}) async-start(bf16[8,48,896]{2,1,0:T(8,128)(2,1)} %pad_maximum_fusion), calls=%async_computation.2 | async-start | bytes 1376256 | tf_op jit(solution)/shard_map/all_to_all | solution.py:537
  (13 other events, 187.1 us)

commit v5 on v4

--- a/solution.py
+++ b/solution.py
@@ -201,6 +201,7 @@
 
 def expert_kernel(counts, sources, coef_sources, start, coef_at, me, *refs):
     blocks = len(sources)
+    refs = refs[counts[3] :]
     (x, dy), (stride, shift), refs = split_refs(counts, refs)
     coefs, refs = refs[: counts[1]], refs[counts[1] :]
     w_down, w_gate, w_up, rows_out, grad_gate, grad_up = refs[:6]
@@ -295,7 +296,7 @@
         store.wait()
 
 
-def expert_pass(me, sources, arrays, coef_sources, coefs, coef_at, weights, start, rows):
+def expert_pass(me, sources, arrays, coef_sources, coefs, coef_at, weights, start, rows, after):
     feat = arrays[0].shape[1]
     _, model, hidden = weights[1].shape
     pieces = model // feat
@@ -307,9 +308,9 @@
     big = (pieces, total, feat)
     results = pl.pallas_call(
         functools.partial(
-            expert_kernel, (count, len(coefs), apart), sources, coef_sources, start, coef_at
+            expert_kernel, (count, len(coefs), apart, len(after)), sources, coef_sources, start, coef_at
         ),
-        in_specs=[SCALAR] + [IN_HBM] * (len(arrays) + len(coefs) + 3),
+        in_specs=[SCALAR] + [IN_HBM] * (len(after) + len(arrays) + len(coefs) + 3),
         out_specs=[IN_HBM] + in_vmem(2) + [IN_HBM] * blocks,
         out_shape=[
             jax.ShapeDtypeStruct(big, BF),
@@ -332,9 +333,9 @@
             pltpu.SemaphoreType.DMA((2, pieces)),
         ],
         compiler_params=params(),
-        cost_estimate=cost(10 * total * model * hidden, 6 * model * hidden),
+        cost_estimate=cost(100 * total * model * hidden, 60 * model * hidden),
         name="expert",
-    )(me, *arrays, *coefs, *weights)
+    )(me, *after, *arrays, *coefs, *weights)
     return results[0], results[1:3], results[3:]
 
 
@@ -485,19 +486,21 @@
     def __init__(self, parts):
         self.parts = parts
         self.got = []
-
-    def first(self):
+        self.sent = []
+
+    def first(self, last=None):
         n = len(self.parts)
         if n == FOUR:
-            self.got = [send(self.parts[3], INWARD), send(self.parts[3], MIDDLE)]
+            last = self.parts[3] if last is None else last
+            self.got = [send(last, INWARD), send(self.parts[3], MIDDLE)]
         else:
             self.got = [send(self.parts[k], shift(n, n - k)) for k in range(1, n)]
 
     def second(self):
         if len(self.parts) == FOUR:
             inward, middle = self.got
-            two_on = send(add(self.parts[1], inward), TWO_ON)
-            self.got = [two_on, send(self.parts[2], PAIRS), middle]
+            self.sent = [add(self.parts[1], inward)]
+            self.got = [send(self.sent[0], TWO_ON), send(self.parts[2], PAIRS), middle]
 
     def result(self):
         return add(self.parts[0], *self.got)
@@ -561,7 +564,7 @@
     coefs = dy.got if fold == 1 else [v[coef_at:] for v in dy.got]
     coef_sources = Steps.sources(groups)
 
-    def run(sources, arrays, start, count, parts_in):
+    def run(sources, arrays, start, count, parts_in, after=()):
         if fold > 1:
             size = experts * count * parts_in
             arrays = [
@@ -569,21 +572,24 @@
             ]
         at = coef_at if fold == 1 else 0
         x_rows, grads, parts = expert_pass(
-            me, sources, arrays, coef_sources, coefs, at, weights, start, count
+            me, sources, arrays, coef_sources, coefs, at, weights, start, count, after
         )
         return x_rows, grads, [narrow(v, fold) for v in parts]
 
     xs1, grads1, parts1 = run(coef_sources, x.got + dy.got, 0, first, 1)
+    last1 = parts1[3 % groups]
     two.got, parts1 = together(two.got, parts1)
     two.second()
     back1 = Sum(parts1)
-    back1.first()
-    two.got, back1.got[:1] = together(two.got, back1.got[:1])
+    back1.first(last1)
     back1.second()
-    xs2, grads2, parts2 = run(Gather.sources(groups), two.got, first, second, 2)
+    xs2, grads2, parts2 = run(
+        Gather.sources(groups), two.got, first, second, 2, back1.sent
+    )
+    last2 = parts2[3 % groups]
     back1.got, parts2 = together(back1.got, parts2)
     back2 = Sum(parts2)
-    back2.first()
+    back2.first(last2)
     g_gate, g_up = weight_grads([xs1, xs2], *[list(pair) for pair in zip(grads1, grads2)])
     back2.second()
     total = jnp.concatenate([back1.result(), back2.result()], axis=1)

time: 203 us -> 199 us (0.980)
  waiting for transfers between devices: 74.4 us -> 72.3 us
  starting transfers between devices: 59.8 us -> 57.7 us
    ppermute x24, starting transfers between devices: 45.7 us -> 43.6 us  [send(): return lax.ppermute(value, 'dp', pairs)]
  transfers between devices with their start and end apart: 27 -> 27, of which waited for: 14 -> 12; matrix products, arithmetic and copies ran while one was open for 2% -> 2% of each run, Pallas kernels for 20% -> 21%
where the time goes in v5:
time: 199 us; the launch traced here: 198 us
  waiting for transfers between devices  72.3 us (36%)
  starting transfers between devices  57.7 us (29%)
  Pallas kernels  49 us (25%)
  blocking collectives  11.5 us (6%)
  other arithmetic  4.81 us (2%)
    ppermute x24, waiting for transfers between devices, send(): return lax.ppermute(value, 'dp', pairs)  51.7 us
    ppermute x24, starting transfers between devices, send(): return lax.ppermute(value, 'dp', pairs)  43.6 us
    pallas_call x2, Pallas kernels, expert_pass(): pl.pallas_call(functools.partial(expert_kernel, (count, len(coefs), apart...  31.1 us
    all_to_all x3, waiting for transfers between devices, exchange(): lax.all_to_all(values, 'expert', split_axis=0, concat_axis=0, tiled=True)  20.7 us
    all_to_all x3, starting transfers between devices, exchange(): lax.all_to_all(values, 'expert', split_axis=0, concat_axis=0, tiled=True)  14.1 us
    all_gather x1, blocking collectives, per_device(): table = lax.all_gather(label(routes.T, gates.T, experts), 'expert', axis=0)  11.5 us
    pallas_call x1, Pallas kernels, weight_grads(): pl.pallas_call(functools.partial(weights_kernel, len(x)), grid=(pieces,),...  10.1 us
    pallas_call x1, Pallas kernels, compact(): pl.pallas_call(functools.partial(compact_kernel, experts, first, second),...  5.37 us
  transfers between devices with their start and end apart: 27, of which 12 were waited for; matrix products, arithmetic and copies ran while one was open for 2% of the time, Pallas kernels for 21%

profile of v5, /device:TPU:0, one launch (start us, length us, event | category | flops | bytes accessed | tf_op | source)
XLA Modules:
  0.0 198.1 jit_solution(15969627064730021292)
XLA Ops:
  2.0 11.5 %all-gather = bf16[128,128]{1,0:T(8,128)(2,1)} all-gather(bf16[16,128]{1,0:T(8,128)(2,1)S(1)} %add_convert_fusion.4), channel_id=2, replica_groups=mesh['expert'=8,'dp'=4] {'expert'}, dimensions={0}, use_global_device_ids=true | all-gather | bytes 36864 | tf_op jit(solution)/shard_map/all_gather | solution.py:542
  13.5 5.4 %compact.1 = (bf16[8,64,896]{2,1,0:T(8,128)(2,1)}, bf16[8,32,896]{2,1,0:T(8,128)(2,1)}, bf16[8,16,896]{2,1,0:T(8,128)(2,1)}, bf16[384,1024]{1,0:T(8,128)(2,1)}) custom-call(bf16[8,16,128]{2,1,0:T(8,128)(2,1)} %bitcast.18, bf16[1024,896]{1,0:T(8,128)(2,1)} %x_hbm.1, bf16[1024,896]{1,0:T(8,128)(2,1)} %dy_hbm.1), custom_call_target="tpu_custom_call" | custom-call | flops 1409286144 | bytes 5046272 | tf_op jit(solution)/shard_map/compact/pallas_call | solution.py:88
  18.9 3.6 %all-to-all-start = ((bf16[8,64,896]{2,1,0:T(8,128)(2,1)}), bf16[8,64,896]{2,1,0:T(8,128)(2,1)S(1)}, u32[]{:S(2)}, u32[]{:S(2)}) async-start(bf16[8,64,896]{2,1,0:T(8,128)(2,1)} %get-tuple-element.54), calls=%async_computation | async-start | bytes 1835008 | tf_op jit(solution)/shard_map/all_to_all | solution.py:540
  23.2 13.2 %all-to-all-done = bf16[8,64,896]{2,1,0:T(8,128)(2,1)S(1)} async-done(((bf16[8,64,896]{2,1,0:T(8,128)(2,1)}), bf16[8,64,896]{2,1,0:T(8,128)(2,1)S(1)}, u32[]{:S(2)}, u32[]{:S(2)}) %all-to-all-start) | async-done | bytes 917536 | tf_op jit(solution)/shard_map/all_to_all | solution.py:540
  37.9 4.6 %collective-permute-start.6 = (bf16[272,896]{1,0:T(8,128)(2,1)S(1)}, bf16[272,896]{1,0:T(8,128)(2,1)S(1)}, u32[]{:S(2)}, u32[]{:S(2)}) collective-permute-start(bf16[272,896]{1,0:T(8,128)(2,1)S(1)} %pad_maximum_fusion.1.refs_7_.refs_14_.refs_6_), channel_id=1, source_target_pairs={{0,1},{1,2},{2,3},{4,5},{5,6},{6,7},{8,9},{9,10},{10,11},{12,13},{... | collective-permute-start | bytes 1462280 | tf_op jit(solution)/shard_map/ppermute | solution.py:409
  43.7 5.3 %collective-permute-start = (bf16[256,896]{1,0:T(8,128)(2,1)S(1)}, bf16[256,896]{1,0:T(8,128)(2,1)}, u32[]{:S(2)}, u32[]{:S(2)}) collective-permute-start(bf16[256,896]{1,0:T(8,128)(2,1)S(1)} %bitcast.12), channel_id=1, source_target_pairs={{0,1},{1,2},{2,3},{4,5},{5,6},{6,7},{8,9},{9,10},{10,11},{12,13},{... | collective-permute-start | bytes 1376264 | tf_op jit(solution)/shard_map/ppermute | solution.py:409
  49.1 3.5 %all-to-all-start.1 = ((bf16[8,32,896]{2,1,0:T(8,128)(2,1)}), bf16[8,32,896]{2,1,0:T(8,128)(2,1)S(1)}, u32[]{:S(2)}, u32[]{:S(2)}) async-start(bf16[8,32,896]{2,1,0:T(8,128)(2,1)} %get-tuple-element.58), calls=%async_computation.1 | async-start | bytes 917504 | tf_op jit(solution)/shard_map/all_to_all | solution.py:540
  54.0 1.4 collective-permute-start.7
  55.4 6.1 %all-to-all-done.1 = bf16[8,32,896]{2,1,0:T(8,128)(2,1)S(1)} async-done(((bf16[8,32,896]{2,1,0:T(8,128)(2,1)}), bf16[8,32,896]{2,1,0:T(8,128)(2,1)S(1)}, u32[]{:S(2)}, u32[]{:S(2)}) %all-to-all-start.1) | async-done | bytes 458784 | tf_op jit(solution)/shard_map/all_to_all | solution.py:540
  61.5 1.5 collective-permute-start.2
  64.3 5.2 %collective-permute-done.9.refs_12_.refs_19_.refs_11_ = bf16[272,896]{1,0:T(8,128)(2,1)S(1)} collective-permute-done((bf16[272,896]{1,0:T(8,128)(2,1)S(1)}, bf16[272,896]{1,0:T(8,128)(2,1)S(1)}, u32[]{:S(2)}, u32[]{:S(2)}) %collective-permute-start.9) | collective-permute-done | bytes 487456 | tf_op jit(solution)/shard_map/ppermute | solution.py:409
  69.5 1.4 collective-permute-start.10
  72.3 1.5 collective-permute-start.3
  73.7 8.1 %collective-permute-done.4.refs_5_ = bf16[256,896]{1,0:T(8,128)(2,1)} collective-permute-done((bf16[256,896]{1,0:T(8,128)(2,1)}, bf16[256,896]{1,0:T(8,128)(2,1)}, u32[]{:S(2)}, u32[]{:S(2)}) %collective-permute-start.4) | collective-permute-done | bytes 458784 | tf_op jit(solution)/shard_map/ppermute | solution.py:409
  83.1 1.5 collective-permute-start.12
  84.6 14.6 %collective-permute-done.5.refs_6_ = bf16[256,896]{1,0:T(8,128)(2,1)} collective-permute-done((bf16[256,896]{1,0:T(8,128)(2,1)}, bf16[256,896]{1,0:T(8,128)(2,1)}, u32[]{:S(2)}, u32[]{:S(2)}) %collective-permute-start.5) | collective-permute-done | bytes 458784 | tf_op jit(solution)/shard_map/ppermute | solution.py:409
  99.2 1.8 collective-permute-start.14
  100.9 4.4 %collective-permute-start.13 = (bf16[256,896]{1,0:T(8,128)(2,1)S(1)}, bf16[256,896]{1,0:T(8,128)(2,1)}, u32[]{:S(2)}, u32[]{:S(2)}) collective-permute-start(bf16[256,896]{1,0:T(8,128)(2,1)S(1)} %bitcast.16), channel_id=1, source_target_pairs={{0,2},{1,3},{2,0},{3,1},{4,6},{5,7},{6,4},{7,5},{8,10},{9,11},{10,... | collective-permute-start | bytes 1376264 | tf_op jit(solution)/shard_map/ppermute | solution.py:409
  105.3 16.0 %expert.2 = (bf16[8,128,896]{2,1,0:T(8,128)(2,1)}, bf16[128,512]{1,0:T(8,128)(2,1)}, bf16[128,512]{1,0:T(8,128)(2,1)}, bf16[8,32,896]{2,1,0:T(8,128)(2,1)}, bf16...) custom-call(s32[1]{0:T(128)} %bitcast.7.me, bf16[256,896]{1,0:T(8,128)(2,1)} %bitcast.13, ...), custom_call_target="tpu_custom_call" | custom-call | flops 46976204800 | bytes 220200960 | tf_op jit(solution)/shard_map/expert/pallas_call | solution.py:309
  121.3 2.0 %collective-permute-start.15 = (bf16[8,32,896]{2,1,0:T(8,128)(2,1)}, bf16[8,32,896]{2,1,0:T(8,128)(2,1)S(1)}, u32[]{:S(2)}, u32[]{:S(2)}) collective-permute-start(bf16[8,32,896]{2,1,0:T(8,128)(2,1)} %get-tuple-element.79), channel_id=1, source_target_pairs={{0,1},{3,2},{4,5},{7,6},{8,9},{11,10},{12,13},{15,14},{16,17},{19,... | collective-permute-start | bytes 1376264 | tf_op jit(solution)/shard_map/ppermute | solution.py:409
  124.7 2.7 %collective-permute-start.17 = (bf16[8,32,896]{2,1,0:T(8,128)(2,1)}, bf16[8,32,896]{2,1,0:T(8,128)(2,1)S(1)}, u32[]{:S(2)}, u32[]{:S(2)}) collective-permute-start(bf16[8,32,896]{2,1,0:T(8,128)(2,1)} %get-tuple-element.78), channel_id=1, source_target_pairs={{0,1},{1,0},{2,3},{3,2},{4,5},{5,4},{6,7},{7,6},{8,9},{9,8},{10,11... | collective-permute-start | bytes 1376264 | tf_op jit(solution)/shard_map/ppermute | solution.py:409
  128.3 6.3 %collective-permute-done.15 = bf16[8,32,896]{2,1,0:T(8,128)(2,1)S(1)} collective-permute-done((bf16[8,32,896]{2,1,0:T(8,128)(2,1)}, bf16[8,32,896]{2,1,0:T(8,128)(2,1)S(1)}, u32[]{:S(2)}, u32[]{:S(2)}) %collective-permute-start.15) | collective-permute-done | bytes 458784 | tf_op jit(solution)/shard_map/ppermute | solution.py:409
  135.8 2.4 %collective-permute-start.16 = (bf16[8,32,896]{2,1,0:T(8,128)(2,1)S(1)}, bf16[8,32,896]{2,1,0:T(8,128)(2,1)S(1)}, u32[]{:S(2)}, u32[]{:S(2)}) collective-permute-start(bf16[8,32,896]{2,1,0:T(8,128)(2,1)S(1)} %add_convert_fusion.1.refs_0_), channel_id=1, source_target_pairs={{0,2},{1,3},{2,0},{3,1},{4,6},{5,7},{6,4},{7,5},{8,10},{9,11},{10,... | collective-permute-start | bytes 1376264 | tf_op jit(solution)/shard_map/ppermute | solution.py:409
  138.1 3.9 %collective-permute-done.19.refs_5_ = bf16[256,896]{1,0:T(8,128)(2,1)S(1)} collective-permute-done((bf16[256,896]{1,0:T(8,128)(2,1)}, bf16[256,896]{1,0:T(8,128)(2,1)S(1)}, u32[]{:S(2)}, u32[]{:S(2)}) %collective-permute-start.19) | collective-permute-done | bytes 458784 | tf_op jit(solution)/shard_map/ppermute | solution.py:409
  142.8 15.1 %expert.3 = (bf16[8,64,896]{2,1,0:T(8,128)(2,1)}, bf16[64,512]{1,0:T(8,128)(2,1)}, bf16[64,512]{1,0:T(8,128)(2,1)}, bf16[8,16,896]{2,1,0:T(8,128)(2,1)}, bf16[8,...) custom-call(s32[1]{0:T(128)} %bitcast.7.me, bf16[8,32,896]{2,1,0:T(8,128)(2,1)} %copy-done.5, ...), custom_call_target="tpu_custom_call" | custom-call | flops 23488102400 | bytes 220200960 | tf_op jit(solution)/shard_map/expert/pallas_call | solution.py:309
  157.9 1.4 collective-permute-start.20
  160.1 5.4 %collective-permute-done.20 = bf16[8,16,896]{2,1,0:T(8,128)(2,1)S(1)} collective-permute-done((bf16[8,16,896]{2,1,0:T(8,128)(2,1)}, bf16[8,16,896]{2,1,0:T(8,128)(2,1)S(1)}, u32[]{:S(2)}, u32[]{:S(2)}) %collective-permute-start.20) | collective-permute-done | bytes 229408 | tf_op jit(solution)/shard_map/ppermute | solution.py:409
  168.0 8.0 %collective-permute-done.21 = bf16[8,16,896]{2,1,0:T(8,128)(2,1)S(1)} collective-permute-done((bf16[8,16,896]{2,1,0:T(8,128)(2,1)S(1)}, bf16[8,16,896]{2,1,0:T(8,128)(2,1)S(1)}, u32[]{:S(2)}, u32[]{:S(2)}) %collective-permute-start.21) | collective-permute-done | bytes 229408 | tf_op jit(solution)/shard_map/ppermute | solution.py:409
  177.0 7.1 %all-to-all-start.2 = ((bf16[8,48,896]{2,1,0:T(8,128)(2,1)}), bf16[8,48,896]{2,1,0:T(8,128)(2,1)S(1)}, u32[]{:S(2)}, u32[]{:S(2)}) async-start(bf16[8,48,896]{2,1,0:T(8,128)(2,1)} %pad_maximum_fusion), calls=%async_computation.2 | async-start | bytes 1376256 | tf_op jit(solution)/shard_map/all_to_all | solution.py:540
  184.1 10.1 %weight_grads.1 = (bf16[1,7168,512]{2,1,0:T(8,128)(2,1)}, bf16[1,7168,512]{2,1,0:T(8,128)(2,1)}) custom-call(bf16[8,128,896]{2,1,0:T(8,128)(2,1)} %get-tuple-element.95.refs_0_, bf16[8,64,896]{2,1,0:T(8,128)(2,1)} %get-tuple-element.96.refs_1_, bf16[128,512]{1,0:T(8,128)(2,1)} %get-tuple-element.97.refs_2_, bf16[64,512]{1,0:T(8,128)(2,1)} %get-tuple-element.98.refs_3_, ...), custom_call_target="tpu_custom_call" | custom-call | flops 2818572288 | bytes 14680064 | tf_op jit(solution)/shard_map/weight_grads/pallas_call | solution.py:360
  194.2 1.4 all-to-all-done.2.rows
  195.6 2.5 %scatter.1 = bf16[1024,896]{1,0:T(8,128)(2,1)} custom-call(bf16[384,1024]{1,0:T(8,128)(2,1)S(1)} %copy-done, bf16[8,48,896]{2,1,0:T(8,128)(2,1)S(1)} %all-to-all-done.2.rows), custom_call_target="tpu_custom_call" | custom-call | flops 704643072 | bytes 4456448 | tf_op jit(solution)/shard_map/scatter/pallas_call | solution.py:382
  (62 shorter events, 18.4 us)
Async XLA Ops:
  18.9 17.5 %all-to-all-start = ((bf16[8,64,896]{2,1,0:T(8,128)(2,1)}), bf16[8,64,896]{2,1,0:T(8,128)(2,1)S(1)}, u32[]{:S(2)}, u32[]{:S(2)}) async-start(bf16[8,64,896]{2,1,0:T(8,128)(2,1)} %get-tuple-element.54), calls=%async_computation | async-start | bytes 1835008 | tf_op jit(solution)/shard_map/all_to_all | solution.py:540
  36.5 68.8 %copy-start.2 = (bf16[8,32,896]{2,1,0:T(8,128)(2,1)}, bf16[8,32,896]{2,1,0:T(8,128)(2,1)S(1)}, u32[]{:S(2)}) copy-start(bf16[8,32,896]{2,1,0:T(8,128)(2,1)S(1)} %get-tuple-element.104) | copy-start | bytes 1376260
  36.5 68.8 %copy-start.1 = (bf16[272,896]{1,0:T(8,128)(2,1)}, bf16[272,896]{1,0:T(8,128)(2,1)S(1)}, u32[]{:S(2)}) copy-start(bf16[272,896]{1,0:T(8,128)(2,1)S(1)} %pad_maximum_fusion.1.refs_7_.refs_14_.refs_6_) | copy-start | bytes 1462276
  36.6 16.0 %collective-permute-start.8 = (bf16[272,896]{1,0:T(8,128)(2,1)S(1)}, bf16[272,896]{1,0:T(8,128)(2,1)S(1)}, u32[]{:S(2)}, u32[]{:S(2)}) collective-permute-start(bf16[272,896]{1,0:T(8,128)(2,1)S(1)} %pad_maximum_fusion.1.refs_7_.refs_14_.refs_6_), channel_id=1, source_target_pairs={{1,0},{2,1},{3,2},{5,4},{6,5},{7,6},{9,8},{10,9},{11,10},{13,12},{... | collective-permute-start | bytes 1462280 | tf_op jit(solution)/shard_map/ppermute | solution.py:409
  37.9 16.1 %collective-permute-start.6 = (bf16[272,896]{1,0:T(8,128)(2,1)S(1)}, bf16[272,896]{1,0:T(8,128)(2,1)S(1)}, u32[]{:S(2)}, u32[]{:S(2)}) collective-permute-start(bf16[272,896]{1,0:T(8,128)(2,1)S(1)} %pad_maximum_fusion.1.refs_7_.refs_14_.refs_6_), channel_id=1, source_target_pairs={{0,1},{1,2},{2,3},{4,5},{5,6},{6,7},{8,9},{9,10},{10,11},{12,13},{... | collective-permute-start | bytes 1462280 | tf_op jit(solution)/shard_map/ppermute | solution.py:409
  42.4 19.1 %collective-permute-start.1 = (bf16[256,896]{1,0:T(8,128)(2,1)S(1)}, bf16[256,896]{1,0:T(8,128)(2,1)}, u32[]{:S(2)}, u32[]{:S(2)}) collective-permute-start(bf16[256,896]{1,0:T(8,128)(2,1)S(1)} %bitcast.11), channel_id=1, source_target_pairs={{1,0},{2,1},{3,2},{5,4},{6,5},{7,6},{9,8},{10,9},{11,10},{13,12},{... | collective-permute-start | bytes 1376264 | tf_op jit(solution)/shard_map/ppermute | solution.py:409
  43.7 17.8 %collective-permute-start = (bf16[256,896]{1,0:T(8,128)(2,1)S(1)}, bf16[256,896]{1,0:T(8,128)(2,1)}, u32[]{:S(2)}, u32[]{:S(2)}) collective-permute-start(bf16[256,896]{1,0:T(8,128)(2,1)S(1)} %bitcast.12), channel_id=1, source_target_pairs={{0,1},{1,2},{2,3},{4,5},{5,6},{6,7},{8,9},{9,10},{10,11},{12,13},{... | collective-permute-start | bytes 1376264 | tf_op jit(solution)/shard_map/ppermute | solution.py:409
  49.1 12.5 %all-to-all-start.1 = ((bf16[8,32,896]{2,1,0:T(8,128)(2,1)}), bf16[8,32,896]{2,1,0:T(8,128)(2,1)S(1)}, u32[]{:S(2)}, u32[]{:S(2)}) async-start(bf16[8,32,896]{2,1,0:T(8,128)(2,1)} %get-tuple-element.58), calls=%async_computation.1 | async-start | bytes 917504 | tf_op jit(solution)/shard_map/all_to_all | solution.py:540
  52.6 52.8 %copy-start.7 = (bf16[272,896]{1,0:T(8,128)(2,1)}, bf16[272,896]{1,0:T(8,128)(2,1)S(1)}, u32[]{:S(2)}) copy-start(bf16[272,896]{1,0:T(8,128)(2,1)S(1)} %collective-permute-done.8.refs_11_.refs_18_.refs_10_) | copy-start | bytes 1462276
  52.6 16.9 %collective-permute-start.9 = (bf16[272,896]{1,0:T(8,128)(2,1)S(1)}, bf16[272,896]{1,0:T(8,128)(2,1)S(1)}, u32[]{:S(2)}, u32[]{:S(2)}) collective-permute-start(bf16[272,896]{1,0:T(8,128)(2,1)S(1)} %collective-permute-done.8.refs_11_.refs_18_.refs_10_), channel_id=1, source_target_pairs={{1,0},{2,1},{5,4},{6,5},{9,8},{10,9},{13,12},{14,13},{17,16},{18,1... | collective-permute-start | bytes 1462280 | tf_op jit(solution)/shard_map/ppermute | solution.py:409
  54.0 51.3 %copy-start.8 = (bf16[272,896]{1,0:T(8,128)(2,1)}, bf16[272,896]{1,0:T(8,128)(2,1)S(1)}, u32[]{:S(2)}) copy-start(bf16[272,896]{1,0:T(8,128)(2,1)S(1)} %collective-permute-done.6.refs_8_.refs_15_.refs_7_) | copy-start | bytes 1462276
  54.0 15.5 %collective-permute-start.7 = (bf16[272,896]{1,0:T(8,128)(2,1)S(1)}, bf16[272,896]{1,0:T(8,128)(2,1)}, u32[]{:S(2)}, u32[]{:S(2)}) collective-permute-start(bf16[272,896]{1,0:T(8,128)(2,1)S(1)} %collective-permute-done.6.refs_8_.refs_15_.refs_7_), channel_id=1, source_target_pairs={{1,2},{2,3},{5,6},{6,7},{9,10},{10,11},{13,14},{14,15},{17,18},{18... | collective-permute-start | bytes 1462280 | tf_op jit(solution)/shard_map/ppermute | solution.py:409
  61.5 59.8 %copy-start.3 = (bf16[8,32,896]{2,1,0:T(8,128)(2,1)}, bf16[8,32,896]{2,1,0:T(8,128)(2,1)S(1)}, u32[]{:S(2)}) copy-start(bf16[8,32,896]{2,1,0:T(8,128)(2,1)S(1)} %all-to-all-done.1) | copy-start | bytes 1376260
  61.5 10.7 %collective-permute-start.2 = (bf16[256,896]{1,0:T(8,128)(2,1)}, bf16[256,896]{1,0:T(8,128)(2,1)}, u32[]{:S(2)}, u32[]{:S(2)}) collective-permute-start(bf16[256,896]{1,0:T(8,128)(2,1)} %collective-permute-done.refs_1_), channel_id=1, source_target_pairs={{1,2},{2,3},{5,6},{6,7},{9,10},{10,11},{13,14},{14,15},{17,18},{18... | collective-permute-start | bytes 1376264 | tf_op jit(solution)/shard_map/ppermute | solution.py:409
  63.0 18.8 %collective-permute-start.4 = (bf16[256,896]{1,0:T(8,128)(2,1)}, bf16[256,896]{1,0:T(8,128)(2,1)}, u32[]{:S(2)}, u32[]{:S(2)}) collective-permute-start(bf16[256,896]{1,0:T(8,128)(2,1)} %collective-permute-done.1.refs_4_), channel_id=1, source_target_pairs={{1,0},{2,1},{5,4},{6,5},{9,8},{10,9},{13,12},{14,13},{17,16},{18,1... | collective-permute-start | bytes 1376264 | tf_op jit(solution)/shard_map/ppermute | solution.py:409
  69.5 29.6 %collective-permute-start.10 = (bf16[272,896]{1,0:T(8,128)(2,1)}, bf16[272,896]{1,0:T(8,128)(2,1)}, u32[]{:S(2)}, u32[]{:S(2)}) collective-permute-start(bf16[272,896]{1,0:T(8,128)(2,1)} %collective-permute-done.7.refs_9_.refs_16_.refs_8_), channel_id=1, source_target_pairs={{2,3},{6,7},{10,11},{14,15},{18,19},{22,23},{26,27},{30,31}} | collective-permute-start | bytes 1462280 | tf_op jit(solution)/shard_map/ppermute | solution.py:409
  71.0 28.2 %collective-permute-start.11 = (bf16[272,896]{1,0:T(8,128)(2,1)S(1)}, bf16[272,896]{1,0:T(8,128)(2,1)}, u32[]{:S(2)}, u32[]{:S(2)}) collective-permute-start(bf16[272,896]{1,0:T(8,128)(2,1)S(1)} %collective-permute-done.9.refs_12_.refs_19_.refs_11_), channel_id=1, source_target_pairs={{1,0},{5,4},{9,8},{13,12},{17,16},{21,20},{25,24},{29,28}} | collective-permute-start | bytes 1462280 | tf_op jit(solution)/shard_map/ppermute | solution.py:409
  72.3 12.3 %collective-permute-start.3 = (bf16[256,896]{1,0:T(8,128)(2,1)}, bf16[256,896]{1,0:T(8,128)(2,1)}, u32[]{:S(2)}, u32[]{:S(2)}) collective-permute-start(bf16[256,896]{1,0:T(8,128)(2,1)} %collective-permute-done.2.refs_2_), channel_id=1, source_target_pairs={{2,3},{6,7},{10,11},{14,15},{18,19},{22,23},{26,27},{30,31}} | collective-permute-start | bytes 1376264 | tf_op jit(solution)/shard_map/ppermute | solution.py:409
  81.8 17.3 %collective-permute-start.5 = (bf16[256,896]{1,0:T(8,128)(2,1)}, bf16[256,896]{1,0:T(8,128)(2,1)}, u32[]{:S(2)}, u32[]{:S(2)}) collective-permute-start(bf16[256,896]{1,0:T(8,128)(2,1)} %collective-permute-done.4.refs_5_), channel_id=1, source_target_pairs={{1,0},{5,4},{9,8},{13,12},{17,16},{21,20},{25,24},{29,28}} | collective-permute-start | bytes 1376264 | tf_op jit(solution)/shard_map/ppermute | solution.py:409
  83.1 16.0 %collective-permute-start.12 = (bf16[256,896]{1,0:T(8,128)(2,1)S(1)}, bf16[256,896]{1,0:T(8,128)(2,1)}, u32[]{:S(2)}, u32[]{:S(2)}) collective-permute-start(bf16[256,896]{1,0:T(8,128)(2,1)S(1)} %bitcast.14), channel_id=1, source_target_pairs={{1,2},{2,1},{5,6},{6,5},{9,10},{10,9},{13,14},{14,13},{17,18},{18,... | collective-permute-start | bytes 1376264 | tf_op jit(solution)/shard_map/ppermute | solution.py:409
  99.2 24.2 %collective-permute-start.14 = (bf16[256,896]{1,0:T(8,128)(2,1)S(1)}, bf16[256,896]{1,0:T(8,128)(2,1)S(1)}, u32[]{:S(2)}, u32[]{:S(2)}) collective-permute-start(bf16[256,896]{1,0:T(8,128)(2,1)S(1)} %bitcast.15), channel_id=1, source_target_pairs={{0,1},{1,0},{2,3},{3,2},{4,5},{5,4},{6,7},{7,6},{8,9},{9,8},{10,11... | collective-permute-start | bytes 1376264 | tf_op jit(solution)/shard_map/ppermute | solution.py:409
  100.9 22.5 %collective-permute-start.13 = (bf16[256,896]{1,0:T(8,128)(2,1)S(1)}, bf16[256,896]{1,0:T(8,128)(2,1)}, u32[]{:S(2)}, u32[]{:S(2)}) collective-permute-start(bf16[256,896]{1,0:T(8,128)(2,1)S(1)} %bitcast.16), channel_id=1, source_target_pairs={{0,2},{1,3},{2,0},{3,1},{4,6},{5,7},{6,4},{7,5},{8,10},{9,11},{10,... | collective-permute-start | bytes 1376264 | tf_op jit(solution)/shard_map/ppermute | solution.py:409
  121.3 13.3 %collective-permute-start.15 = (bf16[8,32,896]{2,1,0:T(8,128)(2,1)}, bf16[8,32,896]{2,1,0:T(8,128)(2,1)S(1)}, u32[]{:S(2)}, u32[]{:S(2)}) collective-permute-start(bf16[8,32,896]{2,1,0:T(8,128)(2,1)} %get-tuple-element.79), channel_id=1, source_target_pairs={{0,1},{3,2},{4,5},{7,6},{8,9},{11,10},{12,13},{15,14},{16,17},{19,... | collective-permute-start | bytes 1376264 | tf_op jit(solution)/shard_map/ppermute | solution.py:409
  123.4 18.6 %collective-permute-start.19 = (bf16[256,896]{1,0:T(8,128)(2,1)}, bf16[256,896]{1,0:T(8,128)(2,1)S(1)}, u32[]{:S(2)}, u32[]{:S(2)}) collective-permute-start(bf16[256,896]{1,0:T(8,128)(2,1)} %collective-permute-done.13.refs_3_), channel_id=1, source_target_pairs={{1,0},{2,3},{5,4},{6,7},{9,8},{10,11},{13,12},{14,15},{17,16},{18,... | collective-permute-start | bytes 1376264 | tf_op jit(solution)/shard_map/ppermute | solution.py:409
  124.7 34.6 %collective-permute-start.17 = (bf16[8,32,896]{2,1,0:T(8,128)(2,1)}, bf16[8,32,896]{2,1,0:T(8,128)(2,1)S(1)}, u32[]{:S(2)}, u32[]{:S(2)}) collective-permute-start(bf16[8,32,896]{2,1,0:T(8,128)(2,1)} %get-tuple-element.78), channel_id=1, source_target_pairs={{0,1},{1,0},{2,3},{3,2},{4,5},{5,4},{6,7},{7,6},{8,9},{9,8},{10,11... | collective-permute-start | bytes 1376264 | tf_op jit(solution)/shard_map/ppermute | solution.py:409
  127.4 31.9 %collective-permute-start.18 = (bf16[8,32,896]{2,1,0:T(8,128)(2,1)}, bf16[8,32,896]{2,1,0:T(8,128)(2,1)S(1)}, u32[]{:S(2)}, u32[]{:S(2)}) collective-permute-start(bf16[8,32,896]{2,1,0:T(8,128)(2,1)} %get-tuple-element.79), channel_id=1, source_target_pairs={{1,2},{2,1},{5,6},{6,5},{9,10},{10,9},{13,14},{14,13},{17,18},{18,... | collective-permute-start | bytes 1376264 | tf_op jit(solution)/shard_map/ppermute | solution.py:409
  135.8 23.6 %collective-permute-start.16 = (bf16[8,32,896]{2,1,0:T(8,128)(2,1)S(1)}, bf16[8,32,896]{2,1,0:T(8,128)(2,1)S(1)}, u32[]{:S(2)}, u32[]{:S(2)}) collective-permute-start(bf16[8,32,896]{2,1,0:T(8,128)(2,1)S(1)} %add_convert_fusion.1.refs_0_), channel_id=1, source_target_pairs={{0,2},{1,3},{2,0},{3,1},{4,6},{5,7},{6,4},{7,5},{8,10},{9,11},{10,... | collective-permute-start | bytes 1376264 | tf_op jit(solution)/shard_map/ppermute | solution.py:409
  157.9 7.6 %collective-permute-start.20 = (bf16[8,16,896]{2,1,0:T(8,128)(2,1)}, bf16[8,16,896]{2,1,0:T(8,128)(2,1)S(1)}, u32[]{:S(2)}, u32[]{:S(2)}) collective-permute-start(bf16[8,16,896]{2,1,0:T(8,128)(2,1)} %get-tuple-element.94), channel_id=1, source_target_pairs={{0,1},{3,2},{4,5},{7,6},{8,9},{11,10},{12,13},{15,14},{16,17},{19,... | collective-permute-start | bytes 688136 | tf_op jit(solution)/shard_map/ppermute | solution.py:409
  159.4 8.6 %collective-permute-start.22 = (bf16[8,16,896]{2,1,0:T(8,128)(2,1)}, bf16[8,16,896]{2,1,0:T(8,128)(2,1)S(1)}, u32[]{:S(2)}, u32[]{:S(2)}) collective-permute-start(bf16[8,16,896]{2,1,0:T(8,128)(2,1)} %get-tuple-element.93), channel_id=1, source_target_pairs={{0,1},{1,0},{2,3},{3,2},{4,5},{5,4},{6,7},{7,6},{8,9},{9,8},{10,11... | collective-permute-start | bytes 688136 | tf_op jit(solution)/shard_map/ppermute | solution.py:409
  159.4 8.5 %collective-permute-start.23 = (bf16[8,16,896]{2,1,0:T(8,128)(2,1)}, bf16[8,16,896]{2,1,0:T(8,128)(2,1)S(1)}, u32[]{:S(2)}, u32[]{:S(2)}) collective-permute-start(bf16[8,16,896]{2,1,0:T(8,128)(2,1)} %get-tuple-element.94), channel_id=1, source_target_pairs={{1,2},{2,1},{5,6},{6,5},{9,10},{10,9},{13,14},{14,13},{17,18},{18,... | collective-permute-start | bytes 688136 | tf_op jit(solution)/shard_map/ppermute | solution.py:409
  166.5 9.4 %collective-permute-start.21 = (bf16[8,16,896]{2,1,0:T(8,128)(2,1)S(1)}, bf16[8,16,896]{2,1,0:T(8,128)(2,1)S(1)}, u32[]{:S(2)}, u32[]{:S(2)}) collective-permute-start(bf16[8,16,896]{2,1,0:T(8,128)(2,1)S(1)} %add_convert_fusion.3), channel_id=1, source_target_pairs={{0,2},{1,3},{2,0},{3,1},{4,6},{5,7},{6,4},{7,5},{8,10},{9,11},{10,... | collective-permute-start | bytes 688136 | tf_op jit(solution)/shard_map/ppermute | solution.py:409
  177.0 18.6 %all-to-all-start.2 = ((bf16[8,48,896]{2,1,0:T(8,128)(2,1)}), bf16[8,48,896]{2,1,0:T(8,128)(2,1)S(1)}, u32[]{:S(2)}, u32[]{:S(2)}) async-start(bf16[8,48,896]{2,1,0:T(8,128)(2,1)} %pad_maximum_fusion), calls=%async_computation.2 | async-start | bytes 1376256 | tf_op jit(solution)/shard_map/all_to_all | solution.py:540
  (7 other events, 109.2 us)

commit v6 on v5

--- a/solution.py
+++ b/solution.py
@@ -582,6 +582,8 @@
     two.second()
     back1 = Sum(parts1)
     back1.first(last1)
+    back1.parts = list(back1.parts)
+    two.got, back1.parts[2:3] = together(two.got, back1.parts[2:3])
     back1.second()
     xs2, grads2, parts2 = run(
         Gather.sources(groups), two.got, first, second, 2, back1.sent

time: 199 us -> 195 us (0.980)
  waiting for transfers between devices: 72.3 us -> 67.3 us
    ppermute x24, waiting for transfers between devices: 51.7 us -> 46.6 us  [send(): return lax.ppermute(value, 'dp', pairs)]
  transfers between devices with their start and end apart: 27 -> 27, of which waited for: 12 -> 13; matrix products, arithmetic and copies ran while one was open for 2% -> 1% of each run, Pallas kernels for 21% -> 21%
where the time goes in v6:
time: 195 us; the launch traced here: 194 us
  waiting for transfers between devices  67.3 us (35%)
  starting transfers between devices  58 us (30%)
  Pallas kernels  49 us (25%)
  blocking collectives  11.5 us (6%)
  other arithmetic  4.8 us (2%)
  local copies, waits for them, and re-layouts  2.41 us (1%)
    ppermute x24, waiting for transfers between devices, send(): return lax.ppermute(value, 'dp', pairs)  46.6 us
    ppermute x24, starting transfers between devices, send(): return lax.ppermute(value, 'dp', pairs)  43.9 us
    pallas_call x2, Pallas kernels, expert_pass(): pl.pallas_call(functools.partial(expert_kernel, (count, len(coefs), apart...  31.1 us
    all_to_all x3, waiting for transfers between devices, exchange(): lax.all_to_all(values, 'expert', split_axis=0, concat_axis=0, tiled=True)  20.7 us
    all_to_all x3, starting transfers between devices, exchange(): lax.all_to_all(values, 'expert', split_axis=0, concat_axis=0, tiled=True)  14.1 us
    all_gather x1, blocking collectives, per_device(): table = lax.all_gather(label(routes.T, gates.T, experts), 'expert', axis=0)  11.5 us
    pallas_call x1, Pallas kernels, weight_grads(): pl.pallas_call(functools.partial(weights_kernel, len(x)), grid=(pieces,),...  10.1 us
    pallas_call x1, Pallas kernels, compact(): pl.pallas_call(functools.partial(compact_kernel, experts, first, second),...  5.37 us
  transfers between devices with their start and end apart: 27, of which 13 were waited for; matrix products, arithmetic and copies ran while one was open for 1% of the time, Pallas kernels for 21%

profile of v6, /device:TPU:0, one launch (start us, length us, event | category | flops | bytes accessed | tf_op | source)
XLA Modules:
  0.0 194.0 jit_solution(12584341830223248032)
XLA Ops:
  2.0 11.5 %all-gather = bf16[128,128]{1,0:T(8,128)(2,1)} all-gather(bf16[16,128]{1,0:T(8,128)(2,1)S(1)} %add_convert_fusion.4), channel_id=2, replica_groups=mesh['expert'=8,'dp'=4] {'expert'}, dimensions={0}, use_global_device_ids=true | all-gather | bytes 36864 | tf_op jit(solution)/shard_map/all_gather | solution.py:542
  13.5 5.4 %compact.1 = (bf16[8,64,896]{2,1,0:T(8,128)(2,1)}, bf16[8,32,896]{2,1,0:T(8,128)(2,1)}, bf16[8,16,896]{2,1,0:T(8,128)(2,1)}, bf16[384,1024]{1,0:T(8,128)(2,1)}) custom-call(bf16[8,16,128]{2,1,0:T(8,128)(2,1)} %bitcast.18, bf16[1024,896]{1,0:T(8,128)(2,1)} %x_hbm.1, bf16[1024,896]{1,0:T(8,128)(2,1)} %dy_hbm.1), custom_call_target="tpu_custom_call" | custom-call | flops 1409286144 | bytes 5046272 | tf_op jit(solution)/shard_map/compact/pallas_call | solution.py:88
  18.9 3.6 %all-to-all-start = ((bf16[8,64,896]{2,1,0:T(8,128)(2,1)}), bf16[8,64,896]{2,1,0:T(8,128)(2,1)S(1)}, u32[]{:S(2)}, u32[]{:S(2)}) async-start(bf16[8,64,896]{2,1,0:T(8,128)(2,1)} %get-tuple-element.60), calls=%async_computation | async-start | bytes 1835008 | tf_op jit(solution)/shard_map/all_to_all | solution.py:540
  23.2 13.2 %all-to-all-done = bf16[8,64,896]{2,1,0:T(8,128)(2,1)S(1)} async-done(((bf16[8,64,896]{2,1,0:T(8,128)(2,1)}), bf16[8,64,896]{2,1,0:T(8,128)(2,1)S(1)}, u32[]{:S(2)}, u32[]{:S(2)}) %all-to-all-start) | async-done | bytes 917536 | tf_op jit(solution)/shard_map/all_to_all | solution.py:540
  37.8 4.6 %collective-permute-start.6 = (bf16[272,896]{1,0:T(8,128)(2,1)S(1)}, bf16[272,896]{1,0:T(8,128)(2,1)S(1)}, u32[]{:S(2)}, u32[]{:S(2)}) collective-permute-start(bf16[272,896]{1,0:T(8,128)(2,1)S(1)} %pad_maximum_fusion.1.refs_7_.refs_14_.refs_6_), channel_id=1, source_target_pairs={{0,1},{1,2},{2,3},{4,5},{5,6},{6,7},{8,9},{9,10},{10,11},{12,13},{... | collective-permute-start | bytes 1462280 | tf_op jit(solution)/shard_map/ppermute | solution.py:409
  43.7 5.3 %collective-permute-start = (bf16[256,896]{1,0:T(8,128)(2,1)S(1)}, bf16[256,896]{1,0:T(8,128)(2,1)}, u32[]{:S(2)}, u32[]{:S(2)}) collective-permute-start(bf16[256,896]{1,0:T(8,128)(2,1)S(1)} %bitcast.12), channel_id=1, source_target_pairs={{0,1},{1,2},{2,3},{4,5},{5,6},{6,7},{8,9},{9,10},{10,11},{12,13},{... | collective-permute-start | bytes 1376264 | tf_op jit(solution)/shard_map/ppermute | solution.py:409
  49.1 3.5 %all-to-all-start.1 = ((bf16[8,32,896]{2,1,0:T(8,128)(2,1)}), bf16[8,32,896]{2,1,0:T(8,128)(2,1)S(1)}, u32[]{:S(2)}, u32[]{:S(2)}) async-start(bf16[8,32,896]{2,1,0:T(8,128)(2,1)} %get-tuple-element.64), calls=%async_computation.1 | async-start | bytes 917504 | tf_op jit(solution)/shard_map/all_to_all | solution.py:540
  54.0 1.4 collective-permute-start.7
  55.4 6.1 %all-to-all-done.1 = bf16[8,32,896]{2,1,0:T(8,128)(2,1)S(1)} async-done(((bf16[8,32,896]{2,1,0:T(8,128)(2,1)}), bf16[8,32,896]{2,1,0:T(8,128)(2,1)S(1)}, u32[]{:S(2)}, u32[]{:S(2)}) %all-to-all-start.1) | async-done | bytes 458784 | tf_op jit(solution)/shard_map/all_to_all | solution.py:540
  63.5 6.0 %collective-permute-done.9.refs_12_.refs_19_.refs_11_ = bf16[272,896]{1,0:T(8,128)(2,1)S(1)} collective-permute-done((bf16[272,896]{1,0:T(8,128)(2,1)S(1)}, bf16[272,896]{1,0:T(8,128)(2,1)S(1)}, u32[]{:S(2)}, u32[]{:S(2)}) %collective-permute-start.9) | collective-permute-done | bytes 487456 | tf_op jit(solution)/shard_map/ppermute | solution.py:409
  69.5 1.4 collective-permute-start.10
  72.2 1.5 collective-permute-start.3
  73.7 7.3 %collective-permute-done.4.refs_5_ = bf16[256,896]{1,0:T(8,128)(2,1)} collective-permute-done((bf16[256,896]{1,0:T(8,128)(2,1)}, bf16[256,896]{1,0:T(8,128)(2,1)}, u32[]{:S(2)}, u32[]{:S(2)}) %collective-permute-start.4) | collective-permute-done | bytes 458784 | tf_op jit(solution)/shard_map/ppermute | solution.py:409
  82.3 1.4 collective-permute-start.12
  83.8 15.2 %collective-permute-done.5.refs_6_ = bf16[256,896]{1,0:T(8,128)(2,1)} collective-permute-done((bf16[256,896]{1,0:T(8,128)(2,1)}, bf16[256,896]{1,0:T(8,128)(2,1)}, u32[]{:S(2)}, u32[]{:S(2)}) %collective-permute-start.5) | collective-permute-done | bytes 458784 | tf_op jit(solution)/shard_map/ppermute | solution.py:409
  98.9 1.9 collective-permute-start.14
  100.8 4.5 %collective-permute-start.13 = (bf16[256,896]{1,0:T(8,128)(2,1)S(1)}, bf16[256,896]{1,0:T(8,128)(2,1)S(1)}, u32[]{:S(2)}, u32[]{:S(2)}) collective-permute-start(bf16[256,896]{1,0:T(8,128)(2,1)S(1)} %bitcast.16), channel_id=1, source_target_pairs={{0,2},{1,3},{2,0},{3,1},{4,6},{5,7},{6,4},{7,5},{8,10},{9,11},{10,... | collective-permute-start | bytes 1376264 | tf_op jit(solution)/shard_map/ppermute | solution.py:409
  105.3 16.0 %expert.2 = (bf16[8,128,896]{2,1,0:T(8,128)(2,1)}, bf16[128,512]{1,0:T(8,128)(2,1)}, bf16[128,512]{1,0:T(8,128)(2,1)}, bf16[8,32,896]{2,1,0:T(8,128)(2,1)}, bf16...) custom-call(s32[1]{0:T(128)} %bitcast.7.me, bf16[256,896]{1,0:T(8,128)(2,1)} %bitcast.13, ...), custom_call_target="tpu_custom_call" | custom-call | flops 46976204800 | bytes 220200960 | tf_op jit(solution)/shard_map/expert/pallas_call | solution.py:309
  121.3 2.0 %collective-permute-start.15 = (bf16[8,32,896]{2,1,0:T(8,128)(2,1)}, bf16[8,32,896]{2,1,0:T(8,128)(2,1)S(1)}, u32[]{:S(2)}, u32[]{:S(2)}) collective-permute-start(bf16[8,32,896]{2,1,0:T(8,128)(2,1)} %get-tuple-element.90), channel_id=1, source_target_pairs={{0,1},{3,2},{4,5},{7,6},{8,9},{11,10},{12,13},{15,14},{16,17},{19,... | collective-permute-start | bytes 1376264 | tf_op jit(solution)/shard_map/ppermute | solution.py:409
  126.3 4.3 %collective-permute-done.15 = bf16[8,32,896]{2,1,0:T(8,128)(2,1)S(1)} collective-permute-done((bf16[8,32,896]{2,1,0:T(8,128)(2,1)}, bf16[8,32,896]{2,1,0:T(8,128)(2,1)S(1)}, u32[]{:S(2)}, u32[]{:S(2)}) %collective-permute-start.15) | collective-permute-done | bytes 458784 | tf_op jit(solution)/shard_map/ppermute | solution.py:409
  131.7 2.5 %collective-permute-start.16 = (bf16[8,32,896]{2,1,0:T(8,128)(2,1)S(1)}, bf16[8,32,896]{2,1,0:T(8,128)(2,1)S(1)}, u32[]{:S(2)}, u32[]{:S(2)}) collective-permute-start(bf16[8,32,896]{2,1,0:T(8,128)(2,1)S(1)} %add_convert_fusion.1.refs_0_), channel_id=1, source_target_pairs={{0,2},{1,3},{2,0},{3,1},{4,6},{5,7},{6,4},{7,5},{8,10},{9,11},{10,... | collective-permute-start | bytes 1376264 | tf_op jit(solution)/shard_map/ppermute | solution.py:409
  134.2 2.3 %collective-permute-done.17.refs_5_ = bf16[256,896]{1,0:T(8,128)(2,1)S(1)} collective-permute-done((bf16[256,896]{1,0:T(8,128)(2,1)S(1)}, bf16[256,896]{1,0:T(8,128)(2,1)S(1)}, u32[]{:S(2)}, u32[]{:S(2)}) %collective-permute-start.17) | collective-permute-done | bytes 458784 | tf_op jit(solution)/shard_map/ppermute | solution.py:409
  137.3 15.1 %expert.3 = (bf16[8,64,896]{2,1,0:T(8,128)(2,1)}, bf16[64,512]{1,0:T(8,128)(2,1)}, bf16[64,512]{1,0:T(8,128)(2,1)}, bf16[8,16,896]{2,1,0:T(8,128)(2,1)}, bf16[8,...) custom-call(s32[1]{0:T(128)} %bitcast.7.me, bf16[8,32,896]{2,1,0:T(8,128)(2,1)} %copy-done.5, ...), custom_call_target="tpu_custom_call" | custom-call | flops 23488102400 | bytes 220200960 | tf_op jit(solution)/shard_map/expert/pallas_call | solution.py:309
  152.4 3.3 %collective-permute-start.20 = (bf16[8,16,896]{2,1,0:T(8,128)(2,1)}, bf16[8,16,896]{2,1,0:T(8,128)(2,1)S(1)}, u32[]{:S(2)}, u32[]{:S(2)}) collective-permute-start(bf16[8,16,896]{2,1,0:T(8,128)(2,1)} %get-tuple-element.106), channel_id=1, source_target_pairs={{0,1},{3,2},{4,5},{7,6},{8,9},{11,10},{12,13},{15,14},{16,17},{19,... | collective-permute-start | bytes 688136 | tf_op jit(solution)/shard_map/ppermute | solution.py:409
  155.7 2.5 %collective-permute-done.16 = bf16[8,32,896]{2,1,0:T(8,128)(2,1)S(1)} collective-permute-done((bf16[8,32,896]{2,1,0:T(8,128)(2,1)S(1)}, bf16[8,32,896]{2,1,0:T(8,128)(2,1)S(1)}, u32[]{:S(2)}, u32[]{:S(2)}) %collective-permute-start.16) | collective-permute-done | bytes 458784 | tf_op jit(solution)/shard_map/ppermute | solution.py:409
  158.2 3.1 %collective-permute-done.20 = bf16[8,16,896]{2,1,0:T(8,128)(2,1)S(1)} collective-permute-done((bf16[8,16,896]{2,1,0:T(8,128)(2,1)}, bf16[8,16,896]{2,1,0:T(8,128)(2,1)S(1)}, u32[]{:S(2)}, u32[]{:S(2)}) %collective-permute-start.20) | collective-permute-done | bytes 229408 | tf_op jit(solution)/shard_map/ppermute | solution.py:409
  162.3 2.9 %collective-permute-start.21 = (bf16[8,16,896]{2,1,0:T(8,128)(2,1)S(1)}, bf16[8,16,896]{2,1,0:T(8,128)(2,1)S(1)}, u32[]{:S(2)}, u32[]{:S(2)}) collective-permute-start(bf16[8,16,896]{2,1,0:T(8,128)(2,1)S(1)} %add_convert_fusion.3), channel_id=1, source_target_pairs={{0,2},{1,3},{2,0},{3,1},{4,6},{5,7},{6,4},{7,5},{8,10},{9,11},{10,... | collective-permute-start | bytes 688136 | tf_op jit(solution)/shard_map/ppermute | solution.py:409
  166.1 5.8 %collective-permute-done.21 = bf16[8,16,896]{2,1,0:T(8,128)(2,1)S(1)} collective-permute-done((bf16[8,16,896]{2,1,0:T(8,128)(2,1)S(1)}, bf16[8,16,896]{2,1,0:T(8,128)(2,1)S(1)}, u32[]{:S(2)}, u32[]{:S(2)}) %collective-permute-start.21) | collective-permute-done | bytes 229408 | tf_op jit(solution)/shard_map/ppermute | solution.py:409
  173.0 7.0 %all-to-all-start.2 = ((bf16[8,48,896]{2,1,0:T(8,128)(2,1)}), bf16[8,48,896]{2,1,0:T(8,128)(2,1)S(1)}, u32[]{:S(2)}, u32[]{:S(2)}) async-start(bf16[8,48,896]{2,1,0:T(8,128)(2,1)} %pad_maximum_fusion), calls=%async_computation.2 | async-start | bytes 1376256 | tf_op jit(solution)/shard_map/all_to_all | solution.py:540
  180.0 10.1 %weight_grads.1 = (bf16[1,7168,512]{2,1,0:T(8,128)(2,1)}, bf16[1,7168,512]{2,1,0:T(8,128)(2,1)}) custom-call(bf16[8,128,896]{2,1,0:T(8,128)(2,1)} %get-tuple-element.107.refs_0_, bf16[8,64,896]{2,1,0:T(8,128)(2,1)} %get-tuple-element.108.refs_1_, bf16[128,512]{1,0:T(8,128)(2,1)} %get-tuple-element.109.refs_2_, bf16[64,512]{1,0:T(8,128)(2,1)} %get-tuple-element.110.refs_3_, ...), custom_call_target="tpu_custom_call" | custom-call | flops 2818572288 | bytes 14680064 | tf_op jit(solution)/shard_map/weight_grads/pallas_call | solution.py:360
  190.1 1.4 all-to-all-done.2.rows
  191.5 2.5 %scatter.1 = bf16[1024,896]{1,0:T(8,128)(2,1)} custom-call(bf16[384,1024]{1,0:T(8,128)(2,1)S(1)} %copy-done, bf16[8,48,896]{2,1,0:T(8,128)(2,1)S(1)} %all-to-all-done.2.rows), custom_call_target="tpu_custom_call" | custom-call | flops 704643072 | bytes 4456448 | tf_op jit(solution)/shard_map/scatter/pallas_call | solution.py:382
  (66 shorter events, 18.7 us)
Async XLA Ops:
  18.9 17.5 %all-to-all-start = ((bf16[8,64,896]{2,1,0:T(8,128)(2,1)}), bf16[8,64,896]{2,1,0:T(8,128)(2,1)S(1)}, u32[]{:S(2)}, u32[]{:S(2)}) async-start(bf16[8,64,896]{2,1,0:T(8,128)(2,1)} %get-tuple-element.60), calls=%async_computation | async-start | bytes 1835008 | tf_op jit(solution)/shard_map/all_to_all | solution.py:540
  36.5 68.8 %copy-start.2 = (bf16[8,32,896]{2,1,0:T(8,128)(2,1)}, bf16[8,32,896]{2,1,0:T(8,128)(2,1)S(1)}, u32[]{:S(2)}) copy-start(bf16[8,32,896]{2,1,0:T(8,128)(2,1)S(1)} %get-tuple-element.116) | copy-start | bytes 1376260
  36.5 68.8 %copy-start.1 = (bf16[272,896]{1,0:T(8,128)(2,1)}, bf16[272,896]{1,0:T(8,128)(2,1)S(1)}, u32[]{:S(2)}) copy-start(bf16[272,896]{1,0:T(8,128)(2,1)S(1)} %pad_maximum_fusion.1.refs_7_.refs_14_.refs_6_) | copy-start | bytes 1462276
  36.5 16.0 %collective-permute-start.8 = (bf16[272,896]{1,0:T(8,128)(2,1)S(1)}, bf16[272,896]{1,0:T(8,128)(2,1)S(1)}, u32[]{:S(2)}, u32[]{:S(2)}) collective-permute-start(bf16[272,896]{1,0:T(8,128)(2,1)S(1)} %pad_maximum_fusion.1.refs_7_.refs_14_.refs_6_), channel_id=1, source_target_pairs={{1,0},{2,1},{3,2},{5,4},{6,5},{7,6},{9,8},{10,9},{11,10},{13,12},{... | collective-permute-start | bytes 1462280 | tf_op jit(solution)/shard_map/ppermute | solution.py:409
  37.8 16.1 %collective-permute-start.6 = (bf16[272,896]{1,0:T(8,128)(2,1)S(1)}, bf16[272,896]{1,0:T(8,128)(2,1)S(1)}, u32[]{:S(2)}, u32[]{:S(2)}) collective-permute-start(bf16[272,896]{1,0:T(8,128)(2,1)S(1)} %pad_maximum_fusion.1.refs_7_.refs_14_.refs_6_), channel_id=1, source_target_pairs={{0,1},{1,2},{2,3},{4,5},{5,6},{6,7},{8,9},{9,10},{10,11},{12,13},{... | collective-permute-start | bytes 1462280 | tf_op jit(solution)/shard_map/ppermute | solution.py:409
  42.4 19.1 %collective-permute-start.1 = (bf16[256,896]{1,0:T(8,128)(2,1)S(1)}, bf16[256,896]{1,0:T(8,128)(2,1)}, u32[]{:S(2)}, u32[]{:S(2)}) collective-permute-start(bf16[256,896]{1,0:T(8,128)(2,1)S(1)} %bitcast.11), channel_id=1, source_target_pairs={{1,0},{2,1},{3,2},{5,4},{6,5},{7,6},{9,8},{10,9},{11,10},{13,12},{... | collective-permute-start | bytes 1376264 | tf_op jit(solution)/shard_map/ppermute | solution.py:409
  43.7 17.8 %collective-permute-start = (bf16[256,896]{1,0:T(8,128)(2,1)S(1)}, bf16[256,896]{1,0:T(8,128)(2,1)}, u32[]{:S(2)}, u32[]{:S(2)}) collective-permute-start(bf16[256,896]{1,0:T(8,128)(2,1)S(1)} %bitcast.12), channel_id=1, source_target_pairs={{0,1},{1,2},{2,3},{4,5},{5,6},{6,7},{8,9},{9,10},{10,11},{12,13},{... | collective-permute-start | bytes 1376264 | tf_op jit(solution)/shard_map/ppermute | solution.py:409
  49.1 12.5 %all-to-all-start.1 = ((bf16[8,32,896]{2,1,0:T(8,128)(2,1)}), bf16[8,32,896]{2,1,0:T(8,128)(2,1)S(1)}, u32[]{:S(2)}, u32[]{:S(2)}) async-start(bf16[8,32,896]{2,1,0:T(8,128)(2,1)} %get-tuple-element.64), calls=%async_computation.1 | async-start | bytes 917504 | tf_op jit(solution)/shard_map/all_to_all | solution.py:540
  52.6 52.8 %copy-start.7 = (bf16[272,896]{1,0:T(8,128)(2,1)}, bf16[272,896]{1,0:T(8,128)(2,1)S(1)}, u32[]{:S(2)}) copy-start(bf16[272,896]{1,0:T(8,128)(2,1)S(1)} %collective-permute-done.8.refs_11_.refs_18_.refs_10_) | copy-start | bytes 1462276
  52.6 16.9 %collective-permute-start.9 = (bf16[272,896]{1,0:T(8,128)(2,1)S(1)}, bf16[272,896]{1,0:T(8,128)(2,1)S(1)}, u32[]{:S(2)}, u32[]{:S(2)}) collective-permute-start(bf16[272,896]{1,0:T(8,128)(2,1)S(1)} %collective-permute-done.8.refs_11_.refs_18_.refs_10_), channel_id=1, source_target_pairs={{1,0},{2,1},{5,4},{6,5},{9,8},{10,9},{13,12},{14,13},{17,16},{18,1... | collective-permute-start | bytes 1462280 | tf_op jit(solution)/shard_map/ppermute | solution.py:409
  54.0 51.3 %copy-start.8 = (bf16[272,896]{1,0:T(8,128)(2,1)}, bf16[272,896]{1,0:T(8,128)(2,1)S(1)}, u32[]{:S(2)}) copy-start(bf16[272,896]{1,0:T(8,128)(2,1)S(1)} %collective-permute-done.6.refs_8_.refs_15_.refs_7_) | copy-start | bytes 1462276
  54.0 15.5 %collective-permute-start.7 = (bf16[272,896]{1,0:T(8,128)(2,1)S(1)}, bf16[272,896]{1,0:T(8,128)(2,1)}, u32[]{:S(2)}, u32[]{:S(2)}) collective-permute-start(bf16[272,896]{1,0:T(8,128)(2,1)S(1)} %collective-permute-done.6.refs_8_.refs_15_.refs_7_), channel_id=1, source_target_pairs={{1,2},{2,3},{5,6},{6,7},{9,10},{10,11},{13,14},{14,15},{17,18},{18... | collective-permute-start | bytes 1462280 | tf_op jit(solution)/shard_map/ppermute | solution.py:409
  61.5 59.8 %copy-start.3 = (bf16[8,32,896]{2,1,0:T(8,128)(2,1)}, bf16[8,32,896]{2,1,0:T(8,128)(2,1)S(1)}, u32[]{:S(2)}) copy-start(bf16[8,32,896]{2,1,0:T(8,128)(2,1)S(1)} %all-to-all-done.1) | copy-start | bytes 1376260
  61.5 10.7 %collective-permute-start.2 = (bf16[256,896]{1,0:T(8,128)(2,1)}, bf16[256,896]{1,0:T(8,128)(2,1)S(1)}, u32[]{:S(2)}, u32[]{:S(2)}) collective-permute-start(bf16[256,896]{1,0:T(8,128)(2,1)} %collective-permute-done.refs_1_), channel_id=1, source_target_pairs={{1,2},{2,3},{5,6},{6,7},{9,10},{10,11},{13,14},{14,15},{17,18},{18... | collective-permute-start | bytes 1376264 | tf_op jit(solution)/shard_map/ppermute | solution.py:409
  62.2 18.8 %collective-permute-start.4 = (bf16[256,896]{1,0:T(8,128)(2,1)}, bf16[256,896]{1,0:T(8,128)(2,1)}, u32[]{:S(2)}, u32[]{:S(2)}) collective-permute-start(bf16[256,896]{1,0:T(8,128)(2,1)} %collective-permute-done.1.refs_4_), channel_id=1, source_target_pairs={{1,0},{2,1},{5,4},{6,5},{9,8},{10,9},{13,12},{14,13},{17,16},{18,1... | collective-permute-start | bytes 1376264 | tf_op jit(solution)/shard_map/ppermute | solution.py:409
  69.5 29.5 %collective-permute-start.10 = (bf16[272,896]{1,0:T(8,128)(2,1)}, bf16[272,896]{1,0:T(8,128)(2,1)}, u32[]{:S(2)}, u32[]{:S(2)}) collective-permute-start(bf16[272,896]{1,0:T(8,128)(2,1)} %collective-permute-done.7.refs_9_.refs_16_.refs_8_), channel_id=1, source_target_pairs={{2,3},{6,7},{10,11},{14,15},{18,19},{22,23},{26,27},{30,31}} | collective-permute-start | bytes 1462280 | tf_op jit(solution)/shard_map/ppermute | solution.py:409
  70.9 28.0 %collective-permute-start.11 = (bf16[272,896]{1,0:T(8,128)(2,1)S(1)}, bf16[272,896]{1,0:T(8,128)(2,1)}, u32[]{:S(2)}, u32[]{:S(2)}) collective-permute-start(bf16[272,896]{1,0:T(8,128)(2,1)S(1)} %collective-permute-done.9.refs_12_.refs_19_.refs_11_), channel_id=1, source_target_pairs={{1,0},{5,4},{9,8},{13,12},{17,16},{21,20},{25,24},{29,28}} | collective-permute-start | bytes 1462280 | tf_op jit(solution)/shard_map/ppermute | solution.py:409
  72.2 11.5 %collective-permute-start.3 = (bf16[256,896]{1,0:T(8,128)(2,1)S(1)}, bf16[256,896]{1,0:T(8,128)(2,1)}, u32[]{:S(2)}, u32[]{:S(2)}) collective-permute-start(bf16[256,896]{1,0:T(8,128)(2,1)S(1)} %collective-permute-done.2.refs_2_), channel_id=1, source_target_pairs={{2,3},{6,7},{10,11},{14,15},{18,19},{22,23},{26,27},{30,31}} | collective-permute-start | bytes 1376264 | tf_op jit(solution)/shard_map/ppermute | solution.py:409
  81.0 17.9 %collective-permute-start.5 = (bf16[256,896]{1,0:T(8,128)(2,1)}, bf16[256,896]{1,0:T(8,128)(2,1)}, u32[]{:S(2)}, u32[]{:S(2)}) collective-permute-start(bf16[256,896]{1,0:T(8,128)(2,1)} %collective-permute-done.4.refs_5_), channel_id=1, source_target_pairs={{1,0},{5,4},{9,8},{13,12},{17,16},{21,20},{25,24},{29,28}} | collective-permute-start | bytes 1376264 | tf_op jit(solution)/shard_map/ppermute | solution.py:409
  82.3 16.6 %collective-permute-start.12 = (bf16[256,896]{1,0:T(8,128)(2,1)S(1)}, bf16[256,896]{1,0:T(8,128)(2,1)}, u32[]{:S(2)}, u32[]{:S(2)}) collective-permute-start(bf16[256,896]{1,0:T(8,128)(2,1)S(1)} %bitcast.14), channel_id=1, source_target_pairs={{1,2},{2,1},{5,6},{6,5},{9,10},{10,9},{13,14},{14,13},{17,18},{18,... | collective-permute-start | bytes 1376264 | tf_op jit(solution)/shard_map/ppermute | solution.py:409
  98.9 24.4 %collective-permute-start.14 = (bf16[256,896]{1,0:T(8,128)(2,1)S(1)}, bf16[256,896]{1,0:T(8,128)(2,1)S(1)}, u32[]{:S(2)}, u32[]{:S(2)}) collective-permute-start(bf16[256,896]{1,0:T(8,128)(2,1)S(1)} %bitcast.15), channel_id=1, source_target_pairs={{0,1},{1,0},{2,3},{3,2},{4,5},{5,4},{6,7},{7,6},{8,9},{9,8},{10,11... | collective-permute-start | bytes 1376264 | tf_op jit(solution)/shard_map/ppermute | solution.py:409
  100.8 22.5 %collective-permute-start.13 = (bf16[256,896]{1,0:T(8,128)(2,1)S(1)}, bf16[256,896]{1,0:T(8,128)(2,1)S(1)}, u32[]{:S(2)}, u32[]{:S(2)}) collective-permute-start(bf16[256,896]{1,0:T(8,128)(2,1)S(1)} %bitcast.16), channel_id=1, source_target_pairs={{0,2},{1,3},{2,0},{3,1},{4,6},{5,7},{6,4},{7,5},{8,10},{9,11},{10,... | collective-permute-start | bytes 1376264 | tf_op jit(solution)/shard_map/ppermute | solution.py:409
  121.3 9.2 %collective-permute-start.15 = (bf16[8,32,896]{2,1,0:T(8,128)(2,1)}, bf16[8,32,896]{2,1,0:T(8,128)(2,1)S(1)}, u32[]{:S(2)}, u32[]{:S(2)}) collective-permute-start(bf16[8,32,896]{2,1,0:T(8,128)(2,1)} %get-tuple-element.90), channel_id=1, source_target_pairs={{0,1},{3,2},{4,5},{7,6},{8,9},{11,10},{12,13},{15,14},{16,17},{19,... | collective-permute-start | bytes 1376264 | tf_op jit(solution)/shard_map/ppermute | solution.py:409
  124.1 12.4 %collective-permute-start.17 = (bf16[256,896]{1,0:T(8,128)(2,1)S(1)}, bf16[256,896]{1,0:T(8,128)(2,1)S(1)}, u32[]{:S(2)}, u32[]{:S(2)}) collective-permute-start(bf16[256,896]{1,0:T(8,128)(2,1)S(1)} %collective-permute-done.13.refs_3_), channel_id=1, source_target_pairs={{1,0},{2,3},{5,4},{6,7},{9,8},{10,11},{13,12},{14,15},{17,16},{18,... | collective-permute-start | bytes 1376264 | tf_op jit(solution)/shard_map/ppermute | solution.py:409
  125.4 30.3 %collective-permute-start.19 = (bf16[8,32,896]{2,1,0:T(8,128)(2,1)}, bf16[8,32,896]{2,1,0:T(8,128)(2,1)S(1)}, u32[]{:S(2)}, u32[]{:S(2)}) collective-permute-start(bf16[8,32,896]{2,1,0:T(8,128)(2,1)} %get-tuple-element.90), channel_id=1, source_target_pairs={{1,2},{2,1},{5,6},{6,5},{9,10},{10,9},{13,14},{14,13},{17,18},{18,... | collective-permute-start | bytes 1376264 | tf_op jit(solution)/shard_map/ppermute | solution.py:409
  131.7 26.4 %collective-permute-start.16 = (bf16[8,32,896]{2,1,0:T(8,128)(2,1)S(1)}, bf16[8,32,896]{2,1,0:T(8,128)(2,1)S(1)}, u32[]{:S(2)}, u32[]{:S(2)}) collective-permute-start(bf16[8,32,896]{2,1,0:T(8,128)(2,1)S(1)} %add_convert_fusion.1.refs_0_), channel_id=1, source_target_pairs={{0,2},{1,3},{2,0},{3,1},{4,6},{5,7},{6,4},{7,5},{8,10},{9,11},{10,... | collective-permute-start | bytes 1376264 | tf_op jit(solution)/shard_map/ppermute | solution.py:409
  136.5 21.7 %collective-permute-start.18 = (bf16[8,32,896]{2,1,0:T(8,128)(2,1)}, bf16[8,32,896]{2,1,0:T(8,128)(2,1)S(1)}, u32[]{:S(2)}, u32[]{:S(2)}) collective-permute-start(bf16[8,32,896]{2,1,0:T(8,128)(2,1)} %get-tuple-element.89), channel_id=1, source_target_pairs={{0,1},{1,0},{2,3},{3,2},{4,5},{5,4},{6,7},{7,6},{8,9},{9,8},{10,11... | collective-permute-start | bytes 1376264 | tf_op jit(solution)/shard_map/ppermute | solution.py:409
  152.4 8.9 %collective-permute-start.20 = (bf16[8,16,896]{2,1,0:T(8,128)(2,1)}, bf16[8,16,896]{2,1,0:T(8,128)(2,1)S(1)}, u32[]{:S(2)}, u32[]{:S(2)}) collective-permute-start(bf16[8,16,896]{2,1,0:T(8,128)(2,1)} %get-tuple-element.106), channel_id=1, source_target_pairs={{0,1},{3,2},{4,5},{7,6},{8,9},{11,10},{12,13},{15,14},{16,17},{19,... | collective-permute-start | bytes 688136 | tf_op jit(solution)/shard_map/ppermute | solution.py:409
  162.3 9.5 %collective-permute-start.21 = (bf16[8,16,896]{2,1,0:T(8,128)(2,1)S(1)}, bf16[8,16,896]{2,1,0:T(8,128)(2,1)S(1)}, u32[]{:S(2)}, u32[]{:S(2)}) collective-permute-start(bf16[8,16,896]{2,1,0:T(8,128)(2,1)S(1)} %add_convert_fusion.3), channel_id=1, source_target_pairs={{0,2},{1,3},{2,0},{3,1},{4,6},{5,7},{6,4},{7,5},{8,10},{9,11},{10,... | collective-permute-start | bytes 688136 | tf_op jit(solution)/shard_map/ppermute | solution.py:409
  165.1 6.8 %collective-permute-start.22 = (bf16[8,16,896]{2,1,0:T(8,128)(2,1)}, bf16[8,16,896]{2,1,0:T(8,128)(2,1)S(1)}, u32[]{:S(2)}, u32[]{:S(2)}) collective-permute-start(bf16[8,16,896]{2,1,0:T(8,128)(2,1)} %get-tuple-element.105), channel_id=1, source_target_pairs={{0,1},{1,0},{2,3},{3,2},{4,5},{5,4},{6,7},{7,6},{8,9},{9,8},{10,11... | collective-permute-start | bytes 688136 | tf_op jit(solution)/shard_map/ppermute | solution.py:409
  165.1 6.8 %collective-permute-start.23 = (bf16[8,16,896]{2,1,0:T(8,128)(2,1)}, bf16[8,16,896]{2,1,0:T(8,128)(2,1)S(1)}, u32[]{:S(2)}, u32[]{:S(2)}) collective-permute-start(bf16[8,16,896]{2,1,0:T(8,128)(2,1)} %get-tuple-element.106), channel_id=1, source_target_pairs={{1,2},{2,1},{5,6},{6,5},{9,10},{10,9},{13,14},{14,13},{17,18},{18,... | collective-permute-start | bytes 688136 | tf_op jit(solution)/shard_map/ppermute | solution.py:409
  173.0 18.5 %all-to-all-start.2 = ((bf16[8,48,896]{2,1,0:T(8,128)(2,1)}), bf16[8,48,896]{2,1,0:T(8,128)(2,1)S(1)}, u32[]{:S(2)}, u32[]{:S(2)}) async-start(bf16[8,48,896]{2,1,0:T(8,128)(2,1)} %pad_maximum_fusion), calls=%async_computation.2 | async-start | bytes 1376256 | tf_op jit(solution)/shard_map/all_to_all | solution.py:540
  (9 other events, 151.3 us)

commit v7 on v6

--- a/solution.py
+++ b/solution.py
@@ -206,7 +206,7 @@
     coefs, refs = refs[: counts[1]], refs[counts[1] :]
     w_down, w_gate, w_up, rows_out, grad_gate, grad_up = refs[:6]
     parts, refs = refs[6 : 6 + blocks], refs[6 + blocks :]
-    x_buf, dy_buf, coef_buf, down_buf, gate_buf, up_buf, gate_pre, up_proj, out_buf = refs[:-3]
+    x_buf, dy_buf, coef_buf, down_buf, both_buf, both_pre, out_buf = refs[:-3]
     sems, coef_sem, out_sems = refs[-3:]
     pieces, total, feat = x_buf.shape
     rows = total // blocks
@@ -237,8 +237,13 @@
     x_loads = load(x, x_buf, 0, sems.at[0])
     dy_loads = load(dy, dy_buf, shift, sems.at[1])
     down_loads = weight_copies(w_down, down_buf, sems.at[2], pieces, False)
-    gate_loads = weight_copies(w_gate, gate_buf, sems.at[3], pieces, True)
-    up_loads = weight_copies(w_up, up_buf, sems.at[4], pieces, True)
+    hidden = down_buf.shape[0]
+    gate_loads = weight_copies(
+        w_gate, both_buf.at[:, :hidden], sems.at[3], pieces, True
+    )
+    up_loads = weight_copies(
+        w_up, both_buf.at[:, hidden:], sems.at[4], pieces, True
+    )
     queue = Queue(
         [[*dy_loads[f], down_loads[f]] for f in range(pieces)]
         + [coef_loads]
@@ -260,27 +265,22 @@
         stores.append(pltpu.make_async_copy(x_buf.at[f], rows_out.at[f], out_sems.at[0, f]))
         stores[-1].start()
         here = slice(f * feat, (f + 1) * feat)
-        gate = jnp.dot(x_buf[f], gate_buf[here, :], preferred_element_type=F32)
-        proj = jnp.dot(x_buf[f], up_buf[here, :], preferred_element_type=F32)
+        both = jnp.dot(x_buf[f], both_buf[here, :], preferred_element_type=F32)
         if f == 0:
-            gate_pre[...] = gate
-            up_proj[...] = proj
+            both_pre[...] = both
         else:
-            gate_pre[...] += gate
-            up_proj[...] += proj
-    pre = gate_pre[...]
+            both_pre[...] += both
+    pre, proj = both_pre[:, :hidden], both_pre[:, hidden:]
     sigma = jax.nn.sigmoid(pre)
     grad_gate[...] = (
-        grad_hidden * up_proj[...] * sigma * (1.0 + pre * (1.0 - sigma))
+        grad_hidden * proj * sigma * (1.0 + pre * (1.0 - sigma))
     ).astype(BF)
     grad_up[...] = (grad_hidden * (pre * sigma)).astype(BF)
+    both_grads = jnp.concatenate([grad_gate[...], grad_up[...]], axis=1)
     for f in range(pieces):
         here = slice(f * feat, (f + 1) * feat)
         value = lax.dot_general(
-            grad_gate[...], gate_buf[here, :], ROWS_DIMS, preferred_element_type=F32
-        )
-        value += lax.dot_general(
-            grad_up[...], up_buf[here, :], ROWS_DIMS, preferred_element_type=F32
+            both_grads, both_buf[here, :], ROWS_DIMS, preferred_element_type=F32
         )
         out_buf[f] = value.astype(BF)
         for k in range(blocks):
@@ -323,10 +323,8 @@
             pltpu.VMEM(big, BF),
             pltpu.VMEM((blocks, TILE, coefs[0].shape[1]), BF),
             pltpu.VMEM((hidden, model), BF),
-            pltpu.VMEM((model, hidden), BF),
-            pltpu.VMEM((model, hidden), BF),
-            pltpu.VMEM((total, hidden), F32),
-            pltpu.VMEM((total, hidden), F32),
+            pltpu.VMEM((model, 2 * hidden), BF),
+            pltpu.VMEM((total, 2 * hidden), F32),
             pltpu.VMEM(big, BF),
             pltpu.SemaphoreType.DMA((5, pieces)),
             pltpu.SemaphoreType.DMA((1,)),

time: 195 us -> 195 us (level)
  transfers between devices with their start and end apart: 27 -> 27, of which waited for: 13 -> 12; matrix products, arithmetic and copies ran while one was open for 1% -> 1% of each run, Pallas kernels for 21% -> 21%
where the time goes in v7:
time: 195 us; the launch traced here: 194 us
  waiting for transfers between devices  67.8 us (35%)
  starting transfers between devices  57.3 us (29%)
  Pallas kernels  49.2 us (25%)
  blocking collectives  11.5 us (6%)
  other arithmetic  4.8 us (2%)
  local copies, waits for them, and re-layouts  2.41 us (1%)
    ppermute x24, waiting for transfers between devices, send(): return lax.ppermute(value, 'dp', pairs)  47.1 us
    ppermute x24, starting transfers between devices, send(): return lax.ppermute(value, 'dp', pairs)  43.5 us
    pallas_call x2, Pallas kernels, expert_pass(): pl.pallas_call(functools.partial(expert_kernel, (count, len(coefs), apart...  31.2 us
    all_to_all x3, waiting for transfers between devices, exchange(): lax.all_to_all(values, 'expert', split_axis=0, concat_axis=0, tiled=True)  20.7 us
    all_to_all x3, starting transfers between devices, exchange(): lax.all_to_all(values, 'expert', split_axis=0, concat_axis=0, tiled=True)  13.8 us
    all_gather x1, blocking collectives, per_device(): table = lax.all_gather(label(routes.T, gates.T, experts), 'expert', axis=0)  11.5 us
    pallas_call x1, Pallas kernels, weight_grads(): pl.pallas_call(functools.partial(weights_kernel, len(x)), grid=(pieces,),...  10.1 us
    pallas_call x1, Pallas kernels, compact(): pl.pallas_call(functools.partial(compact_kernel, experts, first, second),...  5.37 us
  transfers between devices with their start and end apart: 27, of which 12 were waited for; matrix products, arithmetic and copies ran while one was open for 1% of the time, Pallas kernels for 21%

profile of v7, /device:TPU:0, one launch (start us, length us, event | category | flops | bytes accessed | tf_op | source)
XLA Modules:
  0.0 194.0 jit_solution(17110958184875896148)
XLA Ops:
  2.0 11.5 %all-gather = bf16[128,128]{1,0:T(8,128)(2,1)} all-gather(bf16[16,128]{1,0:T(8,128)(2,1)S(1)} %add_convert_fusion.4), channel_id=2, replica_groups=mesh['expert'=8,'dp'=4] {'expert'}, dimensions={0}, use_global_device_ids=true | all-gather | bytes 36864 | tf_op jit(solution)/shard_map/all_gather | solution.py:540
  13.5 5.4 %compact.1 = (bf16[8,64,896]{2,1,0:T(8,128)(2,1)}, bf16[8,32,896]{2,1,0:T(8,128)(2,1)}, bf16[8,16,896]{2,1,0:T(8,128)(2,1)}, bf16[384,1024]{1,0:T(8,128)(2,1)}) custom-call(bf16[8,16,128]{2,1,0:T(8,128)(2,1)} %bitcast.18, bf16[1024,896]{1,0:T(8,128)(2,1)} %x_hbm.1, bf16[1024,896]{1,0:T(8,128)(2,1)} %dy_hbm.1), custom_call_target="tpu_custom_call" | custom-call | flops 1409286144 | bytes 5046272 | tf_op jit(solution)/shard_map/compact/pallas_call | solution.py:88
  18.9 3.6 %all-to-all-start = ((bf16[8,64,896]{2,1,0:T(8,128)(2,1)}), bf16[8,64,896]{2,1,0:T(8,128)(2,1)S(1)}, u32[]{:S(2)}, u32[]{:S(2)}) async-start(bf16[8,64,896]{2,1,0:T(8,128)(2,1)} %get-tuple-element.60), calls=%async_computation | async-start | bytes 1835008 | tf_op jit(solution)/shard_map/all_to_all | solution.py:538
  23.2 13.2 %all-to-all-done = bf16[8,64,896]{2,1,0:T(8,128)(2,1)S(1)} async-done(((bf16[8,64,896]{2,1,0:T(8,128)(2,1)}), bf16[8,64,896]{2,1,0:T(8,128)(2,1)S(1)}, u32[]{:S(2)}, u32[]{:S(2)}) %all-to-all-start) | async-done | bytes 917536 | tf_op jit(solution)/shard_map/all_to_all | solution.py:538
  37.8 4.6 %collective-permute-start.6 = (bf16[272,896]{1,0:T(8,128)(2,1)S(1)}, bf16[272,896]{1,0:T(8,128)(2,1)S(1)}, u32[]{:S(2)}, u32[]{:S(2)}) collective-permute-start(bf16[272,896]{1,0:T(8,128)(2,1)S(1)} %pad_maximum_fusion.1.refs_7_.refs_14_.refs_6_), channel_id=1, source_target_pairs={{0,1},{1,2},{2,3},{4,5},{5,6},{6,7},{8,9},{9,10},{10,11},{12,13},{... | collective-permute-start | bytes 1462280 | tf_op jit(solution)/shard_map/ppermute | solution.py:407
  43.7 5.3 %collective-permute-start = (bf16[256,896]{1,0:T(8,128)(2,1)S(1)}, bf16[256,896]{1,0:T(8,128)(2,1)}, u32[]{:S(2)}, u32[]{:S(2)}) collective-permute-start(bf16[256,896]{1,0:T(8,128)(2,1)S(1)} %bitcast.12), channel_id=1, source_target_pairs={{0,1},{1,2},{2,3},{4,5},{5,6},{6,7},{8,9},{9,10},{10,11},{12,13},{... | collective-permute-start | bytes 1376264 | tf_op jit(solution)/shard_map/ppermute | solution.py:407
  49.1 3.5 %all-to-all-start.1 = ((bf16[8,32,896]{2,1,0:T(8,128)(2,1)}), bf16[8,32,896]{2,1,0:T(8,128)(2,1)S(1)}, u32[]{:S(2)}, u32[]{:S(2)}) async-start(bf16[8,32,896]{2,1,0:T(8,128)(2,1)} %get-tuple-element.64), calls=%async_computation.1 | async-start | bytes 917504 | tf_op jit(solution)/shard_map/all_to_all | solution.py:538
  54.0 1.4 collective-permute-start.7
  55.4 6.1 %all-to-all-done.1 = bf16[8,32,896]{2,1,0:T(8,128)(2,1)S(1)} async-done(((bf16[8,32,896]{2,1,0:T(8,128)(2,1)}), bf16[8,32,896]{2,1,0:T(8,128)(2,1)S(1)}, u32[]{:S(2)}, u32[]{:S(2)}) %all-to-all-start.1) | async-done | bytes 458784 | tf_op jit(solution)/shard_map/all_to_all | solution.py:538
  63.5 6.0 %collective-permute-done.9.refs_12_.refs_19_.refs_11_ = bf16[272,896]{1,0:T(8,128)(2,1)S(1)} collective-permute-done((bf16[272,896]{1,0:T(8,128)(2,1)S(1)}, bf16[272,896]{1,0:T(8,128)(2,1)S(1)}, u32[]{:S(2)}, u32[]{:S(2)}) %collective-permute-start.9) | collective-permute-done | bytes 487456 | tf_op jit(solution)/shard_map/ppermute | solution.py:407
  69.5 1.4 collective-permute-start.10
  72.2 1.5 collective-permute-start.3
  73.7 7.3 %collective-permute-done.4.refs_5_ = bf16[256,896]{1,0:T(8,128)(2,1)} collective-permute-done((bf16[256,896]{1,0:T(8,128)(2,1)}, bf16[256,896]{1,0:T(8,128)(2,1)}, u32[]{:S(2)}, u32[]{:S(2)}) %collective-permute-start.4) | collective-permute-done | bytes 458784 | tf_op jit(solution)/shard_map/ppermute | solution.py:407
  82.3 1.4 collective-permute-start.12
  83.8 15.2 %collective-permute-done.5.refs_6_ = bf16[256,896]{1,0:T(8,128)(2,1)} collective-permute-done((bf16[256,896]{1,0:T(8,128)(2,1)}, bf16[256,896]{1,0:T(8,128)(2,1)}, u32[]{:S(2)}, u32[]{:S(2)}) %collective-permute-start.5) | collective-permute-done | bytes 458784 | tf_op jit(solution)/shard_map/ppermute | solution.py:407
  98.9 1.9 collective-permute-start.14
  100.8 4.5 %collective-permute-start.13 = (bf16[256,896]{1,0:T(8,128)(2,1)S(1)}, bf16[256,896]{1,0:T(8,128)(2,1)S(1)}, u32[]{:S(2)}, u32[]{:S(2)}) collective-permute-start(bf16[256,896]{1,0:T(8,128)(2,1)S(1)} %bitcast.16), channel_id=1, source_target_pairs={{0,2},{1,3},{2,0},{3,1},{4,6},{5,7},{6,4},{7,5},{8,10},{9,11},{10,... | collective-permute-start | bytes 1376264 | tf_op jit(solution)/shard_map/ppermute | solution.py:407
  105.3 16.1 %expert.2 = (bf16[8,128,896]{2,1,0:T(8,128)(2,1)}, bf16[128,512]{1,0:T(8,128)(2,1)}, bf16[128,512]{1,0:T(8,128)(2,1)}, bf16[8,32,896]{2,1,0:T(8,128)(2,1)}, bf16...) custom-call(s32[1]{0:T(128)} %bitcast.7.me, bf16[256,896]{1,0:T(8,128)(2,1)} %bitcast.13, ...), custom_call_target="tpu_custom_call" | custom-call | flops 46976204800 | bytes 220200960 | tf_op jit(solution)/shard_map/expert/pallas_call | solution.py:309
  121.4 2.0 %collective-permute-start.15 = (bf16[8,32,896]{2,1,0:T(8,128)(2,1)}, bf16[8,32,896]{2,1,0:T(8,128)(2,1)S(1)}, u32[]{:S(2)}, u32[]{:S(2)}) collective-permute-start(bf16[8,32,896]{2,1,0:T(8,128)(2,1)} %get-tuple-element.90), channel_id=1, source_target_pairs={{0,1},{3,2},{4,5},{7,6},{8,9},{11,10},{12,13},{15,14},{16,17},{19,... | collective-permute-start | bytes 1376264 | tf_op jit(solution)/shard_map/ppermute | solution.py:407
  126.4 4.4 %collective-permute-done.15 = bf16[8,32,896]{2,1,0:T(8,128)(2,1)S(1)} collective-permute-done((bf16[8,32,896]{2,1,0:T(8,128)(2,1)}, bf16[8,32,896]{2,1,0:T(8,128)(2,1)S(1)}, u32[]{:S(2)}, u32[]{:S(2)}) %collective-permute-start.15) | collective-permute-done | bytes 458784 | tf_op jit(solution)/shard_map/ppermute | solution.py:407
  131.9 2.3 %collective-permute-start.16 = (bf16[8,32,896]{2,1,0:T(8,128)(2,1)S(1)}, bf16[8,32,896]{2,1,0:T(8,128)(2,1)S(1)}, u32[]{:S(2)}, u32[]{:S(2)}) collective-permute-start(bf16[8,32,896]{2,1,0:T(8,128)(2,1)S(1)} %add_convert_fusion.1.refs_0_), channel_id=1, source_target_pairs={{0,2},{1,3},{2,0},{3,1},{4,6},{5,7},{6,4},{7,5},{8,10},{9,11},{10,... | collective-permute-start | bytes 1376264 | tf_op jit(solution)/shard_map/ppermute | solution.py:407
  134.2 2.4 %collective-permute-done.17.refs_5_ = bf16[256,896]{1,0:T(8,128)(2,1)S(1)} collective-permute-done((bf16[256,896]{1,0:T(8,128)(2,1)S(1)}, bf16[256,896]{1,0:T(8,128)(2,1)S(1)}, u32[]{:S(2)}, u32[]{:S(2)}) %collective-permute-start.17) | collective-permute-done | bytes 458784 | tf_op jit(solution)/shard_map/ppermute | solution.py:407
  137.4 15.1 %expert.3 = (bf16[8,64,896]{2,1,0:T(8,128)(2,1)}, bf16[64,512]{1,0:T(8,128)(2,1)}, bf16[64,512]{1,0:T(8,128)(2,1)}, bf16[8,16,896]{2,1,0:T(8,128)(2,1)}, bf16[8,...) custom-call(s32[1]{0:T(128)} %bitcast.7.me, bf16[8,32,896]{2,1,0:T(8,128)(2,1)} %copy-done.5, ...), custom_call_target="tpu_custom_call" | custom-call | flops 23488102400 | bytes 220200960 | tf_op jit(solution)/shard_map/expert/pallas_call | solution.py:309
  152.5 3.3 %collective-permute-start.20 = (bf16[8,16,896]{2,1,0:T(8,128)(2,1)}, bf16[8,16,896]{2,1,0:T(8,128)(2,1)S(1)}, u32[]{:S(2)}, u32[]{:S(2)}) collective-permute-start(bf16[8,16,896]{2,1,0:T(8,128)(2,1)} %get-tuple-element.106), channel_id=1, source_target_pairs={{0,1},{3,2},{4,5},{7,6},{8,9},{11,10},{12,13},{15,14},{16,17},{19,... | collective-permute-start | bytes 688136 | tf_op jit(solution)/shard_map/ppermute | solution.py:407
  155.8 2.5 %collective-permute-done.16 = bf16[8,32,896]{2,1,0:T(8,128)(2,1)S(1)} collective-permute-done((bf16[8,32,896]{2,1,0:T(8,128)(2,1)S(1)}, bf16[8,32,896]{2,1,0:T(8,128)(2,1)S(1)}, u32[]{:S(2)}, u32[]{:S(2)}) %collective-permute-start.16) | collective-permute-done | bytes 458784 | tf_op jit(solution)/shard_map/ppermute | solution.py:407
  158.3 3.4 %collective-permute-done.20 = bf16[8,16,896]{2,1,0:T(8,128)(2,1)S(1)} collective-permute-done((bf16[8,16,896]{2,1,0:T(8,128)(2,1)}, bf16[8,16,896]{2,1,0:T(8,128)(2,1)S(1)}, u32[]{:S(2)}, u32[]{:S(2)}) %collective-permute-start.20) | collective-permute-done | bytes 229408 | tf_op jit(solution)/shard_map/ppermute | solution.py:407
  162.7 2.6 %collective-permute-start.21 = (bf16[8,16,896]{2,1,0:T(8,128)(2,1)S(1)}, bf16[8,16,896]{2,1,0:T(8,128)(2,1)S(1)}, u32[]{:S(2)}, u32[]{:S(2)}) collective-permute-start(bf16[8,16,896]{2,1,0:T(8,128)(2,1)S(1)} %add_convert_fusion.3), channel_id=1, source_target_pairs={{0,2},{1,3},{2,0},{3,1},{4,6},{5,7},{6,4},{7,5},{8,10},{9,11},{10,... | collective-permute-start | bytes 688136 | tf_op jit(solution)/shard_map/ppermute | solution.py:407
  166.3 5.9 %collective-permute-done.21 = bf16[8,16,896]{2,1,0:T(8,128)(2,1)S(1)} collective-permute-done((bf16[8,16,896]{2,1,0:T(8,128)(2,1)S(1)}, bf16[8,16,896]{2,1,0:T(8,128)(2,1)S(1)}, u32[]{:S(2)}, u32[]{:S(2)}) %collective-permute-start.21) | collective-permute-done | bytes 229408 | tf_op jit(solution)/shard_map/ppermute | solution.py:407
  173.2 6.8 %all-to-all-start.2 = ((bf16[8,48,896]{2,1,0:T(8,128)(2,1)}), bf16[8,48,896]{2,1,0:T(8,128)(2,1)S(1)}, u32[]{:S(2)}, u32[]{:S(2)}) async-start(bf16[8,48,896]{2,1,0:T(8,128)(2,1)} %pad_maximum_fusion), calls=%async_computation.2 | async-start | bytes 1376256 | tf_op jit(solution)/shard_map/all_to_all | solution.py:538
  180.0 10.1 %weight_grads.1 = (bf16[1,7168,512]{2,1,0:T(8,128)(2,1)}, bf16[1,7168,512]{2,1,0:T(8,128)(2,1)}) custom-call(bf16[8,128,896]{2,1,0:T(8,128)(2,1)} %get-tuple-element.107.refs_0_, bf16[8,64,896]{2,1,0:T(8,128)(2,1)} %get-tuple-element.108.refs_1_, bf16[128,512]{1,0:T(8,128)(2,1)} %get-tuple-element.109.refs_2_, bf16[64,512]{1,0:T(8,128)(2,1)} %get-tuple-element.110.refs_3_, ...), custom_call_target="tpu_custom_call" | custom-call | flops 2818572288 | bytes 14680064 | tf_op jit(solution)/shard_map/weight_grads/pallas_call | solution.py:358
  190.1 1.4 all-to-all-done.2.rows
  191.5 2.5 %scatter.1 = bf16[1024,896]{1,0:T(8,128)(2,1)} custom-call(bf16[384,1024]{1,0:T(8,128)(2,1)S(1)} %copy-done, bf16[8,48,896]{2,1,0:T(8,128)(2,1)S(1)} %all-to-all-done.2.rows), custom_call_target="tpu_custom_call" | custom-call | flops 704643072 | bytes 4456448 | tf_op jit(solution)/shard_map/scatter/pallas_call | solution.py:380
  (66 shorter events, 18.6 us)
Async XLA Ops:
  18.9 17.5 %all-to-all-start = ((bf16[8,64,896]{2,1,0:T(8,128)(2,1)}), bf16[8,64,896]{2,1,0:T(8,128)(2,1)S(1)}, u32[]{:S(2)}, u32[]{:S(2)}) async-start(bf16[8,64,896]{2,1,0:T(8,128)(2,1)} %get-tuple-element.60), calls=%async_computation | async-start | bytes 1835008 | tf_op jit(solution)/shard_map/all_to_all | solution.py:538
  36.5 68.8 %copy-start.2 = (bf16[8,32,896]{2,1,0:T(8,128)(2,1)}, bf16[8,32,896]{2,1,0:T(8,128)(2,1)S(1)}, u32[]{:S(2)}) copy-start(bf16[8,32,896]{2,1,0:T(8,128)(2,1)S(1)} %get-tuple-element.116) | copy-start | bytes 1376260
  36.5 68.8 %copy-start.1 = (bf16[272,896]{1,0:T(8,128)(2,1)}, bf16[272,896]{1,0:T(8,128)(2,1)S(1)}, u32[]{:S(2)}) copy-start(bf16[272,896]{1,0:T(8,128)(2,1)S(1)} %pad_maximum_fusion.1.refs_7_.refs_14_.refs_6_) | copy-start | bytes 1462276
  36.5 16.0 %collective-permute-start.8 = (bf16[272,896]{1,0:T(8,128)(2,1)S(1)}, bf16[272,896]{1,0:T(8,128)(2,1)S(1)}, u32[]{:S(2)}, u32[]{:S(2)}) collective-permute-start(bf16[272,896]{1,0:T(8,128)(2,1)S(1)} %pad_maximum_fusion.1.refs_7_.refs_14_.refs_6_), channel_id=1, source_target_pairs={{1,0},{2,1},{3,2},{5,4},{6,5},{7,6},{9,8},{10,9},{11,10},{13,12},{... | collective-permute-start | bytes 1462280 | tf_op jit(solution)/shard_map/ppermute | solution.py:407
  37.8 16.1 %collective-permute-start.6 = (bf16[272,896]{1,0:T(8,128)(2,1)S(1)}, bf16[272,896]{1,0:T(8,128)(2,1)S(1)}, u32[]{:S(2)}, u32[]{:S(2)}) collective-permute-start(bf16[272,896]{1,0:T(8,128)(2,1)S(1)} %pad_maximum_fusion.1.refs_7_.refs_14_.refs_6_), channel_id=1, source_target_pairs={{0,1},{1,2},{2,3},{4,5},{5,6},{6,7},{8,9},{9,10},{10,11},{12,13},{... | collective-permute-start | bytes 1462280 | tf_op jit(solution)/shard_map/ppermute | solution.py:407
  42.4 19.1 %collective-permute-start.1 = (bf16[256,896]{1,0:T(8,128)(2,1)S(1)}, bf16[256,896]{1,0:T(8,128)(2,1)}, u32[]{:S(2)}, u32[]{:S(2)}) collective-permute-start(bf16[256,896]{1,0:T(8,128)(2,1)S(1)} %bitcast.11), channel_id=1, source_target_pairs={{1,0},{2,1},{3,2},{5,4},{6,5},{7,6},{9,8},{10,9},{11,10},{13,12},{... | collective-permute-start | bytes 1376264 | tf_op jit(solution)/shard_map/ppermute | solution.py:407
  43.7 17.8 %collective-permute-start = (bf16[256,896]{1,0:T(8,128)(2,1)S(1)}, bf16[256,896]{1,0:T(8,128)(2,1)}, u32[]{:S(2)}, u32[]{:S(2)}) collective-permute-start(bf16[256,896]{1,0:T(8,128)(2,1)S(1)} %bitcast.12), channel_id=1, source_target_pairs={{0,1},{1,2},{2,3},{4,5},{5,6},{6,7},{8,9},{9,10},{10,11},{12,13},{... | collective-permute-start | bytes 1376264 | tf_op jit(solution)/shard_map/ppermute | solution.py:407
  49.1 12.5 %all-to-all-start.1 = ((bf16[8,32,896]{2,1,0:T(8,128)(2,1)}), bf16[8,32,896]{2,1,0:T(8,128)(2,1)S(1)}, u32[]{:S(2)}, u32[]{:S(2)}) async-start(bf16[8,32,896]{2,1,0:T(8,128)(2,1)} %get-tuple-element.64), calls=%async_computation.1 | async-start | bytes 917504 | tf_op jit(solution)/shard_map/all_to_all | solution.py:538
  52.6 52.8 %copy-start.7 = (bf16[272,896]{1,0:T(8,128)(2,1)}, bf16[272,896]{1,0:T(8,128)(2,1)S(1)}, u32[]{:S(2)}) copy-start(bf16[272,896]{1,0:T(8,128)(2,1)S(1)} %collective-permute-done.8.refs_11_.refs_18_.refs_10_) | copy-start | bytes 1462276
  52.6 16.9 %collective-permute-start.9 = (bf16[272,896]{1,0:T(8,128)(2,1)S(1)}, bf16[272,896]{1,0:T(8,128)(2,1)S(1)}, u32[]{:S(2)}, u32[]{:S(2)}) collective-permute-start(bf16[272,896]{1,0:T(8,128)(2,1)S(1)} %collective-permute-done.8.refs_11_.refs_18_.refs_10_), channel_id=1, source_target_pairs={{1,0},{2,1},{5,4},{6,5},{9,8},{10,9},{13,12},{14,13},{17,16},{18,1... | collective-permute-start | bytes 1462280 | tf_op jit(solution)/shard_map/ppermute | solution.py:407
  54.0 51.3 %copy-start.8 = (bf16[272,896]{1,0:T(8,128)(2,1)}, bf16[272,896]{1,0:T(8,128)(2,1)S(1)}, u32[]{:S(2)}) copy-start(bf16[272,896]{1,0:T(8,128)(2,1)S(1)} %collective-permute-done.6.refs_8_.refs_15_.refs_7_) | copy-start | bytes 1462276
  54.0 15.5 %collective-permute-start.7 = (bf16[272,896]{1,0:T(8,128)(2,1)S(1)}, bf16[272,896]{1,0:T(8,128)(2,1)}, u32[]{:S(2)}, u32[]{:S(2)}) collective-permute-start(bf16[272,896]{1,0:T(8,128)(2,1)S(1)} %collective-permute-done.6.refs_8_.refs_15_.refs_7_), channel_id=1, source_target_pairs={{1,2},{2,3},{5,6},{6,7},{9,10},{10,11},{13,14},{14,15},{17,18},{18... | collective-permute-start | bytes 1462280 | tf_op jit(solution)/shard_map/ppermute | solution.py:407
  61.5 59.9 %copy-start.3 = (bf16[8,32,896]{2,1,0:T(8,128)(2,1)}, bf16[8,32,896]{2,1,0:T(8,128)(2,1)S(1)}, u32[]{:S(2)}) copy-start(bf16[8,32,896]{2,1,0:T(8,128)(2,1)S(1)} %all-to-all-done.1) | copy-start | bytes 1376260
  61.5 10.7 %collective-permute-start.2 = (bf16[256,896]{1,0:T(8,128)(2,1)}, bf16[256,896]{1,0:T(8,128)(2,1)S(1)}, u32[]{:S(2)}, u32[]{:S(2)}) collective-permute-start(bf16[256,896]{1,0:T(8,128)(2,1)} %collective-permute-done.refs_1_), channel_id=1, source_target_pairs={{1,2},{2,3},{5,6},{6,7},{9,10},{10,11},{13,14},{14,15},{17,18},{18... | collective-permute-start | bytes 1376264 | tf_op jit(solution)/shard_map/ppermute | solution.py:407
  62.2 18.8 %collective-permute-start.4 = (bf16[256,896]{1,0:T(8,128)(2,1)}, bf16[256,896]{1,0:T(8,128)(2,1)}, u32[]{:S(2)}, u32[]{:S(2)}) collective-permute-start(bf16[256,896]{1,0:T(8,128)(2,1)} %collective-permute-done.1.refs_4_), channel_id=1, source_target_pairs={{1,0},{2,1},{5,4},{6,5},{9,8},{10,9},{13,12},{14,13},{17,16},{18,1... | collective-permute-start | bytes 1376264 | tf_op jit(solution)/shard_map/ppermute | solution.py:407
  69.5 29.5 %collective-permute-start.10 = (bf16[272,896]{1,0:T(8,128)(2,1)}, bf16[272,896]{1,0:T(8,128)(2,1)}, u32[]{:S(2)}, u32[]{:S(2)}) collective-permute-start(bf16[272,896]{1,0:T(8,128)(2,1)} %collective-permute-done.7.refs_9_.refs_16_.refs_8_), channel_id=1, source_target_pairs={{2,3},{6,7},{10,11},{14,15},{18,19},{22,23},{26,27},{30,31}} | collective-permute-start | bytes 1462280 | tf_op jit(solution)/shard_map/ppermute | solution.py:407
  70.9 28.0 %collective-permute-start.11 = (bf16[272,896]{1,0:T(8,128)(2,1)S(1)}, bf16[272,896]{1,0:T(8,128)(2,1)}, u32[]{:S(2)}, u32[]{:S(2)}) collective-permute-start(bf16[272,896]{1,0:T(8,128)(2,1)S(1)} %collective-permute-done.9.refs_12_.refs_19_.refs_11_), channel_id=1, source_target_pairs={{1,0},{5,4},{9,8},{13,12},{17,16},{21,20},{25,24},{29,28}} | collective-permute-start | bytes 1462280 | tf_op jit(solution)/shard_map/ppermute | solution.py:407
  72.2 11.5 %collective-permute-start.3 = (bf16[256,896]{1,0:T(8,128)(2,1)S(1)}, bf16[256,896]{1,0:T(8,128)(2,1)}, u32[]{:S(2)}, u32[]{:S(2)}) collective-permute-start(bf16[256,896]{1,0:T(8,128)(2,1)S(1)} %collective-permute-done.2.refs_2_), channel_id=1, source_target_pairs={{2,3},{6,7},{10,11},{14,15},{18,19},{22,23},{26,27},{30,31}} | collective-permute-start | bytes 1376264 | tf_op jit(solution)/shard_map/ppermute | solution.py:407
  81.0 17.9 %collective-permute-start.5 = (bf16[256,896]{1,0:T(8,128)(2,1)}, bf16[256,896]{1,0:T(8,128)(2,1)}, u32[]{:S(2)}, u32[]{:S(2)}) collective-permute-start(bf16[256,896]{1,0:T(8,128)(2,1)} %collective-permute-done.4.refs_5_), channel_id=1, source_target_pairs={{1,0},{5,4},{9,8},{13,12},{17,16},{21,20},{25,24},{29,28}} | collective-permute-start | bytes 1376264 | tf_op jit(solution)/shard_map/ppermute | solution.py:407
  82.3 16.6 %collective-permute-start.12 = (bf16[256,896]{1,0:T(8,128)(2,1)S(1)}, bf16[256,896]{1,0:T(8,128)(2,1)}, u32[]{:S(2)}, u32[]{:S(2)}) collective-permute-start(bf16[256,896]{1,0:T(8,128)(2,1)S(1)} %bitcast.14), channel_id=1, source_target_pairs={{1,2},{2,1},{5,6},{6,5},{9,10},{10,9},{13,14},{14,13},{17,18},{18,... | collective-permute-start | bytes 1376264 | tf_op jit(solution)/shard_map/ppermute | solution.py:407
  98.9 24.5 %collective-permute-start.14 = (bf16[256,896]{1,0:T(8,128)(2,1)S(1)}, bf16[256,896]{1,0:T(8,128)(2,1)S(1)}, u32[]{:S(2)}, u32[]{:S(2)}) collective-permute-start(bf16[256,896]{1,0:T(8,128)(2,1)S(1)} %bitcast.15), channel_id=1, source_target_pairs={{0,1},{1,0},{2,3},{3,2},{4,5},{5,4},{6,7},{7,6},{8,9},{9,8},{10,11... | collective-permute-start | bytes 1376264 | tf_op jit(solution)/shard_map/ppermute | solution.py:407
  100.8 22.6 %collective-permute-start.13 = (bf16[256,896]{1,0:T(8,128)(2,1)S(1)}, bf16[256,896]{1,0:T(8,128)(2,1)S(1)}, u32[]{:S(2)}, u32[]{:S(2)}) collective-permute-start(bf16[256,896]{1,0:T(8,128)(2,1)S(1)} %bitcast.16), channel_id=1, source_target_pairs={{0,2},{1,3},{2,0},{3,1},{4,6},{5,7},{6,4},{7,5},{8,10},{9,11},{10,... | collective-permute-start | bytes 1376264 | tf_op jit(solution)/shard_map/ppermute | solution.py:407
  121.4 9.3 %collective-permute-start.15 = (bf16[8,32,896]{2,1,0:T(8,128)(2,1)}, bf16[8,32,896]{2,1,0:T(8,128)(2,1)S(1)}, u32[]{:S(2)}, u32[]{:S(2)}) collective-permute-start(bf16[8,32,896]{2,1,0:T(8,128)(2,1)} %get-tuple-element.90), channel_id=1, source_target_pairs={{0,1},{3,2},{4,5},{7,6},{8,9},{11,10},{12,13},{15,14},{16,17},{19,... | collective-permute-start | bytes 1376264 | tf_op jit(solution)/shard_map/ppermute | solution.py:407
  124.2 12.4 %collective-permute-start.17 = (bf16[256,896]{1,0:T(8,128)(2,1)S(1)}, bf16[256,896]{1,0:T(8,128)(2,1)S(1)}, u32[]{:S(2)}, u32[]{:S(2)}) collective-permute-start(bf16[256,896]{1,0:T(8,128)(2,1)S(1)} %collective-permute-done.13.refs_3_), channel_id=1, source_target_pairs={{1,0},{2,3},{5,4},{6,7},{9,8},{10,11},{13,12},{14,15},{17,16},{18,... | collective-permute-start | bytes 1376264 | tf_op jit(solution)/shard_map/ppermute | solution.py:407
  125.5 30.3 %collective-permute-start.19 = (bf16[8,32,896]{2,1,0:T(8,128)(2,1)}, bf16[8,32,896]{2,1,0:T(8,128)(2,1)S(1)}, u32[]{:S(2)}, u32[]{:S(2)}) collective-permute-start(bf16[8,32,896]{2,1,0:T(8,128)(2,1)} %get-tuple-element.90), channel_id=1, source_target_pairs={{1,2},{2,1},{5,6},{6,5},{9,10},{10,9},{13,14},{14,13},{17,18},{18,... | collective-permute-start | bytes 1376264 | tf_op jit(solution)/shard_map/ppermute | solution.py:407
  131.9 26.4 %collective-permute-start.16 = (bf16[8,32,896]{2,1,0:T(8,128)(2,1)S(1)}, bf16[8,32,896]{2,1,0:T(8,128)(2,1)S(1)}, u32[]{:S(2)}, u32[]{:S(2)}) collective-permute-start(bf16[8,32,896]{2,1,0:T(8,128)(2,1)S(1)} %add_convert_fusion.1.refs_0_), channel_id=1, source_target_pairs={{0,2},{1,3},{2,0},{3,1},{4,6},{5,7},{6,4},{7,5},{8,10},{9,11},{10,... | collective-permute-start | bytes 1376264 | tf_op jit(solution)/shard_map/ppermute | solution.py:407
  136.6 21.7 %collective-permute-start.18 = (bf16[8,32,896]{2,1,0:T(8,128)(2,1)}, bf16[8,32,896]{2,1,0:T(8,128)(2,1)S(1)}, u32[]{:S(2)}, u32[]{:S(2)}) collective-permute-start(bf16[8,32,896]{2,1,0:T(8,128)(2,1)} %get-tuple-element.89), channel_id=1, source_target_pairs={{0,1},{1,0},{2,3},{3,2},{4,5},{5,4},{6,7},{7,6},{8,9},{9,8},{10,11... | collective-permute-start | bytes 1376264 | tf_op jit(solution)/shard_map/ppermute | solution.py:407
  152.5 9.2 %collective-permute-start.20 = (bf16[8,16,896]{2,1,0:T(8,128)(2,1)}, bf16[8,16,896]{2,1,0:T(8,128)(2,1)S(1)}, u32[]{:S(2)}, u32[]{:S(2)}) collective-permute-start(bf16[8,16,896]{2,1,0:T(8,128)(2,1)} %get-tuple-element.106), channel_id=1, source_target_pairs={{0,1},{3,2},{4,5},{7,6},{8,9},{11,10},{12,13},{15,14},{16,17},{19,... | collective-permute-start | bytes 688136 | tf_op jit(solution)/shard_map/ppermute | solution.py:407
  162.7 9.5 %collective-permute-start.21 = (bf16[8,16,896]{2,1,0:T(8,128)(2,1)S(1)}, bf16[8,16,896]{2,1,0:T(8,128)(2,1)S(1)}, u32[]{:S(2)}, u32[]{:S(2)}) collective-permute-start(bf16[8,16,896]{2,1,0:T(8,128)(2,1)S(1)} %add_convert_fusion.3), channel_id=1, source_target_pairs={{0,2},{1,3},{2,0},{3,1},{4,6},{5,7},{6,4},{7,5},{8,10},{9,11},{10,... | collective-permute-start | bytes 688136 | tf_op jit(solution)/shard_map/ppermute | solution.py:407
  165.3 6.8 %collective-permute-start.22 = (bf16[8,16,896]{2,1,0:T(8,128)(2,1)}, bf16[8,16,896]{2,1,0:T(8,128)(2,1)S(1)}, u32[]{:S(2)}, u32[]{:S(2)}) collective-permute-start(bf16[8,16,896]{2,1,0:T(8,128)(2,1)} %get-tuple-element.105), channel_id=1, source_target_pairs={{0,1},{1,0},{2,3},{3,2},{4,5},{5,4},{6,7},{7,6},{8,9},{9,8},{10,11... | collective-permute-start | bytes 688136 | tf_op jit(solution)/shard_map/ppermute | solution.py:407
  165.3 6.8 %collective-permute-start.23 = (bf16[8,16,896]{2,1,0:T(8,128)(2,1)}, bf16[8,16,896]{2,1,0:T(8,128)(2,1)S(1)}, u32[]{:S(2)}, u32[]{:S(2)}) collective-permute-start(bf16[8,16,896]{2,1,0:T(8,128)(2,1)} %get-tuple-element.106), channel_id=1, source_target_pairs={{1,2},{2,1},{5,6},{6,5},{9,10},{10,9},{13,14},{14,13},{17,18},{18,... | collective-permute-start | bytes 688136 | tf_op jit(solution)/shard_map/ppermute | solution.py:407
  173.2 18.3 %all-to-all-start.2 = ((bf16[8,48,896]{2,1,0:T(8,128)(2,1)}), bf16[8,48,896]{2,1,0:T(8,128)(2,1)S(1)}, u32[]{:S(2)}, u32[]{:S(2)}) async-start(bf16[8,48,896]{2,1,0:T(8,128)(2,1)} %pad_maximum_fusion), calls=%async_computation.2 | async-start | bytes 1376256 | tf_op jit(solution)/shard_map/all_to_all | solution.py:538
  (9 other events, 151.2 us)
